TPU v7x, 128 devices: a whole 4x4x4 slice. The times are simulated.
128 devices in a mesh: attn: 16 (over y, z), expert: 8 (over x, core).
Axes of the slice: x: 4, y: 4, z: 4, core: 2. Of those that a mesh axis runs over, the one named last changes fastest.
Arguments:
- resid: bfloat16 [1024, 6144], P('attn')
- queries: bfloat16 [1024, 3072], P('attn', 'expert')
- new_keys: bfloat16 [1024, 1024], P('attn', 'expert'), may hold values from -6 to 6
- new_values: bfloat16 [1024, 1024], P('attn', 'expert'), may hold values from -12 to 12
- cache_k: bfloat16 [1024, 256, 1024], P('attn', None, 'expert')
- cache_v: bfloat16 [1024, 256, 1024], P('attn', None, 'expert'), may hold values from -12 to 12
- lengths: int32 [1024], P('attn'), may hold values from 2 to 256, as said below
- out_proj: bfloat16 [3072, 6144], P('expert'), may hold values from -0.109375 to 0.109375
- norm_gain: bfloat16 [6144], replicated, may hold values from 0.099609375 to 1.8984375
- router: bfloat16 [6144, 8], replicated, may hold values from -0.078125 to 0.078125
- route_ids: int32 [1024, 2], P('attn'), may hold values from 0 to 7, all different within a row; in each aligned block of 32 rows (0 to 31, 32 to 63, ...) at most 16 rows name the same one
- w_gate: bfloat16 [8, 6144, 8192], P('expert', None, 'attn'), may hold values from -0.078125 to 0.078125
- w_up: bfloat16 [8, 6144, 8192], P('expert', None, 'attn'), may hold values from -0.078125 to 0.078125
- w_down: bfloat16 [8, 8192, 6144], P('expert', 'attn'), may hold values from -0.0625 to 0.0625
Outputs:
- layer_out: bfloat16 [1024, 6144], P('attn', 'expert')
Inputs may be any that keep to these rules, and one draw needn't show every extreme that they name: `route_ids`: each row names two different experts. Within each aligned block of 32 rows (one micro-batch of one attention index) no expert is named by more than 16 rows, and some expert reaches 16 in some blocks. `lengths`: the first row of each attention index uses all 256 positions.
All inputs are finite; a program needn't handle non-finite values.
Results may differ from a plain program's by a relative error of at most 0.023.
Values may be sent and summed in bfloat16 or wider, within the bound.
No kernel may reach another device: no remote copies, remote signals or barrier semaphores. Data moves between devices by JAX's collectives and lax.ppermute only.
A program may use at most 192 MiB of HBM per device.

v0:
```python
import math

import jax
import jax.numpy as jnp
from jax import lax
from jax.sharding import PartitionSpec as P

HD = 128
TOP = 2
MICRO = 2
MB = 32


epsilon = 1e-05


def attend(queries, new_keys, new_values, cache_k, cache_v, lengths):
    count = queries.shape[0]
    length = cache_k.shape[1]
    kv_heads = new_keys.shape[1] // HD
    group = queries.shape[1] // (kv_heads * HD)
    query = queries.reshape(count, kv_heads, group, HD)
    keys = cache_k.reshape(count, length, kv_heads, HD)
    values = cache_v.reshape(count, length, kv_heads, HD)
    fresh_key = new_keys.reshape(count, kv_heads, HD)
    fresh_value = new_values.reshape(count, kv_heads, HD)
    factor = 1.0 / math.sqrt(HD)
    scores = jnp.einsum("rjhd,rljd->rjhl", query, keys, preferred_element_type=jnp.float32) * factor
    itself = (
        jnp.einsum("rjhd,rjd->rjh", query, fresh_key, preferred_element_type=jnp.float32) * factor
    )
    valid = (jnp.arange(length)[None, :] < lengths[:, None])[:, None, None, :]
    masked = jnp.where(valid, scores, -jnp.inf)
    highest = jnp.maximum(jnp.max(masked, axis=-1), itself)
    spread = jnp.exp(masked - highest[..., None])
    own_exp = jnp.exp(itself - highest)
    total = jnp.sum(spread, axis=-1) + own_exp
    weights = (spread / total[..., None]).astype(jnp.bfloat16)
    own_weight = (own_exp / total).astype(jnp.bfloat16)
    mixed = jnp.einsum("rjhl,rljd->rjhd", weights, values, preferred_element_type=jnp.float32)
    mixed = (
        mixed
        + own_weight.astype(jnp.float32)[..., None] * fresh_value.astype(jnp.float32)[:, :, None, :]
    )
    return mixed.reshape(count, -1).astype(jnp.bfloat16)


def slot_numbers(routes, experts):
    blocks, size, top_count = routes.shape
    onehot = (
        routes[..., None] == jnp.arange(experts, dtype=jnp.int32)[None, None, None, :]
    ).astype(jnp.int32)
    flat = onehot.reshape(blocks, size * top_count, experts)
    before = jnp.cumsum(flat, axis=1) - flat
    return jnp.sum(before * flat, axis=-1).reshape(blocks, size, top_count)


def layer(
    resid,
    queries,
    new_keys,
    new_values,
    cache_k,
    cache_v,
    lengths,
    route_ids,
    out_proj,
    norm_gain,
    router,
    w_gate,
    w_up,
    w_down,
):
    count, model_width = resid.shape
    blocks = count // MB
    experts = router.shape[1]
    capacity = 4 * MB // experts
    heads_out = attend(queries, new_keys, new_values, cache_k, cache_v, lengths)
    partial_out = jnp.dot(heads_out, out_proj, preferred_element_type=jnp.float32)
    gain = norm_gain.astype(jnp.float32)
    total = lax.psum(partial_out.astype(jnp.bfloat16), "expert").astype(jnp.float32)
    state = resid.astype(jnp.float32) + total
    mean_square = jnp.mean(state * state, axis=1, keepdims=True)
    normed = (state * lax.rsqrt(mean_square + epsilon) * gain[None, :]).astype(jnp.bfloat16)
    share_width = model_width // lax.axis_size("expert")
    own_state = lax.dynamic_slice_in_dim(
        state, lax.axis_index("expert") * share_width, share_width, 1
    )
    logits = jnp.dot(normed, router, preferred_element_type=jnp.float32)
    match = route_ids[:, :, None] == jnp.arange(experts, dtype=jnp.int32)[None, None, :]
    chosen = jnp.sum(jnp.where(match, logits[:, None, :], 0.0), axis=-1)
    gates = jax.nn.softmax(chosen, axis=-1).astype(jnp.bfloat16)
    routes = route_ids.reshape(blocks, MB, TOP)
    slots = slot_numbers(routes, experts)
    mine = lax.axis_index("expert")
    placed = (routes == mine)[..., None] & (
        slots[..., None] == jnp.arange(capacity, dtype=jnp.int32)[None, None, None, :]
    )
    dispatch = jnp.sum(placed.astype(jnp.float32), axis=2)
    gate_blocks = gates.astype(jnp.float32).reshape(blocks, MB, TOP)
    combine = jnp.sum(jnp.where(placed, gate_blocks[..., None], 0.0), axis=2)
    sectioned = jnp.einsum(
        "gms,gmd->gsd",
        dispatch.astype(jnp.bfloat16),
        normed.reshape(blocks, MB, model_width),
        preferred_element_type=jnp.float32,
    )
    sectioned = sectioned.astype(jnp.bfloat16).reshape(blocks * capacity, model_width)
    gate_weight = w_gate[0]
    up_weight = w_up[0]
    down_weight = w_down[0]
    piece = lax.all_gather(sectioned, "attn", axis=0, tiled=True)
    gate = jnp.dot(piece, gate_weight, preferred_element_type=jnp.float32)
    upper = jnp.dot(piece, up_weight, preferred_element_type=jnp.float32)
    expanded = (jax.nn.silu(gate) * upper).astype(jnp.bfloat16)
    piece = expanded
    term = jnp.dot(piece, down_weight, preferred_element_type=jnp.float32)
    expert_out = lax.psum_scatter(
        lax.optimization_barrier(term.astype(jnp.bfloat16))
        .astype(jnp.float32)
        .astype(jnp.bfloat16),
        "attn",
        scatter_dimension=0,
        tiled=True,
    ).astype(jnp.float32)
    weighted = jnp.einsum(
        "gms,gsd->gmd",
        combine,
        expert_out.reshape(blocks, capacity, model_width),
        precision=lax.Precision.HIGHEST,
    )
    moe = lax.psum_scatter(
        weighted.reshape(count, model_width).astype(jnp.bfloat16),
        "expert",
        scatter_dimension=1,
        tiled=True,
    ).astype(jnp.float32)
    return (own_state + moe).astype(jnp.bfloat16)


def body(
    resid,
    queries,
    new_keys,
    new_values,
    cache_k,
    cache_v,
    lengths,
    out_proj,
    norm_gain,
    router,
    route_ids,
    w_gate,
    w_up,
    w_down,
):
    row_args = (resid, queries, new_keys, new_values, cache_k, cache_v, lengths, route_ids)
    results = []
    for batch in range(MICRO):
        pieces = [
            lax.slice_in_dim(array, batch * MB, (batch + 1) * MB, axis=0) for array in row_args
        ]
        results.append(layer(*pieces, out_proj, norm_gain, router, w_gate, w_up, w_down))
    return jnp.concatenate(results, axis=0)


def solution(mesh):
    placed = (
        P("attn", None),
        P("attn", "expert"),
        P("attn", "expert"),
        P("attn", "expert"),
        P("attn", None, "expert"),
        P("attn", None, "expert"),
        P("attn"),
        P("expert", None),
        P(),
        P(),
        P("attn", None),
        P("expert", None, "attn"),
        P("expert", None, "attn"),
        P("expert", "attn", None),
    )
    return jax.shard_map(
        body, mesh=mesh, in_specs=placed, out_specs=P("attn", "expert"), check_vma=False
    )
```

profile of v0, /device:TPU:1, one launch (start us, length us, event | category | flops | bytes accessed | tf_op | source)
XLA Modules:
  0.0 414.6 jit_solution(2678793508068454269)
XLA Ops:
  6.5 0.8 fusion.102
  7.3 0.8 fusion.104
  8.2 0.1 iota_compare_fusion.1
  8.2 0.7 slice_bitcast_fusion
  8.9 0.1 fusion.84
  9.1 2.3 fusion.106
  11.4 0.2 fusion.71
  11.7 0.7 slice_convert_fusion
  12.5 2.5 fusion.105
  15.0 0.2 fusion.86
  15.1 0.2 fusion.70
  15.4 2.2 fusion.48
  17.6 1.7 convolution_convert_fusion.4
  19.3 0.5 fusion.51
  19.7 1.7 convolution_convert_fusion.5
  21.6 0.1 copy.31
  21.7 0.1 eq.156
  21.9 0.1 copy.33
  21.9 0.1 eq.168
  22.1 0.1 reduce_window_sum.17
  22.2 0.2 select_reduce_fusion.1
  22.4 0.1 eq.160
  22.5 0.1 copy.32
  22.6 0.1 reduce_window_sum.18
  22.7 0.2 select_reduce_fusion
  22.9 0.1 eq.172
  23.2 61.3 %all-reduce.3.cloned.1.call-done = (bf16[32,6144]{1,0:T(8,128)(2,1)}, bf16[32,6144]{1,0:T(8,128)(2,1)}) async-done(((bf16[32,6144]{1,0:T(8,128)(2,1)}, bf16[32,6144]{1,0:T(8,128)(2,1)}), (bf16[32,6144]{1,0:T(8,128)(2,1)}, bf16[32,6144]{1,0:T(8,128)(2,1)})) %all-reduce.3.cloned.1.call-update) | async-done | bytes 786448 | tf_op jit(solution)/shard_map/psum | solution.py:81
  84.5 1.5 multiply_reduce_fusion.1
  86.0 1.3 fusion.100
  87.4 0.3 fusion.101
  87.9 1.0 convolution_convert_fusion.7
  88.9 1.0 convolution_convert_fusion.6
  89.9 48.2 %all-gather.3.cloned.1.call-done = bf16[256,6144]{1,0:T(8,128)(2,1)} async-done(((bf16[16,6144]{1,0:T(8,128)(2,1)}), bf16[256,6144]{1,0:T(8,128)(2,1)}) %all-gather.3.cloned.1.call-update) | async-done | bytes 3145744 | tf_op jit(solution)/shard_map/all_gather | solution.py:112
  138.1 5.5 %fusion.8 = f32[256,512]{1,0:T(8,128)S(1)} fusion(bf16[256,6144]{1,0:T(8,128)(2,1)} %all-gather.3.cloned.1.call-done, bf16[1,6144,512]{2,1,0:T(8,128)(2,1)} %param.25), kind=kOutput, calls=%fused_computation.16 | convolution fusion | flops 1610612736 | bytes 9961472 | tf_op jit(solution)/shard_map/dot_general | solution.py:113
  143.7 10.7 %convolution_convert_fusion.1 = bf16[256,6144]{1,0:T(8,128)(2,1)} fusion(bf16[1,512,6144]{2,1,0:T(8,128)(2,1)} %param.27, bf16[256,6144]{1,0:T(8,128)(2,1)} %all-gather.3.cloned.1.call-done, bf16[1,6144,512]{2,1,0:T(8,128)(2,1)} %param.26, f32[256,512]{1,0:T(8,128)S(1)} %fusion.8), kind=kOutput, calls=%fused_computation.1 | convolution fusion | flops 3223584768 | bytes 19398656 | tf_op jit(solution)/shard_map/dot_general | solution.py:117
  154.4 0.2 reduce-scatter.9.cloned.1.call-start
  154.6 32.9 %all-gather.5.cloned.1.call-done = bf16[256,6144]{1,0:T(8,128)(2,1)} async-done(((bf16[16,6144]{1,0:T(8,128)(2,1)}), bf16[256,6144]{1,0:T(8,128)(2,1)}) %all-gather.5.cloned.1.call-update) | async-done | bytes 3145744 | tf_op jit(solution)/shard_map/all_gather | solution.py:112
  187.5 5.5 %fusion.6 = f32[256,512]{1,0:T(8,128)S(1)} fusion(bf16[256,6144]{1,0:T(8,128)(2,1)} %all-gather.5.cloned.1.call-done, bf16[1,6144,512]{2,1,0:T(8,128)(2,1)} %param.25), kind=kOutput, calls=%fused_computation.14 | convolution fusion | flops 1610612736 | bytes 9961472 | tf_op jit(solution)/shard_map/dot_general | solution.py:113
  193.0 10.7 %convolution_convert_fusion = bf16[256,6144]{1,0:T(8,128)(2,1)} fusion(bf16[1,512,6144]{2,1,0:T(8,128)(2,1)} %param.27, bf16[256,6144]{1,0:T(8,128)(2,1)} %all-gather.5.cloned.1.call-done, bf16[1,6144,512]{2,1,0:T(8,128)(2,1)} %param.26, f32[256,512]{1,0:T(8,128)S(1)} %fusion.6), kind=kOutput, calls=%fused_computation | convolution fusion | flops 3223584768 | bytes 19398656 | tf_op jit(solution)/shard_map/dot_general | solution.py:117
  203.8 60.6 %reduce-scatter.5.cloned.1.call-done = bf16[16,6144]{1,0:T(8,128)(2,1)} async-done(((bf16[256,6144]{1,0:T(8,128)(2,1)}), bf16[16,6144]{1,0:T(8,128)(2,1)}) %reduce-scatter.5.cloned.1.call-update) | async-done | bytes 196624 | tf_op jit(solution)/shard_map/reduce_scatter | solution.py:118
  264.4 2.2 convolution_convert_fusion.3
  266.7 76.5 %reduce-scatter.9.cloned.1.call-done = bf16[16,6144]{1,0:T(8,128)(2,1)} async-done(((bf16[256,6144]{1,0:T(8,128)(2,1)}), bf16[16,6144]{1,0:T(8,128)(2,1)}) %reduce-scatter.9.cloned.1.call-update) | async-done | bytes 196624 | tf_op jit(solution)/shard_map/reduce_scatter | solution.py:118
  343.1 2.2 convolution_convert_fusion.2
  345.3 29.0 %reduce-scatter.7.cloned.1.call-done = bf16[32,768]{1,0:T(8,128)(2,1)} async-done(((bf16[32,6144]{1,0:T(8,128)(2,1)}), bf16[32,768]{1,0:T(8,128)(2,1)}) %reduce-scatter.7.cloned.1.call-update) | async-done | bytes 49168 | tf_op jit(solution)/shard_map/reduce_scatter | solution.py:132
  374.3 0.8 add_convert_fusion.1
  375.1 31.1 %reduce-scatter.11.cloned.1.call-done = bf16[32,768]{1,0:T(8,128)(2,1)} async-done(((bf16[32,6144]{1,0:T(8,128)(2,1)}), bf16[32,768]{1,0:T(8,128)(2,1)}) %reduce-scatter.11.cloned.1.call-update) | async-done | bytes 49168 | tf_op jit(solution)/shard_map/reduce_scatter | solution.py:132
  406.3 0.8 add_convert_fusion
  407.1 0.6 pad_maximum_fusion
  (53 shorter events, 1.1 us)
Async XLA Ops:
  6.5 79.5 %copy-start = (bf16[6144,8]{0,1:T(8,128)(2,1)S(1)}, bf16[6144,8]{0,1:T(8,128)(2,1)}, u32[]{:S(2)}) copy-start(bf16[6144,8]{0,1:T(8,128)(2,1)} %param.23) | copy-start | bytes 294916
  6.5 77.9 %all-reduce.3.cloned.1.call-start = ((), (), s32[]{:S(2)}) async-start(), calls=%async_computation.10 | async-start | bytes 1572864 | tf_op jit(solution)/shard_map/psum | solution.py:81
  12.4 5.2 %copy-start.1 = (bf16[384,6144]{1,0:T(8,128)(2,1)S(1)}, bf16[384,6144]{1,0:T(8,128)(2,1)}, u32[]{:S(2)}) copy-start(bf16[384,6144]{1,0:T(8,128)(2,1)} %param.21) | copy-start | bytes 14155780
  15.4 3.9 copy-start.7
  19.3 2.2 copy-start.5
  19.3 3.1 copy-start.6
  19.3 65.2 %copy-start.2 = (bf16[64,6144]{1,0:T(8,128)(2,1)S(1)}, bf16[64,6144]{1,0:T(8,128)(2,1)}, u32[]{:S(2)}) copy-start(bf16[64,6144]{1,0:T(8,128)(2,1)} %param.14) | copy-start | bytes 2359300
  21.4 116.7 %all-gather.3.cloned.1.call-start = ((), (), s32[]{:S(2)}) async-start(), calls=%async_computation.4 | async-start | bytes 3342336 | tf_op jit(solution)/shard_map/all_gather | solution.py:112
  84.5 3.0 copy-start.3
  84.5 3.4 copy-start.4
  88.8 98.6 %all-gather.5.cloned.1.call-start = ((), (), s32[]{:S(2)}) async-start(), calls=%async_computation.7 | async-start | bytes 3342336 | tf_op jit(solution)/shard_map/all_gather | solution.py:112
  89.9 174.5 %reduce-scatter.5.cloned.1.call-start = ((), (), s32[]{:S(2)}) async-start(), calls=%async_computation.5 | async-start | bytes 3342336 | tf_op jit(solution)/shard_map/reduce_scatter | solution.py:118
  154.4 188.7 %reduce-scatter.9.cloned.1.call-start = ((), (), s32[]{:S(2)}) async-start(), calls=%async_computation.8 | async-start | bytes 3342336 | tf_op jit(solution)/shard_map/reduce_scatter | solution.py:118
  203.8 170.6 %reduce-scatter.7.cloned.1.call-start = ((), (), s32[]{:S(2)}) async-start(), calls=%async_computation.6 | async-start | bytes 442368 | tf_op jit(solution)/shard_map/reduce_scatter | solution.py:132
  266.6 139.6 %reduce-scatter.11.cloned.1.call-start = ((), (), s32[]{:S(2)}) async-start(), calls=%async_computation.9 | async-start | bytes 442368 | tf_op jit(solution)/shard_map/reduce_scatter | solution.py:132
Sparse Core Ops, SparseCore 0:
  21.6 62.8 all-reduce.2
  89.0 49.1 all-gather.2
  140.6 46.8 all-gather.4
  191.0 73.3 reduce-scatter.4
  268.0 75.1 reduce-scatter.8
  345.5 28.8 reduce-scatter.6
  376.7 29.5 reduce-scatter.10
where the time goes:
time: 417 us; the launch traced here: 415 us
  waiting for transfers between devices  340 us (82%)
  matrix products  51.5 us (12%)
  between operations  13.7 us (3%)
  other arithmetic  6.11 us (1%)
    reduce_scatter x2, waiting for transfers between devices, layer(): lax.psum_scatter(lax.optimization_barrier(term.astype(jnp.bfloat16)).asty...  137 us
    all_gather x2, waiting for transfers between devices, layer(): piece = lax.all_gather(sectioned, 'attn', axis=0, tiled=True)  81.1 us
    psum x1, waiting for transfers between devices, layer(): lax.psum(partial_out.astype(jnp.bfloat16), 'expert').astype(jnp.float32)  61.3 us
    reduce_scatter x2, waiting for transfers between devices, layer(): lax.psum_scatter(weighted.reshape(count, model_width).astype(jnp.bfloat16...  60.1 us
    dot_general x2, matrix products, layer(): term = jnp.dot(piece, down_weight, preferred_element_type=jnp.float32)  21.4 us
    dot_general x2, matrix products, layer(): gate = jnp.dot(piece, gate_weight, preferred_element_type=jnp.float32)  11 us
  transfers between devices with their start and end apart: 7, of which 7 were waited for; matrix products, arithmetic and copies ran while one was open for 10% of the time, Pallas kernels for 0%

commit v1 on v0

v1 whole, which is shorter than its diff:
```python
import math

import jax
import jax.numpy as jnp
from jax import lax
from jax.sharding import Mesh
from jax.sharding import PartitionSpec as P

HD = 128
TOP = 2
MICRO = 2
MB = 32
SIDE = 4
EXPERT_AXES = ("x", "c")

epsilon = 1e-05


def shift(value, axis, step):
    return lax.ppermute(value, axis, [(i, (i + step) % SIDE) for i in range(SIDE)])


def ring(value, axis):
    perm = []
    for i in range(SIDE):
        perm.append((2 * i, 2 * ((i + 1) % SIDE)))
        perm.append((2 * i + 1, 2 * ((i - 1) % SIDE) + 1))
    return lax.ppermute(value, (axis, "c"), perm)


def attend(queries, new_keys, new_values, cache_k, cache_v, lengths):
    count = queries.shape[0]
    length = cache_k.shape[1]
    group = queries.shape[1] // HD
    query = queries.reshape(count, group, HD)
    factor = 1.0 / math.sqrt(HD)
    scores = jnp.einsum("rhd,rld->rhl", query, cache_k, preferred_element_type=jnp.float32) * factor
    itself = (
        jnp.einsum("rhd,rd->rh", query, new_keys, preferred_element_type=jnp.float32) * factor
    )
    valid = (jnp.arange(length)[None, :] < lengths[:, None])[:, None, :]
    masked = jnp.where(valid, scores, -jnp.inf)
    highest = jnp.maximum(jnp.max(masked, axis=-1), itself)
    spread = jnp.exp(masked - highest[..., None])
    own_exp = jnp.exp(itself - highest)
    total = jnp.sum(spread, axis=-1) + own_exp
    weights = (spread / total[..., None]).astype(jnp.bfloat16)
    own_weight = (own_exp / total).astype(jnp.bfloat16)
    mixed = jnp.einsum("rhl,rld->rhd", weights, cache_v, preferred_element_type=jnp.float32)
    mixed = (
        mixed
        + own_weight.astype(jnp.float32)[..., None] * new_values.astype(jnp.float32)[:, None, :]
    )
    return mixed.reshape(count, -1).astype(jnp.bfloat16)


def slot_codes(route_ids, experts, capacity):
    routes = route_ids.reshape(MICRO, MB, TOP)
    onehot = (routes[..., None] == jnp.arange(experts, dtype=jnp.int32)).astype(jnp.int32)
    flat = onehot.reshape(MICRO, MB * TOP, experts)
    before = jnp.cumsum(flat, axis=1) - flat
    slots = jnp.sum(before * flat, axis=-1).reshape(MICRO, MB, TOP)
    batch = jnp.arange(MICRO, dtype=jnp.int32)[:, None, None]
    return ((routes * MICRO + batch) * capacity + slots).reshape(MICRO * MB, TOP)


def spread_over(value, axis):
    return jnp.concatenate([value] + [shift(value, axis, k) for k in range(1, SIDE)], axis=0)


def body(
    resid,
    queries,
    new_keys,
    new_values,
    cache_k,
    cache_v,
    lengths,
    out_proj,
    norm_gain,
    router,
    route_ids,
    w_gate,
    w_up,
    w_down,
):
    count, model_width = resid.shape
    experts = router.shape[1]
    capacity = 4 * MB // experts
    slots = MICRO * capacity
    share = model_width // experts
    mine = lax.axis_index(EXPERT_AXES)

    codes = slot_codes(route_ids, experts, capacity)
    places = jnp.arange(experts * slots, dtype=jnp.int32)[:, None]
    dispatch = ((codes[None, :, 0] == places) | (codes[None, :, 1] == places)).astype(jnp.bfloat16)

    heads_out = attend(queries, new_keys, new_values, cache_k, cache_v, lengths)
    partial_out = jnp.dot(heads_out, out_proj, preferred_element_type=jnp.float32).astype(
        jnp.bfloat16
    )
    partial_out = partial_out.reshape(count, experts, share).transpose(1, 0, 2)
    sums = lax.all_to_all(partial_out, EXPERT_AXES, 0, 0, tiled=True)
    own_resid = lax.dynamic_slice_in_dim(resid, mine * share, share, 1)
    state = own_resid.astype(jnp.float32) + jnp.sum(sums.astype(jnp.float32), axis=0)

    sent = jnp.dot(dispatch, state.astype(jnp.bfloat16), preferred_element_type=jnp.float32)
    sent = sent.astype(jnp.bfloat16).reshape(experts, slots, share)
    rows = lax.all_to_all(sent, EXPERT_AXES, 0, 0, tiled=True).astype(jnp.float32)
    mean_square = jnp.sum(rows * rows, axis=(0, 2)) / model_width
    gain = norm_gain.astype(jnp.float32).reshape(experts, 1, share)
    normed = (rows * lax.rsqrt(mean_square + epsilon)[None, :, None] * gain).astype(jnp.bfloat16)
    normed = normed.transpose(1, 0, 2).reshape(slots, model_width)

    logits = jnp.dot(normed, router, preferred_element_type=jnp.float32)
    own_dispatch = lax.dynamic_slice_in_dim(dispatch, mine * slots, slots, 0)
    expert_ids = jnp.arange(experts, dtype=jnp.int32)
    match = jnp.sum((route_ids[:, :, None] == expert_ids).astype(jnp.bfloat16), axis=1)
    both = jnp.dot(own_dispatch, match, preferred_element_type=jnp.float32)
    own_mask = (expert_ids == mine)[None, :]
    own_logit = jnp.sum(jnp.where(own_mask, logits, 0.0), axis=1)
    other_logit = jnp.sum(jnp.where(own_mask, 0.0, logits * both), axis=1)
    gates = (1.0 / (1.0 + jnp.exp(other_logit - own_logit))).astype(jnp.bfloat16)

    gate_weight = w_gate[0]
    up_weight = w_up[0]
    down_weight = w_down[0]

    def expert(piece):
        gate = jnp.dot(piece, gate_weight, preferred_element_type=jnp.float32)
        upper = jnp.dot(piece, up_weight, preferred_element_type=jnp.float32)
        expanded = (jax.nn.silu(gate) * upper).astype(jnp.bfloat16)
        return jnp.dot(expanded, down_weight, preferred_element_type=jnp.float32).astype(
            jnp.bfloat16
        )

    def add(one, two):
        return (one.astype(jnp.float32) + two.astype(jnp.float32)).astype(jnp.bfloat16)

    first = [spread_over(normed[:capacity], "z")]
    second = [spread_over(normed[capacity:], "y")]
    for _ in range(SIDE - 1):
        first.append(ring(first[-1], "y"))
        second.append(ring(second[-1], "z"))
    parts = []
    for one, two in zip(first, second):
        part = expert(jnp.concatenate([one, two], axis=0))
        parts.append((part[: one.shape[0]], part[one.shape[0] :]))
    one, two = parts[1]
    for step in (2, 3, 0):
        one = add(ring(one, "y"), parts[step][0])
        two = add(ring(two, "z"), parts[step][1])

    def collect(value, axis):
        pieces = value.reshape(SIDE, capacity, model_width)
        total = pieces[0].astype(jnp.float32)
        for k in range(1, SIDE):
            total = total + shift(pieces[k], axis, -k).astype(jnp.float32)
        return total

    expert_out = jnp.concatenate([collect(one, "z"), collect(two, "y")], axis=0)
    weighted = (expert_out * gates.astype(jnp.float32)[:, None]).astype(jnp.bfloat16)
    weighted = weighted.reshape(slots, experts, share).transpose(1, 0, 2)
    back = lax.all_to_all(weighted, EXPERT_AXES, 0, 0, tiled=True)
    moe = lax.dot_general(
        dispatch,
        back.reshape(experts * slots, share),
        (((0,), (0,)), ((), ())),
        preferred_element_type=jnp.float32,
    )
    return (state + moe).astype(jnp.bfloat16)


def solution(mesh):
    fine = Mesh(mesh.devices.reshape(SIDE, SIDE, SIDE, 2), ("y", "z", "x", "c"))
    attn = ("y", "z")
    placed = (
        P(attn, None),
        P(attn, EXPERT_AXES),
        P(attn, EXPERT_AXES),
        P(attn, EXPERT_AXES),
        P(attn, None, EXPERT_AXES),
        P(attn, None, EXPERT_AXES),
        P(attn),
        P(EXPERT_AXES, None),
        P(),
        P(),
        P(attn, None),
        P(EXPERT_AXES, None, attn),
        P(EXPERT_AXES, None, attn),
        P(EXPERT_AXES, attn, None),
    )
    return jax.shard_map(
        body, mesh=fine, in_specs=placed, out_specs=P(attn, EXPERT_AXES), check_vma=False
    )
```

time: 417 us -> 183 us (0.44)
  waiting for transfers between devices: 340 us -> 45.3 us
  starting transfers between devices: 0.43 us -> 47 us
  blocking collectives: 0 us -> 18.3 us
  between operations: 13.7 us -> 0.5 us
  local copies, waits for them, and re-layouts: 3.19 us -> 12.4 us
    reduce_scatter x4 -> x0, waiting for transfers between devices: 197 us -> none  [the longest x2 137 us: layer(): lax.psum_scatter(lax.optimization_barrier(term.astype(jnp.bfloat16)).asty...]
    all_gather x2 -> x0, waiting for transfers between devices: 81.1 us -> none  [layer(): piece = lax.all_gather(sectioned, 'attn', axis=0, tiled=True)]
    psum x1 -> x0, waiting for transfers between devices: 61.3 us -> none  [layer(): lax.psum(partial_out.astype(jnp.bfloat16), 'expert').astype(jnp.float32)]
    ppermute x0 -> x24, starting transfers between devices: none -> 36.8 us  [the longest x12 19.8 us: shift(): lax.ppermute(value, axis, [(i, (i + step) % SIDE) for i in range(SIDE)])]
    ppermute x0 -> x24, waiting for transfers between devices: none -> 25.9 us  [the longest x12 16.8 us: ring(): return lax.ppermute(value, (axis, 'c'), perm)]
    all_to_all x0 -> x2, waiting for transfers between devices: none -> 19.4 us  [the longest x1 11.4 us: body(): sums = lax.all_to_all(partial_out, EXPERT_AXES, 0, 0, tiled=True)]
    all_to_all x0 -> x1, blocking collectives: none -> 18.3 us  [body(): back = lax.all_to_all(weighted, EXPERT_AXES, 0, 0, tiled=True)]
    all_to_all x0 -> x2, starting transfers between devices: none -> 10.2 us  [the longest x1 5.93 us: body(): sums = lax.all_to_all(partial_out, EXPERT_AXES, 0, 0, tiled=True)]
  transfers between devices with their start and end apart: 7 -> 26, of which waited for: 7 -> 13; matrix products, arithmetic and copies ran while one was open for 10% -> 23% of each run, Pallas kernels for 0% -> 0%
where the time goes in v1:
time: 183 us
  matrix products  49.1 us (27%)
  starting transfers between devices  47 us (26%)
  waiting for transfers between devices  45.3 us (25%)
  blocking collectives  18.3 us (10%)
  local copies, waits for them, and re-layouts  12.4 us (7%)
  other arithmetic  10.1 us (6%)
    dot_general x4, matrix products, expert(): jnp.dot(expanded, down_weight, preferred_element_type=jnp.float32)  27.1 us
    ppermute x12, starting transfers between devices, shift(): lax.ppermute(value, axis, [(i, (i + step) % SIDE) for i in range(SIDE)])  19.8 us
    all_to_all x1, blocking collectives, body(): back = lax.all_to_all(weighted, EXPERT_AXES, 0, 0, tiled=True)  18.3 us
    ppermute x12, starting transfers between devices, ring(): return lax.ppermute(value, (axis, 'c'), perm)  17 us
    ppermute x12, waiting for transfers between devices, ring(): return lax.ppermute(value, (axis, 'c'), perm)  16.8 us
    dot_general x4, matrix products, expert(): upper = jnp.dot(piece, up_weight, preferred_element_type=jnp.float32)  11.7 us
    all_to_all x1, waiting for transfers between devices, body(): sums = lax.all_to_all(partial_out, EXPERT_AXES, 0, 0, tiled=True)  11.4 us
    ppermute x12, waiting for transfers between devices, shift(): lax.ppermute(value, axis, [(i, (i + step) % SIDE) for i in range(SIDE)])  9.06 us
  transfers between devices with their start and end apart: 26, of which 13 were waited for; matrix products, arithmetic and copies ran while one was open for 23% of the time, Pallas kernels for 0%

profile of v1, /device:TPU:1, one launch (start us, length us, event | category | flops | bytes accessed | tf_op | source)
XLA Modules:
  0.0 182.7 jit_solution(3278490211702386244)
XLA Ops:
  2.5 3.6 %fusion.80 = (f32[64,3]{1,0:T(8,128)S(1)}, f32[64,3,256]{2,1,0:T(4,128)S(1)}) fusion(bf16[64,3,128]{2,1,0:T(4,128)(2,1)S(1)} %reshape.101, bf16[64,256,128]{2,1,0:T(8,128)(2,1)} %param.18, pred[64,256]{1,0:T(8,128)(4,1)S(1)} %iota_compare_fusion.3), kind=kOutput, calls=%fused_computation.127 | convolution fusion | flops 12730176 | bytes 4457216 | tf_op jit(solution)/shard_map/rhd,rld->rhl/dot_general | solution.py:37
  7.2 1.6 copy-done.5
  10.7 5.9 %all-to-all-start = ((bf16[8,64,768]{2,1,0:T(8,128)(2,1)}), bf16[8,64,768]{2,1,0:T(8,128)(2,1)S(1)}, u32[]{:S(2)}, u32[]{:S(2)}) async-start(bf16[8,64,768]{2,1,0:T(8,128)(2,1)} %bitcast.98), calls=%async_computation | async-start | bytes 1572864 | tf_op jit(solution)/shard_map/all_to_all | solution.py:103
  17.6 11.4 %all-to-all-done = bf16[8,64,768]{2,1,0:T(8,128)(2,1)S(1)} async-done(((bf16[8,64,768]{2,1,0:T(8,128)(2,1)}), bf16[8,64,768]{2,1,0:T(8,128)(2,1)S(1)}, u32[]{:S(2)}, u32[]{:S(2)}) %all-to-all-start) | async-done | bytes 786464 | tf_op jit(solution)/shard_map/all_to_all | solution.py:103
  29.1 1.9 %convolution_convert_fusion.5 = bf16[256,768]{1,0:T(8,128)(2,1)} fusion(f32[64,768]{1,0:T(8,128)S(1)} %convert_reduce_fusion, bf16[64,6144]{1,0:T(8,128)(2,1)} %param.14, s32[]{:T(128)S(6)} %select_n.18, s32[64]{0:T(128)S(1)} %get-tuple-element.26, s32[64]{0:T(128)S(1)} %get-tuple-element.25), kind=kOutput, calls=%fused_computation.32 | convolution fusion | flops 25559040 | bytes 688644 | tf_op jit(solution)/shard_map/dot_general | solution.py:107
  31.0 4.2 %all-to-all-start.1 = ((bf16[8,32,768]{2,1,0:T(8,128)(2,1)}), bf16[8,32,768]{2,1,0:T(8,128)(2,1)S(1)}, u32[]{:S(2)}, u32[]{:S(2)}) async-start(bf16[8,32,768]{2,1,0:T(8,128)(2,1)} %bitcast.6), calls=%async_computation.1 | async-start | bytes 786432 | tf_op jit(solution)/shard_map/all_to_all | solution.py:109
  35.3 8.0 %all-to-all-done.1 = bf16[8,32,768]{2,1,0:T(8,128)(2,1)S(1)} async-done(((bf16[8,32,768]{2,1,0:T(8,128)(2,1)}), bf16[8,32,768]{2,1,0:T(8,128)(2,1)S(1)}, u32[]{:S(2)}, u32[]{:S(2)}) %all-to-all-start.1) | async-done | bytes 393248 | tf_op jit(solution)/shard_map/all_to_all | solution.py:109
  43.8 3.8 %collective-permute-start.2 = (bf16[16,6144]{1,0:T(8,128)(2,1)S(1)}, bf16[16,6144]{1,0:T(8,128)(2,1)S(1)}, u32[]{:S(2)}, u32[]{:S(2)}) collective-permute-start(bf16[16,6144]{1,0:T(8,128)(2,1)S(1)} %bitcast.107), channel_id=1, source_target_pairs={{0,24},{8,0},{16,8},{24,16},{1,25},{9,1},{17,9},{25,17},{2,26},{10... | collective-permute-start | bytes 589832 | tf_op jit(solution)/shard_map/ppermute | solution.py:20
  48.3 2.8 %collective-permute-start.6 = (bf16[16,6144]{1,0:T(8,128)(2,1)S(1)}, bf16[16,6144]{1,0:T(8,128)(2,1)S(1)}, u32[]{:S(2)}, u32[]{:S(2)}) collective-permute-start(bf16[16,6144]{1,0:T(8,128)(2,1)S(1)} %bitcast.102), channel_id=1, source_target_pairs={{0,96},{32,0},{64,32},{96,64},{1,97},{33,1},{65,33},{97,65},{2,98}... | collective-permute-start | bytes 589832 | tf_op jit(solution)/shard_map/ppermute | solution.py:20
  51.9 3.4 %collective-permute-done.2 = bf16[16,6144]{1,0:T(8,128)(2,1)S(1)} collective-permute-done((bf16[16,6144]{1,0:T(8,128)(2,1)S(1)}, bf16[16,6144]{1,0:T(8,128)(2,1)S(1)}, u32[]{:S(2)}, u32[]{:S(2)}) %collective-permute-start.2) | collective-permute-done | bytes 196640 | tf_op jit(solution)/shard_map/ppermute | solution.py:20
  55.4 1.3 collective-permute-start.4
  56.6 2.8 %collective-permute-done = bf16[16,6144]{1,0:T(8,128)(2,1)S(1)} collective-permute-done((bf16[16,6144]{1,0:T(8,128)(2,1)S(1)}, bf16[16,6144]{1,0:T(8,128)(2,1)S(1)}, u32[]{:S(2)}, u32[]{:S(2)}) %collective-permute-start) | collective-permute-done | bytes 196640 | tf_op jit(solution)/shard_map/ppermute | solution.py:20
  59.5 2.8 %collective-permute-start.3 = (bf16[64,6144]{1,0:T(8,128)(2,1)S(1)}, bf16[64,6144]{1,0:T(8,128)(2,1)S(1)}, u32[]{:S(2)}, u32[]{:S(2)}) collective-permute-start(bf16[64,6144]{1,0:T(8,128)(2,1)S(1)} %pad_maximum_fusion), channel_id=1, source_target_pairs={{0,32},{1,97},{32,64},{33,1},{64,96},{65,33},{96,0},{97,65},{2,34}... | collective-permute-start | bytes 2359304 | tf_op jit(solution)/shard_map/ppermute | solution.py:28
  62.7 2.6 %collective-permute-start.7 = (bf16[64,6144]{1,0:T(8,128)(2,1)S(1)}, bf16[64,6144]{1,0:T(8,128)(2,1)S(1)}, u32[]{:S(2)}, u32[]{:S(2)}) collective-permute-start(bf16[64,6144]{1,0:T(8,128)(2,1)S(1)} %pad_maximum_fusion.1), channel_id=1, source_target_pairs={{0,8},{1,25},{8,16},{9,1},{16,24},{17,9},{24,0},{25,17},{2,10},{3,... | collective-permute-start | bytes 2359304 | tf_op jit(solution)/shard_map/ppermute | solution.py:28
  65.5 1.7 fusion.4
  67.2 4.0 %collective-permute-done.3 = bf16[64,6144]{1,0:T(8,128)(2,1)S(1)} collective-permute-done((bf16[64,6144]{1,0:T(8,128)(2,1)S(1)}, bf16[64,6144]{1,0:T(8,128)(2,1)S(1)}, u32[]{:S(2)}, u32[]{:S(2)}) %collective-permute-start.3) | collective-permute-done | bytes 786464 | tf_op jit(solution)/shard_map/ppermute | solution.py:28
  71.3 3.3 %collective-permute-done.7 = bf16[64,6144]{1,0:T(8,128)(2,1)S(1)} collective-permute-done((bf16[64,6144]{1,0:T(8,128)(2,1)S(1)}, bf16[64,6144]{1,0:T(8,128)(2,1)S(1)}, u32[]{:S(2)}, u32[]{:S(2)}) %collective-permute-start.7) | collective-permute-done | bytes 786464 | tf_op jit(solution)/shard_map/ppermute | solution.py:28
  75.5 1.1 copy-done.2
  77.7 7.1 %convolution_convert_fusion.3 = bf16[128,6144]{1,0:T(8,128)(2,1)S(1)} fusion(bf16[1,512,6144]{2,1,0:T(8,128)(2,1)} %param.27, f32[128,512]{1,0:T(8,128)S(1)} %fusion.10, bf16[128,6144]{1,0:T(8,128)(2,1)} %copy-done.2, bf16[1,6144,512]{2,1,0:T(8,128)(2,1)} %param.25), kind=kOutput, calls=%fused_computation.3 | convolution fusion | flops 1611792384 | bytes 15990784 | tf_op jit(solution)/shard_map/dot_general | solution.py:133
  85.9 3.1 %collective-permute-start.10 = (bf16[64,6144]{1,0:T(8,128)(2,1)}, bf16[64,6144]{1,0:T(8,128)(2,1)}, u32[]{:S(2)}, u32[]{:S(2)}) collective-permute-start(bf16[64,6144]{1,0:T(8,128)(2,1)} %copy-done.8), channel_id=1, source_target_pairs={{0,8},{1,25},{8,16},{9,1},{16,24},{17,9},{24,0},{25,17},{2,10},{3,... | collective-permute-start | bytes 2359304 | tf_op jit(solution)/shard_map/ppermute | solution.py:28
  89.0 1.3 fusion.77
  90.8 5.3 %collective-permute-done.9 = bf16[64,6144]{1,0:T(8,128)(2,1)} collective-permute-done((bf16[64,6144]{1,0:T(8,128)(2,1)S(1)}, bf16[64,6144]{1,0:T(8,128)(2,1)}, u32[]{:S(2)}, u32[]{:S(2)}) %collective-permute-start.9) | collective-permute-done | bytes 786464 | tf_op jit(solution)/shard_map/ppermute | solution.py:28
  96.1 1.2 constant_dynamic-update-slice_fusion.3
  98.3 1.2 constant_dynamic-update-slice_fusion.2
  99.5 4.5 %fusion.8 = f32[128,512]{1,0:T(8,128)} fusion(bf16[128,6144]{1,0:T(8,128)(2,1)S(1)} %constant_dynamic-update-slice_fusion.2, bf16[1,6144,512]{2,1,0:T(8,128)(2,1)} %param.26), kind=kOutput, calls=%fused_computation.13 | convolution fusion | flops 805306368 | bytes 8126464 | tf_op jit(solution)/shard_map/dot_general | solution.py:131
  104.0 1.3 collective-permute-start.12
  105.2 2.8 %collective-permute-start.13 = (bf16[64,6144]{1,0:T(8,128)(2,1)}, bf16[64,6144]{1,0:T(8,128)(2,1)}, u32[]{:S(2)}, u32[]{:S(2)}) collective-permute-start(bf16[64,6144]{1,0:T(8,128)(2,1)} %collective-permute-done.10), channel_id=1, source_target_pairs={{0,8},{1,25},{8,16},{9,1},{16,24},{17,9},{24,0},{25,17},{2,10},{3,... | collective-permute-start | bytes 2359304 | tf_op jit(solution)/shard_map/ppermute | solution.py:28
  108.1 6.7 %convolution_convert_fusion.2 = bf16[128,6144]{1,0:T(8,128)(2,1)S(1)} fusion(bf16[1,512,6144]{2,1,0:T(8,128)(2,1)} %param.27, f32[128,512]{1,0:T(8,128)} %fusion.8, bf16[128,6144]{1,0:T(8,128)(2,1)S(1)} %constant_dynamic-update-slice_fusion.2, bf16[1,6144,512]{2,1,0:T(8,128)(2,1)} %param.25), kind=kOutput, calls=%fused_computation.2 | convolution fusion | flops 1611792384 | bytes 15990784 | tf_op jit(solution)/shard_map/dot_general | solution.py:133
  114.8 2.9 %add_convert_fusion.5 = (bf16[64,6144]{1,0:T(8,128)(2,1)}, bf16[64,6144]{1,0:T(8,128)(2,1)}) fusion(bf16[64,6144]{1,0:T(8,128)(2,1)} %collective-permute-done.8, bf16[128,6144]{1,0:T(8,128)(2,1)S(1)} %convolution_convert_fusion.2, bf16[64,6144]{1,0:T(8,128)(2,1)} %collective-permute-done.18), kind=kLoop, calls=%fused_computation.30 | loop fusion | flops 3145728 | bytes 4718592 | tf_op jit(solution)/shard_map/convert_element_type | solution.py:138
  117.7 1.2 constant_dynamic-update-slice_fusion.5
  118.9 1.2 constant_dynamic-update-slice_fusion.4
  120.1 4.5 %fusion.6 = f32[128,512]{1,0:T(8,128)} fusion(bf16[128,6144]{1,0:T(8,128)(2,1)S(1)} %constant_dynamic-update-slice_fusion.4, bf16[1,6144,512]{2,1,0:T(8,128)(2,1)} %param.26), kind=kOutput, calls=%fused_computation.11 | convolution fusion | flops 805306368 | bytes 8126464 | tf_op jit(solution)/shard_map/dot_general | solution.py:131
  124.6 6.7 %convolution_convert_fusion.1 = bf16[128,6144]{1,0:T(8,128)(2,1)S(1)} fusion(bf16[1,512,6144]{2,1,0:T(8,128)(2,1)} %param.27, f32[128,512]{1,0:T(8,128)} %fusion.6, bf16[128,6144]{1,0:T(8,128)(2,1)S(1)} %constant_dynamic-update-slice_fusion.4, bf16[1,6144,512]{2,1,0:T(8,128)(2,1)} %param.25), kind=kOutput, calls=%fused_computation.1 | convolution fusion | flops 1611792384 | bytes 15990784 | tf_op jit(solution)/shard_map/dot_general | solution.py:133
  131.3 3.0 %add_convert_fusion.4 = (bf16[64,6144]{1,0:T(8,128)(2,1)}, bf16[64,6144]{1,0:T(8,128)(2,1)}) fusion(bf16[64,6144]{1,0:T(8,128)(2,1)} %collective-permute-done.11, bf16[128,6144]{1,0:T(8,128)(2,1)S(1)} %convolution_convert_fusion.1, bf16[64,6144]{1,0:T(8,128)(2,1)} %collective-permute-done.19), kind=kLoop, calls=%fused_computation.29 | loop fusion | flops 3145728 | bytes 4718592 | tf_op jit(solution)/shard_map/convert_element_type | solution.py:138
  134.3 1.1 collective-permute-start.14
  135.5 1.6 collective-permute-start.20
  137.0 6.7 %convolution_convert_fusion = bf16[128,6144]{1,0:T(8,128)(2,1)S(1)} fusion(bf16[1,512,6144]{2,1,0:T(8,128)(2,1)} %param.27, f32[128,512]{1,0:T(8,128)} %fusion.4, bf16[128,6144]{1,0:T(8,128)(2,1)S(1)} %copy-done.4, bf16[1,6144,512]{2,1,0:T(8,128)(2,1)} %param.25), kind=kOutput, calls=%fused_computation | convolution fusion | flops 1611792384 | bytes 15990784 | tf_op jit(solution)/shard_map/dot_general | solution.py:133
  143.7 2.0 %collective-permute-done.14 = bf16[64,6144]{1,0:T(8,128)(2,1)} collective-permute-done((bf16[64,6144]{1,0:T(8,128)(2,1)}, bf16[64,6144]{1,0:T(8,128)(2,1)}, u32[]{:S(2)}, u32[]{:S(2)}) %collective-permute-start.14) | collective-permute-done | bytes 786464 | tf_op jit(solution)/shard_map/ppermute | solution.py:28
  145.8 1.1 collective-permute-done.20
  146.9 1.7 add_convert_fusion.3
  149.3 2.6 %collective-permute-start.22 = (bf16[16,6144]{1,0:T(8,128)(2,1)S(1)}, bf16[16,6144]{1,0:T(8,128)(2,1)S(1)}, u32[]{:S(2)}, u32[]{:S(2)}) collective-permute-start(bf16[16,6144]{1,0:T(8,128)(2,1)S(1)} %get-tuple-element.18), channel_id=1, source_target_pairs={{0,64},{32,96},{64,0},{96,32},{1,65},{33,97},{65,1},{97,33},{2,66}... | collective-permute-start | bytes 589832 | tf_op jit(solution)/shard_map/ppermute | solution.py:20
  151.9 1.3 collective-permute-start.21
  153.2 1.5 collective-permute-start.17
  154.7 1.5 collective-permute-start.16
  156.2 3.4 %collective-permute-start.15 = (bf16[16,6144]{1,0:T(8,128)(2,1)S(1)}, bf16[16,6144]{1,0:T(8,128)(2,1)S(1)}, u32[]{:S(2)}, u32[]{:S(2)}) collective-permute-start(bf16[16,6144]{1,0:T(8,128)(2,1)S(1)} %get-tuple-element.13), channel_id=1, source_target_pairs={{0,24},{8,0},{16,8},{24,16},{1,25},{9,1},{17,9},{25,17},{2,26},{10... | collective-permute-start | bytes 589832 | tf_op jit(solution)/shard_map/ppermute | solution.py:20
  159.7 1.6 collective-permute-done.16
  162.5 18.3 %all_to_all.15 = bf16[8,32,768]{2,1,0:T(8,128)(2,1)S(1)} all-to-all(bf16[8,32,768]{2,1,0:T(8,128)(2,1)S(1)} %fusion.29), channel_id=1, replica_groups=mesh['y'=4,'z'=4,'x'=4,'c'=2] {'x','c'}, dimensions={0} | all-to-all | bytes 786432 | tf_op jit(solution)/shard_map/all_to_all | solution.py:164
  180.9 1.8 fusion.21
  (109 shorter events, 15.4 us)
Async XLA Ops:
  0.0 51.5 %copy-start = (bf16[6144,8]{0,1:T(8,128)(2,1)S(1)}, bf16[6144,8]{0,1:T(8,128)(2,1)}, u32[]{:S(2)}) copy-start(bf16[6144,8]{0,1:T(8,128)(2,1)} %param.23) | copy-start | bytes 294916
  2.5 3.9 %copy-start.9 = (bf16[64,128]{1,0:T(8,128)(2,1)S(1)}, bf16[64,128]{1,0:T(8,128)(2,1)}, u32[]{:S(2)}) copy-start(bf16[64,128]{1,0:T(8,128)(2,1)} %param.17) | copy-start | bytes 49156
  2.5 3.9 %copy-start.12 = (bf16[64,256,128]{2,1,0:T(8,128)(2,1)S(1)}, bf16[64,256,128]{2,1,0:T(8,128)(2,1)}, u32[]{:S(2)}) copy-start(bf16[64,256,128]{2,1,0:T(8,128)(2,1)} %param.19) | copy-start | bytes 12582916
  6.5 2.3 %copy-start.5 = (bf16[384,6144]{1,0:T(8,128)(2,1)S(1)}, bf16[384,6144]{1,0:T(8,128)(2,1)}, u32[]{:S(2)}) copy-start(bf16[384,6144]{1,0:T(8,128)(2,1)} %param.21) | copy-start | bytes 14155780
  9.8 6.9 %copy-start.11 = (s32[64,2]{0,1:T(2,128)S(1)}, s32[64,2]{0,1:T(2,128)}, u32[]{:S(2)}) copy-start(s32[64,2]{0,1:T(2,128)} %param.24) | copy-start | bytes 1540
  10.7 54.8 %slice-start = ((s8[6291456]{0:T(1024)(128)(4,1)}), s8[2097152]{0:T(1024)(128)(4,1)S(1)}, s32[]{:S(2)}) async-start(s8[6291456]{0:T(1024)(128)(4,1)} %bitcast.99), calls=%async_computation.3 | async-start | bytes 4194304
  10.7 18.2 %all-to-all-start = ((bf16[8,64,768]{2,1,0:T(8,128)(2,1)}), bf16[8,64,768]{2,1,0:T(8,128)(2,1)S(1)}, u32[]{:S(2)}, u32[]{:S(2)}) async-start(bf16[8,64,768]{2,1,0:T(8,128)(2,1)} %bitcast.98), calls=%async_computation | async-start | bytes 1572864 | tf_op jit(solution)/shard_map/all_to_all | solution.py:103
  16.7 18.5 %copy-start.10 = (bf16[6144]{0:T(1024)(128)(2,1)S(1)}, bf16[6144]{0:T(1024)(128)(2,1)}, u32[]{:S(2)}) copy-start(bf16[6144]{0:T(1024)(128)(2,1)} %param.22) | copy-start | bytes 36868
  31.0 12.3 %all-to-all-start.1 = ((bf16[8,32,768]{2,1,0:T(8,128)(2,1)}), bf16[8,32,768]{2,1,0:T(8,128)(2,1)S(1)}, u32[]{:S(2)}, u32[]{:S(2)}) async-start(bf16[8,32,768]{2,1,0:T(8,128)(2,1)} %bitcast.6), calls=%async_computation.1 | async-start | bytes 786432 | tf_op jit(solution)/shard_map/all_to_all | solution.py:109
  43.8 11.6 %collective-permute-start.2 = (bf16[16,6144]{1,0:T(8,128)(2,1)S(1)}, bf16[16,6144]{1,0:T(8,128)(2,1)S(1)}, u32[]{:S(2)}, u32[]{:S(2)}) collective-permute-start(bf16[16,6144]{1,0:T(8,128)(2,1)S(1)} %bitcast.107), channel_id=1, source_target_pairs={{0,24},{8,0},{16,8},{24,16},{1,25},{9,1},{17,9},{25,17},{2,26},{10... | collective-permute-start | bytes 589832 | tf_op jit(solution)/shard_map/ppermute | solution.py:20
  47.6 9.1 %collective-permute-start.1 = (bf16[16,6144]{1,0:T(8,128)(2,1)S(1)}, bf16[16,6144]{1,0:T(8,128)(2,1)S(1)}, u32[]{:S(2)}, u32[]{:S(2)}) collective-permute-start(bf16[16,6144]{1,0:T(8,128)(2,1)S(1)} %bitcast.108), channel_id=1, source_target_pairs={{0,16},{8,24},{16,0},{24,8},{1,17},{9,25},{17,1},{25,9},{2,18},{10... | collective-permute-start | bytes 589832 | tf_op jit(solution)/shard_map/ppermute | solution.py:20
  47.6 11.9 %collective-permute-start = (bf16[16,6144]{1,0:T(8,128)(2,1)S(1)}, bf16[16,6144]{1,0:T(8,128)(2,1)S(1)}, u32[]{:S(2)}, u32[]{:S(2)}) collective-permute-start(bf16[16,6144]{1,0:T(8,128)(2,1)S(1)} %bitcast.109), channel_id=1, source_target_pairs={{0,8},{8,16},{16,24},{24,0},{1,9},{9,17},{17,25},{25,1},{2,10},{10... | collective-permute-start | bytes 589832 | tf_op jit(solution)/shard_map/ppermute | solution.py:20
  48.3 17.2 %slice-start.1 = ((s8[6291456]{0:T(1024)(128)(4,1)}), s8[4194304]{0:T(1024)(128)(4,1)S(1)}, s32[]{:S(2)}) async-start(s8[6291456]{0:T(1024)(128)(4,1)} %bitcast.99), calls=%async_computation.4 | async-start | bytes 8388608
  48.3 14.0 %collective-permute-start.6 = (bf16[16,6144]{1,0:T(8,128)(2,1)S(1)}, bf16[16,6144]{1,0:T(8,128)(2,1)S(1)}, u32[]{:S(2)}, u32[]{:S(2)}) collective-permute-start(bf16[16,6144]{1,0:T(8,128)(2,1)S(1)} %bitcast.102), channel_id=1, source_target_pairs={{0,96},{32,0},{64,32},{96,64},{1,97},{33,1},{65,33},{97,65},{2,98}... | collective-permute-start | bytes 589832 | tf_op jit(solution)/shard_map/ppermute | solution.py:20
  51.1 11.2 %collective-permute-start.5 = (bf16[16,6144]{1,0:T(8,128)(2,1)S(1)}, bf16[16,6144]{1,0:T(8,128)(2,1)S(1)}, u32[]{:S(2)}, u32[]{:S(2)}) collective-permute-start(bf16[16,6144]{1,0:T(8,128)(2,1)S(1)} %bitcast.103), channel_id=1, source_target_pairs={{0,64},{32,96},{64,0},{96,32},{1,65},{33,97},{65,1},{97,33},{2,66}... | collective-permute-start | bytes 589832 | tf_op jit(solution)/shard_map/ppermute | solution.py:20
  55.4 7.3 %collective-permute-start.4 = (bf16[16,6144]{1,0:T(8,128)(2,1)S(1)}, bf16[16,6144]{1,0:T(8,128)(2,1)S(1)}, u32[]{:S(2)}, u32[]{:S(2)}) collective-permute-start(bf16[16,6144]{1,0:T(8,128)(2,1)S(1)} %bitcast.104), channel_id=1, source_target_pairs={{0,32},{32,64},{64,96},{96,0},{1,33},{33,65},{65,97},{97,1},{2,34}... | collective-permute-start | bytes 589832 | tf_op jit(solution)/shard_map/ppermute | solution.py:20
  59.5 11.7 %collective-permute-start.3 = (bf16[64,6144]{1,0:T(8,128)(2,1)S(1)}, bf16[64,6144]{1,0:T(8,128)(2,1)S(1)}, u32[]{:S(2)}, u32[]{:S(2)}) collective-permute-start(bf16[64,6144]{1,0:T(8,128)(2,1)S(1)} %pad_maximum_fusion), channel_id=1, source_target_pairs={{0,32},{1,97},{32,64},{33,1},{64,96},{65,33},{96,0},{97,65},{2,34}... | collective-permute-start | bytes 2359304 | tf_op jit(solution)/shard_map/ppermute | solution.py:28
  62.7 11.9 %collective-permute-start.7 = (bf16[64,6144]{1,0:T(8,128)(2,1)S(1)}, bf16[64,6144]{1,0:T(8,128)(2,1)S(1)}, u32[]{:S(2)}, u32[]{:S(2)}) collective-permute-start(bf16[64,6144]{1,0:T(8,128)(2,1)S(1)} %pad_maximum_fusion.1), channel_id=1, source_target_pairs={{0,8},{1,25},{8,16},{9,1},{16,24},{17,9},{24,0},{25,17},{2,10},{3,... | collective-permute-start | bytes 2359304 | tf_op jit(solution)/shard_map/ppermute | solution.py:28
  65.5 1.7 copy-start.3
  71.3 3.4 %copy-start.6 = (bf16[64,6144]{1,0:T(8,128)(2,1)}, bf16[64,6144]{1,0:T(8,128)(2,1)S(1)}, u32[]{:S(2)}) copy-start(bf16[64,6144]{1,0:T(8,128)(2,1)S(1)} %collective-permute-done.3) | copy-start | bytes 2359300
  74.6 0.9 copy-start.8
  75.5 1.1 copy-start.2
  77.7 7.1 %copy-start.7 = (bf16[64,6144]{1,0:T(8,128)(2,1)S(1)}, bf16[64,6144]{1,0:T(8,128)(2,1)}, u32[]{:S(2)}) copy-start(bf16[64,6144]{1,0:T(8,128)(2,1)} %copy-done.6) | copy-start | bytes 2359300
  84.8 11.3 %collective-permute-start.9 = (bf16[64,6144]{1,0:T(8,128)(2,1)S(1)}, bf16[64,6144]{1,0:T(8,128)(2,1)}, u32[]{:S(2)}, u32[]{:S(2)}) collective-permute-start(bf16[64,6144]{1,0:T(8,128)(2,1)S(1)} %copy-done.7), channel_id=1, source_target_pairs={{0,32},{1,97},{32,64},{33,1},{64,96},{65,33},{96,0},{97,65},{2,34}... | collective-permute-start | bytes 2359304 | tf_op jit(solution)/shard_map/ppermute | solution.py:28
  85.9 12.4 %collective-permute-start.10 = (bf16[64,6144]{1,0:T(8,128)(2,1)}, bf16[64,6144]{1,0:T(8,128)(2,1)}, u32[]{:S(2)}, u32[]{:S(2)}) collective-permute-start(bf16[64,6144]{1,0:T(8,128)(2,1)} %copy-done.8), channel_id=1, source_target_pairs={{0,8},{1,25},{8,16},{9,1},{16,24},{17,9},{24,0},{25,17},{2,10},{3,... | collective-permute-start | bytes 2359304 | tf_op jit(solution)/shard_map/ppermute | solution.py:28
  90.3 24.4 %collective-permute-start.8 = (bf16[64,6144]{1,0:T(8,128)(2,1)}, bf16[64,6144]{1,0:T(8,128)(2,1)}, u32[]{:S(2)}, u32[]{:S(2)}) collective-permute-start(bf16[64,6144]{1,0:T(8,128)(2,1)} %get-tuple-element.11), channel_id=1, source_target_pairs={{0,32},{1,97},{32,64},{33,1},{64,96},{65,33},{96,0},{97,65},{2,34}... | collective-permute-start | bytes 2359304 | tf_op jit(solution)/shard_map/ppermute | solution.py:28
  90.8 24.0 %collective-permute-start.18 = (bf16[64,6144]{1,0:T(8,128)(2,1)}, bf16[64,6144]{1,0:T(8,128)(2,1)}, u32[]{:S(2)}, u32[]{:S(2)}) collective-permute-start(bf16[64,6144]{1,0:T(8,128)(2,1)} %get-tuple-element.12), channel_id=1, source_target_pairs={{0,8},{1,25},{8,16},{9,1},{16,24},{17,9},{24,0},{25,17},{2,10},{3,... | collective-permute-start | bytes 2359304 | tf_op jit(solution)/shard_map/ppermute | solution.py:28
  104.0 13.7 %collective-permute-start.12 = (bf16[64,6144]{1,0:T(8,128)(2,1)}, bf16[64,6144]{1,0:T(8,128)(2,1)}, u32[]{:S(2)}, u32[]{:S(2)}) collective-permute-start(bf16[64,6144]{1,0:T(8,128)(2,1)} %collective-permute-done.9), channel_id=1, source_target_pairs={{0,32},{1,97},{32,64},{33,1},{64,96},{65,33},{96,0},{97,65},{2,34}... | collective-permute-start | bytes 2359304 | tf_op jit(solution)/shard_map/ppermute | solution.py:28
  105.2 13.7 %collective-permute-start.13 = (bf16[64,6144]{1,0:T(8,128)(2,1)}, bf16[64,6144]{1,0:T(8,128)(2,1)}, u32[]{:S(2)}, u32[]{:S(2)}) collective-permute-start(bf16[64,6144]{1,0:T(8,128)(2,1)} %collective-permute-done.10), channel_id=1, source_target_pairs={{0,8},{1,25},{8,16},{9,1},{16,24},{17,9},{24,0},{25,17},{2,10},{3,... | collective-permute-start | bytes 2359304 | tf_op jit(solution)/shard_map/ppermute | solution.py:28
  117.7 13.6 %collective-permute-start.11 = (bf16[64,6144]{1,0:T(8,128)(2,1)}, bf16[64,6144]{1,0:T(8,128)(2,1)}, u32[]{:S(2)}, u32[]{:S(2)}) collective-permute-start(bf16[64,6144]{1,0:T(8,128)(2,1)} %get-tuple-element.9), channel_id=1, source_target_pairs={{0,32},{1,97},{32,64},{33,1},{64,96},{65,33},{96,0},{97,65},{2,34}... | collective-permute-start | bytes 2359304 | tf_op jit(solution)/shard_map/ppermute | solution.py:28
  117.7 13.6 %collective-permute-start.19 = (bf16[64,6144]{1,0:T(8,128)(2,1)}, bf16[64,6144]{1,0:T(8,128)(2,1)}, u32[]{:S(2)}, u32[]{:S(2)}) collective-permute-start(bf16[64,6144]{1,0:T(8,128)(2,1)} %get-tuple-element.10), channel_id=1, source_target_pairs={{0,8},{1,25},{8,16},{9,1},{16,24},{17,9},{24,0},{25,17},{2,10},{3,... | collective-permute-start | bytes 2359304 | tf_op jit(solution)/shard_map/ppermute | solution.py:28
  131.3 5.8 %copy-start.4 = (bf16[128,6144]{1,0:T(8,128)(2,1)S(1)}, bf16[128,6144]{1,0:T(8,128)(2,1)}, u32[]{:S(2)}) copy-start(bf16[128,6144]{1,0:T(8,128)(2,1)} %copy-done.3) | copy-start | bytes 4718596
  134.3 11.5 %collective-permute-start.14 = (bf16[64,6144]{1,0:T(8,128)(2,1)}, bf16[64,6144]{1,0:T(8,128)(2,1)}, u32[]{:S(2)}, u32[]{:S(2)}) collective-permute-start(bf16[64,6144]{1,0:T(8,128)(2,1)} %get-tuple-element.7), channel_id=1, source_target_pairs={{0,32},{1,97},{32,64},{33,1},{64,96},{65,33},{96,0},{97,65},{2,34}... | collective-permute-start | bytes 2359304 | tf_op jit(solution)/shard_map/ppermute | solution.py:28
  135.5 11.5 %collective-permute-start.20 = (bf16[64,6144]{1,0:T(8,128)(2,1)}, bf16[64,6144]{1,0:T(8,128)(2,1)}, u32[]{:S(2)}, u32[]{:S(2)}) collective-permute-start(bf16[64,6144]{1,0:T(8,128)(2,1)} %get-tuple-element.8), channel_id=1, source_target_pairs={{0,8},{1,25},{8,16},{9,1},{16,24},{17,9},{24,0},{25,17},{2,10},{3,... | collective-permute-start | bytes 2359304 | tf_op jit(solution)/shard_map/ppermute | solution.py:28
  148.7 7.5 %collective-permute-start.23 = (bf16[16,6144]{1,0:T(8,128)(2,1)S(1)}, bf16[16,6144]{1,0:T(8,128)(2,1)S(1)}, u32[]{:S(2)}, u32[]{:S(2)}) collective-permute-start(bf16[16,6144]{1,0:T(8,128)(2,1)S(1)} %get-tuple-element.17), channel_id=1, source_target_pairs={{0,32},{32,64},{64,96},{96,0},{1,33},{33,65},{65,97},{97,1},{2,34}... | collective-permute-start | bytes 589832 | tf_op jit(solution)/shard_map/ppermute | solution.py:20
  149.3 10.3 %collective-permute-start.22 = (bf16[16,6144]{1,0:T(8,128)(2,1)S(1)}, bf16[16,6144]{1,0:T(8,128)(2,1)S(1)}, u32[]{:S(2)}, u32[]{:S(2)}) collective-permute-start(bf16[16,6144]{1,0:T(8,128)(2,1)S(1)} %get-tuple-element.18), channel_id=1, source_target_pairs={{0,64},{32,96},{64,0},{96,32},{1,65},{33,97},{65,1},{97,33},{2,66}... | collective-permute-start | bytes 589832 | tf_op jit(solution)/shard_map/ppermute | solution.py:20
  151.9 7.7 %collective-permute-start.21 = (bf16[16,6144]{1,0:T(8,128)(2,1)S(1)}, bf16[16,6144]{1,0:T(8,128)(2,1)S(1)}, u32[]{:S(2)}, u32[]{:S(2)}) collective-permute-start(bf16[16,6144]{1,0:T(8,128)(2,1)S(1)} %get-tuple-element.16), channel_id=1, source_target_pairs={{0,96},{32,0},{64,32},{96,64},{1,97},{33,1},{65,33},{97,65},{2,98}... | collective-permute-start | bytes 589832 | tf_op jit(solution)/shard_map/ppermute | solution.py:20
  153.2 6.5 %collective-permute-start.17 = (bf16[16,6144]{1,0:T(8,128)(2,1)S(1)}, bf16[16,6144]{1,0:T(8,128)(2,1)S(1)}, u32[]{:S(2)}, u32[]{:S(2)}) collective-permute-start(bf16[16,6144]{1,0:T(8,128)(2,1)S(1)} %get-tuple-element.14), channel_id=1, source_target_pairs={{0,8},{8,16},{16,24},{24,0},{1,9},{9,17},{17,25},{25,1},{2,10},{10... | collective-permute-start | bytes 589832 | tf_op jit(solution)/shard_map/ppermute | solution.py:20
  154.7 6.6 %collective-permute-start.16 = (bf16[16,6144]{1,0:T(8,128)(2,1)S(1)}, bf16[16,6144]{1,0:T(8,128)(2,1)S(1)}, u32[]{:S(2)}, u32[]{:S(2)}) collective-permute-start(bf16[16,6144]{1,0:T(8,128)(2,1)S(1)} %get-tuple-element.15), channel_id=1, source_target_pairs={{0,16},{8,24},{16,0},{24,8},{1,17},{9,25},{17,1},{25,9},{2,18},{10... | collective-permute-start | bytes 589832 | tf_op jit(solution)/shard_map/ppermute | solution.py:20
  156.2 6.0 %collective-permute-start.15 = (bf16[16,6144]{1,0:T(8,128)(2,1)S(1)}, bf16[16,6144]{1,0:T(8,128)(2,1)S(1)}, u32[]{:S(2)}, u32[]{:S(2)}) collective-permute-start(bf16[16,6144]{1,0:T(8,128)(2,1)S(1)} %get-tuple-element.13), channel_id=1, source_target_pairs={{0,24},{8,0},{16,8},{24,16},{1,25},{9,1},{17,9},{25,17},{2,26},{10... | collective-permute-start | bytes 589832 | tf_op jit(solution)/shard_map/ppermute | solution.py:20
  162.3 20.3 %copy-start.1 = (bf16[6144,8]{0,1:T(8,128)(2,1)S(1)}, bf16[6144,8]{0,1:T(8,128)(2,1)}, u32[]{:S(2)}) copy-start(bf16[6144,8]{0,1:T(8,128)(2,1)} %param.23) | copy-start | bytes 294916

commit v2 on v1

v2 whole, which is shorter than its diff:
```python
import math

import jax
import jax.numpy as jnp
from jax import lax
from jax.experimental import pallas as pl
from jax.experimental.pallas import tpu as pltpu
from jax.sharding import Mesh
from jax.sharding import PartitionSpec as P

HD = 128
TOP = 2
MICRO = 2
MB = 32
SIDE = 4
EXPERT_AXES = ("x", "c")
DEEP = 8
WIDE = 6
AHEAD = 4

epsilon = 1e-05


def shift(value, axis, step):
    return lax.ppermute(value, axis, [(i, (i + step) % SIDE) for i in range(SIDE)])


def ring(value, axis):
    perm = []
    for i in range(SIDE):
        perm.append((2 * i, 2 * ((i + 1) % SIDE)))
        perm.append((2 * i + 1, 2 * ((i - 1) % SIDE) + 1))
    return lax.ppermute(value, (axis, "c"), perm)


def swap(value, axis, turn):
    perm = []
    for i in range(SIDE):
        for core in range(2):
            partner = i ^ 1 if core == turn else SIDE - 1 - i
            perm.append((2 * i + core, 2 * partner + core))
    return lax.ppermute(value, (axis, "c"), perm)


def gather_over(value, axis):
    half = jnp.concatenate([value, swap(value, axis, 0)], axis=0)
    return jnp.concatenate([half, swap(half, axis, 1)], axis=0)


def reduce_over(value, axis):
    rows = value.shape[0] // 2
    half = add(value[:rows], swap(value[rows:], axis, 1))
    rows = rows // 2
    return half[:rows].astype(jnp.float32) + swap(half[rows:], axis, 0).astype(jnp.float32)


def add(one, two):
    return (one.astype(jnp.float32) + two.astype(jnp.float32)).astype(jnp.bfloat16)


def expert_kernel(
    first, second, w_gate, w_up, w_down, first_out, second_out, rows, gate_w, up_w, down_w, gate, upper, out, sems, out_sems
):
    count, width = first.shape
    hidden = w_gate.shape[2]
    deep = width // DEEP
    wide = width // WIDE
    copies = [
        (pltpu.make_async_copy(first, rows.at[pl.ds(0, count)], sems.at[0]),),
        (pltpu.make_async_copy(second, rows.at[pl.ds(count, count)], sems.at[1]),),
    ]
    for k in range(DEEP):
        part = pl.ds(k * deep, deep)
        copies.append(
            (
                pltpu.make_async_copy(w_gate.at[0, part], gate_w.at[part], sems.at[2 + 2 * k]),
                pltpu.make_async_copy(w_up.at[0, part], up_w.at[part], sems.at[3 + 2 * k]),
            )
        )
    for n in range(WIDE):
        part = pl.ds(n * wide, wide)
        copies.append(
            (pltpu.make_async_copy(w_down.at[0, :, part], down_w.at[:, part], sems.at[2 + 2 * DEEP + n]),)
        )

    def start(index):
        if index < len(copies):
            for copy in copies[index]:
                copy.start()

    def wait(index):
        for copy in copies[index]:
            copy.wait()

    for index in range(2 + AHEAD):
        start(index)
    wait(0)
    wait(1)
    for k in range(DEEP):
        wait(2 + k)
        start(2 + k + AHEAD)
        part = pl.ds(k * deep, deep)
        more_gate = jnp.dot(rows[:, part], gate_w[part, :], preferred_element_type=jnp.float32)
        more_up = jnp.dot(rows[:, part], up_w[part, :], preferred_element_type=jnp.float32)
        if k == 0:
            gate[...] = more_gate
            upper[...] = more_up
        else:
            gate[...] += more_gate
            upper[...] += more_up
    value = gate[...]
    expanded = (value / (1.0 + jnp.exp(-value)) * upper[...]).astype(jnp.bfloat16)
    writes = []
    for n in range(WIDE):
        wait(2 + DEEP + n)
        start(2 + DEEP + n + AHEAD)
        part = pl.ds(n * wide, wide)
        out[:, part] = jnp.dot(
            expanded, down_w[:, part], preferred_element_type=jnp.float32
        ).astype(jnp.bfloat16)
        for side, target in enumerate((first_out, second_out)):
            write = pltpu.make_async_copy(
                out.at[pl.ds(side * count, count), part], target.at[:, part], out_sems.at[2 * n + side]
            )
            write.start()
            writes.append(write)
    for write in writes:
        write.wait()


def expert(first, second, w_gate, w_up, w_down):
    count, width = first.shape
    hidden = w_gate.shape[2]
    shape = jax.ShapeDtypeStruct((count, width), jnp.bfloat16)
    anywhere = pl.BlockSpec(memory_space=pl.ANY)
    return pl.pallas_call(
        expert_kernel,
        out_shape=(shape, shape),
        in_specs=[anywhere] * 5,
        out_specs=(anywhere, anywhere),
        scratch_shapes=[
            pltpu.VMEM((2 * count, width), jnp.bfloat16),
            pltpu.VMEM((width, hidden), jnp.bfloat16),
            pltpu.VMEM((width, hidden), jnp.bfloat16),
            pltpu.VMEM((hidden, width), jnp.bfloat16),
            pltpu.VMEM((2 * count, hidden), jnp.float32),
            pltpu.VMEM((2 * count, hidden), jnp.float32),
            pltpu.VMEM((2 * count, width), jnp.bfloat16),
            pltpu.SemaphoreType.DMA((2 + 2 * DEEP + WIDE,)),
            pltpu.SemaphoreType.DMA((2 * WIDE,)),
        ],
        compiler_params=pltpu.CompilerParams(vmem_limit_bytes=40 * 1024 * 1024),
        cost_estimate=pl.CostEstimate(
            flops=12 * count * width * hidden, bytes_accessed=6 * width * hidden, transcendentals=0
        ),
        name="expert_rows",
    )(first, second, w_gate, w_up, w_down)


def attend(queries, new_keys, new_values, cache_k, cache_v, lengths):
    count = queries.shape[0]
    length = cache_k.shape[1]
    group = queries.shape[1] // HD
    query = queries.reshape(count, group, HD)
    factor = 1.0 / math.sqrt(HD)
    scores = jnp.einsum("rhd,rld->rhl", query, cache_k, preferred_element_type=jnp.float32) * factor
    itself = (
        jnp.einsum("rhd,rd->rh", query, new_keys, preferred_element_type=jnp.float32) * factor
    )
    valid = (jnp.arange(length)[None, :] < lengths[:, None])[:, None, :]
    masked = jnp.where(valid, scores, -jnp.inf)
    highest = jnp.maximum(jnp.max(masked, axis=-1), itself)
    spread = jnp.exp(masked - highest[..., None])
    own_exp = jnp.exp(itself - highest)
    total = jnp.sum(spread, axis=-1) + own_exp
    weights = (spread / total[..., None]).astype(jnp.bfloat16)
    own_weight = (own_exp / total).astype(jnp.bfloat16)
    mixed = jnp.einsum("rhl,rld->rhd", weights, cache_v, preferred_element_type=jnp.float32)
    mixed = (
        mixed
        + own_weight.astype(jnp.float32)[..., None] * new_values.astype(jnp.float32)[:, None, :]
    )
    return mixed.reshape(count, -1).astype(jnp.bfloat16)


def slot_codes(routes, experts, capacity):
    onehot = (routes[..., None] == jnp.arange(experts, dtype=jnp.int32)).astype(jnp.int32)
    flat = onehot.reshape(MB * TOP, experts)
    before = jnp.cumsum(flat, axis=0) - flat
    return routes * capacity + jnp.sum(before * flat, axis=-1).reshape(MB, TOP)


def body(
    resid,
    queries,
    new_keys,
    new_values,
    cache_k,
    cache_v,
    lengths,
    out_proj,
    norm_gain,
    router,
    route_ids,
    w_gate,
    w_up,
    w_down,
):
    model_width = resid.shape[1]
    experts = router.shape[1]
    capacity = 4 * MB // experts
    share = model_width // experts
    mine = lax.axis_index(EXPERT_AXES)
    places = jnp.arange(experts * capacity, dtype=jnp.int32)[:, None]
    expert_ids = jnp.arange(experts, dtype=jnp.int32)
    own_mask = (expert_ids == mine)[None, :]
    gain = norm_gain.astype(jnp.float32).reshape(experts, 1, share)
    own_resid = lax.dynamic_slice_in_dim(resid, mine * share, share, 1)

    def prepare(batch):
        def part(array):
            return lax.slice_in_dim(array, batch * MB, (batch + 1) * MB, axis=0)

        routes = part(route_ids)
        codes = slot_codes(routes, experts, capacity)
        dispatch = ((codes[None, :, 0] == places) | (codes[None, :, 1] == places)).astype(
            jnp.bfloat16
        )
        heads_out = attend(
            part(queries),
            part(new_keys),
            part(new_values),
            part(cache_k),
            part(cache_v),
            part(lengths),
        )
        partial_out = jnp.dot(heads_out, out_proj, preferred_element_type=jnp.float32).astype(
            jnp.bfloat16
        )
        partial_out = partial_out.reshape(MB, experts, share).transpose(1, 0, 2)
        sums = lax.all_to_all(partial_out, EXPERT_AXES, 0, 0, tiled=True)
        state = part(own_resid).astype(jnp.float32) + jnp.sum(sums.astype(jnp.float32), axis=0)

        sent = jnp.dot(dispatch, state.astype(jnp.bfloat16), preferred_element_type=jnp.float32)
        sent = sent.astype(jnp.bfloat16).reshape(experts, capacity, share)
        rows = lax.all_to_all(sent, EXPERT_AXES, 0, 0, tiled=True).astype(jnp.float32)
        mean_square = jnp.sum(rows * rows, axis=(0, 2)) / model_width
        normed = (rows * lax.rsqrt(mean_square + epsilon)[None, :, None] * gain).astype(
            jnp.bfloat16
        )
        normed = normed.transpose(1, 0, 2).reshape(capacity, model_width)

        logits = jnp.dot(normed, router, preferred_element_type=jnp.float32)
        own_dispatch = lax.dynamic_slice_in_dim(dispatch, mine * capacity, capacity, 0)
        match = jnp.sum((routes[:, :, None] == expert_ids).astype(jnp.bfloat16), axis=1)
        both = jnp.dot(own_dispatch, match, preferred_element_type=jnp.float32)
        own_logit = jnp.sum(jnp.where(own_mask, logits, 0.0), axis=1)
        other_logit = jnp.sum(jnp.where(own_mask, 0.0, logits * both), axis=1)
        gates = (1.0 / (1.0 + jnp.exp(other_logit - own_logit))).astype(jnp.bfloat16)
        return state, dispatch, normed, gates

    def finish(state, dispatch, gates, expert_out):
        weighted = (expert_out * gates.astype(jnp.float32)[:, None]).astype(jnp.bfloat16)
        weighted = weighted.reshape(capacity, experts, share).transpose(1, 0, 2)
        back = lax.all_to_all(weighted, EXPERT_AXES, 0, 0, tiled=True)
        moe = lax.dot_general(
            dispatch,
            back.reshape(experts * capacity, share),
            (((0,), (0,)), ((), ())),
            preferred_element_type=jnp.float32,
        )
        return (state + moe).astype(jnp.bfloat16)

    ready = [prepare(batch) for batch in range(MICRO)]
    first = [gather_over(ready[0][2], "z")]
    second = [gather_over(ready[1][2], "y")]
    for _ in range(SIDE - 1):
        first.append(ring(first[-1], "y"))
        second.append(ring(second[-1], "z"))
    parts = [expert(one, two, w_gate, w_up, w_down) for one, two in zip(first, second)]
    one, two = parts[1]
    for step in (2, 3, 0):
        one = add(ring(one, "y"), parts[step][0])
        two = add(ring(two, "z"), parts[step][1])
    outs = []
    for (state, dispatch, _, gates), total, axis in zip(ready, (one, two), ("z", "y")):
        outs.append(finish(state, dispatch, gates, reduce_over(total, axis)))
    return jnp.concatenate(outs, axis=0)


def solution(mesh):
    fine = Mesh(mesh.devices.reshape(SIDE, SIDE, SIDE, 2), ("y", "z", "x", "c"))
    attn = ("y", "z")
    placed = (
        P(attn, None),
        P(attn, EXPERT_AXES),
        P(attn, EXPERT_AXES),
        P(attn, EXPERT_AXES),
        P(attn, None, EXPERT_AXES),
        P(attn, None, EXPERT_AXES),
        P(attn),
        P(EXPERT_AXES, None),
        P(),
        P(),
        P(attn, None),
        P(EXPERT_AXES, None, attn),
        P(EXPERT_AXES, None, attn),
        P(EXPERT_AXES, attn, None),
    )
    return jax.shard_map(
        body, mesh=fine, in_specs=placed, out_specs=P(attn, EXPERT_AXES), check_vma=False
    )
```

time: 183 us -> 200 us (1.093)
  waiting for transfers between devices: 45.3 us -> 80.9 us
  matrix products: 49.1 us -> 19.4 us
  Pallas kernels: 0 us -> 26.8 us
  blocking collectives: 18.3 us -> 0 us
  starting transfers between devices: 47 us -> 57.5 us
  other arithmetic: 10.1 us -> 4.84 us
  local copies, waits for them, and re-layouts: 12.4 us -> 9.32 us
    dot_general x13 -> x10, matrix products: 43.8 us -> 10.2 us  [the longest x2 4.19 us: prepare(): jnp.dot(heads_out, out_proj, preferred_element_type=jnp.float32)]
    pallas_call x0 -> x4, Pallas kernels: none -> 26.8 us  [expert(): pl.pallas_call(expert_kernel, out_shape=(shape, shape), in_specs=[anywher...]
    all_to_all x2 -> x6, starting transfers between devices: 10.2 us -> 31.9 us  [the longest x2 12.9 us: finish(): back = lax.all_to_all(weighted, EXPERT_AXES, 0, 0, tiled=True)]
    all_to_all x1 -> x0, blocking collectives: 18.3 us -> none  [body(): back = lax.all_to_all(weighted, EXPERT_AXES, 0, 0, tiled=True)]
    ppermute x12, waiting for transfers between devices: 16.8 us -> 33.6 us  [ring(): return lax.ppermute(value, (axis, 'c'), perm)]
    ppermute x12 -> x8, waiting for transfers between devices: 9.06 us -> 21 us  [swap(): return lax.ppermute(value, (axis, 'c'), perm)]
    ppermute x12 -> x8, starting transfers between devices: 19.8 us -> 12.4 us  [swap(): return lax.ppermute(value, (axis, 'c'), perm)]
    all_to_all x2 -> x6, waiting for transfers between devices: 19.4 us -> 26.3 us  [the longest x2 10 us: finish(): back = lax.all_to_all(weighted, EXPERT_AXES, 0, 0, tiled=True)]
  transfers between devices with their start and end apart: 26 -> 26, of which waited for: 13 -> 14; matrix products, arithmetic and copies ran while one was open for 23% -> 10% of each run, Pallas kernels for 0% -> 13%
where the time goes in v2:
time: 200 us; the launch traced here: 199 us
  waiting for transfers between devices  80.9 us (40%)
  starting transfers between devices  57.5 us (29%)
  Pallas kernels  26.8 us (13%)
  matrix products  19.4 us (10%)
  local copies, waits for them, and re-layouts  9.32 us (5%)
  other arithmetic  4.84 us (2%)
    ppermute x12, waiting for transfers between devices, ring(): return lax.ppermute(value, (axis, 'c'), perm)  33.6 us
    pallas_call x4, Pallas kernels, expert(): pl.pallas_call(expert_kernel, out_shape=(shape, shape), in_specs=[anywher...  26.8 us
    ppermute x8, waiting for transfers between devices, swap(): return lax.ppermute(value, (axis, 'c'), perm)  21 us
    ppermute x12, starting transfers between devices, ring(): return lax.ppermute(value, (axis, 'c'), perm)  13.2 us
    all_to_all x2, starting transfers between devices, finish(): back = lax.all_to_all(weighted, EXPERT_AXES, 0, 0, tiled=True)  12.9 us
    ppermute x8, starting transfers between devices, swap(): return lax.ppermute(value, (axis, 'c'), perm)  12.4 us
    all_to_all x2, starting transfers between devices, prepare(): sums = lax.all_to_all(partial_out, EXPERT_AXES, 0, 0, tiled=True)  10.6 us
    all_to_all x2, waiting for transfers between devices, finish(): back = lax.all_to_all(weighted, EXPERT_AXES, 0, 0, tiled=True)  10 us
  transfers between devices with their start and end apart: 26, of which 14 were waited for; matrix products, arithmetic and copies ran while one was open for 10% of the time, Pallas kernels for 13%

profile of v2, /device:TPU:1, one launch (start us, length us, event | category | flops | bytes accessed | tf_op | source)
XLA Modules:
  0.0 199.1 jit_solution(7118761599661959706)
XLA Ops:
  0.0 0.8 fusion.89
  3.3 2.5 %fusion.90 = (f32[32,3]{1,0:T(8,128)S(1)}, f32[32,3,256]{2,1,0:T(4,128)S(1)}) fusion(bf16[32,3,128]{2,1,0:T(4,128)(2,1)S(1)} %reshape.142, bf16[64,256,128]{2,1,0:T(8,128)(2,1)} %param.18, pred[32,256]{1,0:T(8,128)(4,1)S(1)} %get-tuple-element.48), kind=kOutput, calls=%fused_computation.146 | convolution fusion | flops 6365088 | bytes 2228608 | tf_op jit(solution)/shard_map/rhd,rld->rhl/dot_general | solution.py:166
  6.0 2.0 %fusion.28 = bf16[32,3,128]{2,1,0:T(4,128)(2,1)S(1)} fusion(bf16[64,256,128]{2,1,0:T(8,128)(2,1)} %param.19, f32[32,3,256]{2,1,0:T(4,128)S(1)} %get-tuple-element.44, f32[32,3]{1,0:T(8,128)S(1)} %get-tuple-element.28, f32[32,3]{1,0:T(8,128)S(1)} %multiply_maximum_fusion, f32[32,128]{1,0:T(8,128)S(1)} %get-tuple-element.35, f32[32,3]{1,0:T(8,128)S(1)} %get-tuple-element.27), kind=kOutput, calls=%fused_computation.28 | convolution fusion | flops 6402048 | bytes 2237568 | tf_op jit(solution)/shard_map/rhl,rld->rhd/dot_general | solution.py:178
  8.0 0.9 convolution_convert_fusion
  9.0 0.8 copy.73
  9.7 5.8 %all-to-all-start.2 = ((bf16[8,32,768]{2,1,0:T(8,128)(2,1)}), bf16[8,32,768]{2,1,0:T(8,128)(2,1)S(1)}, u32[]{:S(2)}, u32[]{:S(2)}) async-start(bf16[8,32,768]{2,1,0:T(8,128)(2,1)} %bitcast.63), calls=%async_computation.2 | async-start | bytes 786432 | tf_op jit(solution)/shard_map/all_to_all | solution.py:241
  17.3 2.3 %fusion.91 = (f32[32,3]{1,0:T(8,128)S(1)}, f32[32,3,256]{2,1,0:T(4,128)S(1)}) fusion(bf16[32,3,128]{2,1,0:T(4,128)(2,1)S(1)} %reshape.136, bf16[64,256,128]{2,1,0:T(8,128)(2,1)} %param.18, pred[32,256]{1,0:T(8,128)(4,1)S(1)} %get-tuple-element.49), kind=kOutput, calls=%fused_computation.147 | convolution fusion | flops 6365088 | bytes 2228608 | tf_op jit(solution)/shard_map/rhd,rld->rhl/dot_general | solution.py:166
  19.9 2.0 %fusion.31 = bf16[32,3,128]{2,1,0:T(4,128)(2,1)S(1)} fusion(bf16[64,256,128]{2,1,0:T(8,128)(2,1)} %param.19, f32[32,3,256]{2,1,0:T(4,128)S(1)} %get-tuple-element.46, f32[32,3]{1,0:T(8,128)S(1)} %get-tuple-element.32, f32[32,3]{1,0:T(8,128)S(1)} %multiply_maximum_fusion.1, f32[32,128]{1,0:T(8,128)S(1)} %get-tuple-element.36, f32[32,3]{1,0:T(8,128)S(1)} %get-tuple-element.31), kind=kOutput, calls=%fused_computation.29 | convolution fusion | flops 6402048 | bytes 2237568 | tf_op jit(solution)/shard_map/rhl,rld->rhd/dot_general | solution.py:178
  21.9 3.3 %convolution_convert_fusion.1 = bf16[32,6144]{1,0:T(8,128)(2,1)S(1)} fusion(bf16[384,6144]{1,0:T(8,128)(2,1)} %param.21, bf16[4,8,3,128]{3,2,1,0:T(4,128)(2,1)S(1)} %bitcast.89), kind=kOutput, calls=%fused_computation.1 | convolution fusion | flops 151191552 | bytes 5136384 | tf_op jit(solution)/shard_map/dot_general | solution.py:237
  26.3 4.8 %all-to-all-start = ((bf16[8,32,768]{2,1,0:T(8,128)(2,1)}), bf16[8,32,768]{2,1,0:T(8,128)(2,1)S(1)}, u32[]{:S(2)}, u32[]{:S(2)}) async-start(bf16[8,32,768]{2,1,0:T(8,128)(2,1)} %bitcast.65), calls=%async_computation | async-start | bytes 786432 | tf_op jit(solution)/shard_map/all_to_all | solution.py:241
  31.2 1.7 convolution_convert_fusion.2
  32.8 6.4 %all-to-all-done = bf16[8,32,768]{2,1,0:T(8,128)(2,1)S(1)} async-done(((bf16[8,32,768]{2,1,0:T(8,128)(2,1)}), bf16[8,32,768]{2,1,0:T(8,128)(2,1)S(1)}, u32[]{:S(2)}, u32[]{:S(2)}) %all-to-all-start) | async-done | bytes 393248 | tf_op jit(solution)/shard_map/all_to_all | solution.py:241
  39.2 4.2 %all-to-all-start.3 = ((bf16[8,16,768]{2,1,0:T(8,128)(2,1)}), bf16[8,16,768]{2,1,0:T(8,128)(2,1)S(1)}, u32[]{:S(2)}, u32[]{:S(2)}) async-start(bf16[8,16,768]{2,1,0:T(8,128)(2,1)} %bitcast.10), calls=%async_computation.3 | async-start | bytes 393216 | tf_op jit(solution)/shard_map/all_to_all | solution.py:246
  43.4 1.7 convolution_convert_fusion.3
  45.1 4.2 %all-to-all-done.3 = bf16[8,16,768]{2,1,0:T(8,128)(2,1)S(1)} async-done(((bf16[8,16,768]{2,1,0:T(8,128)(2,1)}), bf16[8,16,768]{2,1,0:T(8,128)(2,1)S(1)}, u32[]{:S(2)}, u32[]{:S(2)}) %all-to-all-start.3) | async-done | bytes 196640 | tf_op jit(solution)/shard_map/all_to_all | solution.py:246
  49.3 4.2 %all-to-all-start.1 = ((bf16[8,16,768]{2,1,0:T(8,128)(2,1)}), bf16[8,16,768]{2,1,0:T(8,128)(2,1)S(1)}, u32[]{:S(2)}, u32[]{:S(2)}) async-start(bf16[8,16,768]{2,1,0:T(8,128)(2,1)} %bitcast.4), calls=%async_computation.1 | async-start | bytes 393216 | tf_op jit(solution)/shard_map/all_to_all | solution.py:246
  53.7 5.7 %all-to-all-done.1 = bf16[8,16,768]{2,1,0:T(8,128)(2,1)S(1)} async-done(((bf16[8,16,768]{2,1,0:T(8,128)(2,1)}), bf16[8,16,768]{2,1,0:T(8,128)(2,1)S(1)}, u32[]{:S(2)}, u32[]{:S(2)}) %all-to-all-start.1) | async-done | bytes 196640 | tf_op jit(solution)/shard_map/all_to_all | solution.py:246
  59.8 3.8 %collective-permute-start = (bf16[16,6144]{1,0:T(8,128)(2,1)S(1)}, bf16[16,6144]{1,0:T(8,128)(2,1)S(1)}, u32[]{:S(2)}, u32[]{:S(2)}) collective-permute-start(bf16[16,6144]{1,0:T(8,128)(2,1)S(1)} %bitcast.74), channel_id=1, source_target_pairs={{0,8},{1,25},{8,0},{9,17},{16,24},{17,9},{24,16},{25,1},{2,10},{3,... | collective-permute-start | bytes 589832 | tf_op jit(solution)/shard_map/ppermute | solution.py:42
  63.7 2.8 %collective-permute-start.3 = (bf16[16,6144]{1,0:T(8,128)(2,1)S(1)}, bf16[16,6144]{1,0:T(8,128)(2,1)S(1)}, u32[]{:S(2)}, u32[]{:S(2)}) collective-permute-start(bf16[16,6144]{1,0:T(8,128)(2,1)S(1)} %bitcast.70), channel_id=1, source_target_pairs={{0,32},{1,97},{32,0},{33,65},{64,96},{65,33},{96,64},{97,1},{2,34}... | collective-permute-start | bytes 589832 | tf_op jit(solution)/shard_map/ppermute | solution.py:42
  66.8 2.7 %collective-permute-done.3 = bf16[16,6144]{1,0:T(8,128)(2,1)S(1)} collective-permute-done((bf16[16,6144]{1,0:T(8,128)(2,1)S(1)}, bf16[16,6144]{1,0:T(8,128)(2,1)S(1)}, u32[]{:S(2)}, u32[]{:S(2)}) %collective-permute-start.3) | collective-permute-done | bytes 196640 | tf_op jit(solution)/shard_map/ppermute | solution.py:42
  69.7 6.9 %collective-permute-done.4 = bf16[32,6144]{1,0:T(8,128)(2,1)S(1)} collective-permute-done((bf16[32,6144]{1,0:T(8,128)(2,1)S(1)}, bf16[32,6144]{1,0:T(8,128)(2,1)S(1)}, u32[]{:S(2)}, u32[]{:S(2)}) %collective-permute-start.4) | collective-permute-done | bytes 393248 | tf_op jit(solution)/shard_map/ppermute | solution.py:42
  76.7 2.7 %collective-permute-start.2 = (bf16[64,6144]{1,0:T(8,128)(2,1)S(1)}, bf16[64,6144]{1,0:T(8,128)(2,1)S(1)}, u32[]{:S(2)}, u32[]{:S(2)}) collective-permute-start(bf16[64,6144]{1,0:T(8,128)(2,1)S(1)} %constant_dynamic-update-slice_fusion.first), channel_id=1, source_target_pairs={{0,32},{1,97},{32,64},{33,1},{64,96},{65,33},{96,0},{97,65},{2,34}... | collective-permute-start | bytes 2359304 | tf_op jit(solution)/shard_map/ppermute | solution.py:33
  80.0 7.8 %collective-permute-done.5.second = bf16[64,6144]{1,0:T(8,128)(2,1)S(1)} collective-permute-done((bf16[64,6144]{1,0:T(8,128)(2,1)S(1)}, bf16[64,6144]{1,0:T(8,128)(2,1)S(1)}, u32[]{:S(2)}, u32[]{:S(2)}) %collective-permute-start.5) | collective-permute-done | bytes 786464 | tf_op jit(solution)/shard_map/ppermute | solution.py:33
  87.8 1.2 collective-permute-start.8
  89.0 2.8 %collective-permute-start.7 = (bf16[64,6144]{1,0:T(8,128)(2,1)S(1)}, bf16[64,6144]{1,0:T(8,128)(2,1)S(1)}, u32[]{:S(2)}, u32[]{:S(2)}) collective-permute-start(bf16[64,6144]{1,0:T(8,128)(2,1)S(1)} %collective-permute-done.2.first), channel_id=1, source_target_pairs={{0,32},{1,97},{32,64},{33,1},{64,96},{65,33},{96,0},{97,65},{2,34}... | collective-permute-start | bytes 2359304 | tf_op jit(solution)/shard_map/ppermute | solution.py:33
  91.8 2.8 %copy-done.1 = bf16[1,6144,512]{2,1,0:T(8,128)(2,1)S(1)} copy-done((bf16[1,6144,512]{2,1,0:T(8,128)(2,1)S(1)}, bf16[1,6144,512]{2,1,0:T(8,128)(2,1)}, u32[]{:S(2)}) %copy-start.1) | copy-done | bytes 6291480
  94.6 6.9 %expert_rows.4 = (bf16[64,6144]{1,0:T(8,128)(2,1)S(1)}, bf16[64,6144]{1,0:T(8,128)(2,1)S(1)}) custom-call(bf16[64,6144]{1,0:T(8,128)(2,1)S(1)} %collective-permute-done.2.first, bf16[64,6144]{1,0:T(8,128)(2,1)S(1)} %collective-permute-done.5.second, bf16[1,6144,512]{2,1,0:T(8,128)(2,1)S(1)} %copy-done.1, bf16[1,6144,512]{2,1,0:T(8,128)(2,1)} %w_up.7, ...), custom_call_target="tpu_custom_call" | custom-call | flops 2415919104 | bytes 18874368 | tf_op jit(solution)/shard_map/expert_rows/pallas_call | solution.py:136
  101.5 1.4 collective-permute-start.15
  103.1 6.6 %expert_rows.7 = (bf16[64,6144]{1,0:T(8,128)(2,1)S(1)}, bf16[64,6144]{1,0:T(8,128)(2,1)S(1)}) custom-call(bf16[64,6144]{1,0:T(8,128)(2,1)S(1)} %constant_dynamic-update-slice_fusion.first, bf16[64,6144]{1,0:T(8,128)(2,1)S(1)} %constant_dynamic-update-slice_fusion.3.second, bf16[1,6144,512]{2,1,0:T(8,128)(2,1)S(1)} %copy-done.2, bf16[1,6144,512]{2,1,0:T(8,128)(2,1)} %w_up.7, ...), custom_call_target="tpu_custom_call" | custom-call | flops 2415919104 | bytes 18874368 | tf_op jit(solution)/shard_map/expert_rows/pallas_call | solution.py:136
  109.8 6.6 %expert_rows.5 = (bf16[64,6144]{1,0:T(8,128)(2,1)S(1)}, bf16[64,6144]{1,0:T(8,128)(2,1)S(1)}) custom-call(bf16[64,6144]{1,0:T(8,128)(2,1)S(1)} %collective-permute-done.7.first, bf16[64,6144]{1,0:T(8,128)(2,1)S(1)} %collective-permute-done.8.second, bf16[1,6144,512]{2,1,0:T(8,128)(2,1)S(1)} %copy-done.2, bf16[1,6144,512]{2,1,0:T(8,128)(2,1)} %w_up.7, ...), custom_call_target="tpu_custom_call" | custom-call | flops 2415919104 | bytes 18874368 | tf_op jit(solution)/shard_map/expert_rows/pallas_call | solution.py:136
  116.8 1.9 collective-permute-start.11
  118.8 2.1 %collective-permute-done.6 = bf16[64,6144]{1,0:T(8,128)(2,1)S(1)} collective-permute-done((bf16[64,6144]{1,0:T(8,128)(2,1)S(1)}, bf16[64,6144]{1,0:T(8,128)(2,1)S(1)}, u32[]{:S(2)}, u32[]{:S(2)}) %collective-permute-start.6) | collective-permute-done | bytes 786464 | tf_op jit(solution)/shard_map/ppermute | solution.py:33
  121.1 1.0 collective-permute-start.9
  122.1 14.2 %collective-permute-done.11.second = bf16[64,6144]{1,0:T(8,128)(2,1)S(1)} collective-permute-done((bf16[64,6144]{1,0:T(8,128)(2,1)S(1)}, bf16[64,6144]{1,0:T(8,128)(2,1)S(1)}, u32[]{:S(2)}, u32[]{:S(2)}) %collective-permute-start.11) | collective-permute-done | bytes 786464 | tf_op jit(solution)/shard_map/ppermute | solution.py:33
  136.3 6.6 %expert_rows.6 = (bf16[64,6144]{1,0:T(8,128)(2,1)S(1)}, bf16[64,6144]{1,0:T(8,128)(2,1)S(1)}) custom-call(bf16[64,6144]{1,0:T(8,128)(2,1)S(1)} %collective-permute-done.10.first, bf16[64,6144]{1,0:T(8,128)(2,1)S(1)} %collective-permute-done.11.second, bf16[1,6144,512]{2,1,0:T(8,128)(2,1)S(1)} %copy-done.2, bf16[1,6144,512]{2,1,0:T(8,128)(2,1)} %w_up.7, ...), custom_call_target="tpu_custom_call" | custom-call | flops 2415919104 | bytes 18874368 | tf_op jit(solution)/shard_map/expert_rows/pallas_call | solution.py:136
  143.1 1.7 collective-permute-start.17
  145.0 9.5 %collective-permute-done.17 = bf16[64,6144]{1,0:T(8,128)(2,1)S(1)} collective-permute-done((bf16[64,6144]{1,0:T(8,128)(2,1)S(1)}, bf16[64,6144]{1,0:T(8,128)(2,1)S(1)}, u32[]{:S(2)}, u32[]{:S(2)}) %collective-permute-start.17) | collective-permute-done | bytes 786464 | tf_op jit(solution)/shard_map/ppermute | solution.py:33
  154.7 1.5 collective-permute-start.18
  156.9 7.6 %collective-permute-done.18 = bf16[32,6144]{1,0:T(8,128)(2,1)S(1)} collective-permute-done((bf16[32,6144]{1,0:T(8,128)(2,1)S(1)}, bf16[32,6144]{1,0:T(8,128)(2,1)S(1)}, u32[]{:S(2)}, u32[]{:S(2)}) %collective-permute-start.18) | collective-permute-done | bytes 393248 | tf_op jit(solution)/shard_map/ppermute | solution.py:42
  164.6 1.6 collective-permute-start.19
  166.3 2.0 %collective-permute-start.14 = (bf16[16,6144]{1,0:T(8,128)(2,1)S(1)}, bf16[16,6144]{1,0:T(8,128)(2,1)S(1)}, u32[]{:S(2)}, u32[]{:S(2)}) collective-permute-start(bf16[16,6144]{1,0:T(8,128)(2,1)S(1)} %slice.119), channel_id=1, source_target_pairs={{0,8},{1,25},{8,0},{9,17},{16,24},{17,9},{24,16},{25,1},{2,10},{3,... | collective-permute-start | bytes 589832 | tf_op jit(solution)/shard_map/ppermute | solution.py:42
  168.4 3.6 %collective-permute-done.19 = bf16[16,6144]{1,0:T(8,128)(2,1)S(1)} collective-permute-done((bf16[16,6144]{1,0:T(8,128)(2,1)S(1)}, bf16[16,6144]{1,0:T(8,128)(2,1)S(1)}, u32[]{:S(2)}, u32[]{:S(2)}) %collective-permute-start.19) | collective-permute-done | bytes 196640 | tf_op jit(solution)/shard_map/ppermute | solution.py:42
  172.7 8.6 %all-to-all-start.5 = ((bf16[8,16,768]{2,1,0:T(8,128)(2,1)}), bf16[8,16,768]{2,1,0:T(8,128)(2,1)S(1)}, u32[]{:S(2)}, u32[]{:S(2)}) async-start(bf16[8,16,768]{2,1,0:T(8,128)(2,1)} %bitcast.67), calls=%async_computation.5 | async-start | bytes 393216 | tf_op jit(solution)/shard_map/all_to_all | solution.py:265
  182.2 5.1 %all-to-all-done.5 = bf16[8,16,768]{2,1,0:T(8,128)(2,1)S(1)} async-done(((bf16[8,16,768]{2,1,0:T(8,128)(2,1)}), bf16[8,16,768]{2,1,0:T(8,128)(2,1)S(1)}, u32[]{:S(2)}, u32[]{:S(2)}) %all-to-all-start.5) | async-done | bytes 196640 | tf_op jit(solution)/shard_map/all_to_all | solution.py:265
  187.3 4.2 %all-to-all-start.4 = ((bf16[8,16,768]{2,1,0:T(8,128)(2,1)}), bf16[8,16,768]{2,1,0:T(8,128)(2,1)S(1)}, u32[]{:S(2)}, u32[]{:S(2)}) async-start(bf16[8,16,768]{2,1,0:T(8,128)(2,1)} %bitcast.69), calls=%async_computation.4 | async-start | bytes 393216 | tf_op jit(solution)/shard_map/all_to_all | solution.py:265
  191.5 1.0 fusion.21
  192.5 4.9 %all-to-all-done.4 = bf16[8,16,768]{2,1,0:T(8,128)(2,1)S(1)} async-done(((bf16[8,16,768]{2,1,0:T(8,128)(2,1)}), bf16[8,16,768]{2,1,0:T(8,128)(2,1)S(1)}, u32[]{:S(2)}, u32[]{:S(2)}) %all-to-all-start.4) | async-done | bytes 196640 | tf_op jit(solution)/shard_map/all_to_all | solution.py:265
  197.4 1.0 fusion.20
  (109 shorter events, 12.0 us)
Async XLA Ops:
  0.0 79.5 %copy-start = (bf16[6144,8]{0,1:T(8,128)(2,1)S(1)}, bf16[6144,8]{0,1:T(8,128)(2,1)}, u32[]{:S(2)}) copy-start(bf16[6144,8]{0,1:T(8,128)(2,1)} %param.23) | copy-start | bytes 294916
  3.3 4.8 %copy-start.3 = (bf16[384,6144]{1,0:T(8,128)(2,1)S(1)}, bf16[384,6144]{1,0:T(8,128)(2,1)}, u32[]{:S(2)}) copy-start(bf16[384,6144]{1,0:T(8,128)(2,1)} %param.21) | copy-start | bytes 14155780
  8.0 7.5 %copy-start.5 = (s32[64,2]{0,1:T(2,128)S(1)}, s32[64,2]{0,1:T(2,128)}, u32[]{:S(2)}) copy-start(s32[64,2]{0,1:T(2,128)} %param.24) | copy-start | bytes 1540
  9.7 16.6 %all-to-all-start.2 = ((bf16[8,32,768]{2,1,0:T(8,128)(2,1)}), bf16[8,32,768]{2,1,0:T(8,128)(2,1)S(1)}, u32[]{:S(2)}, u32[]{:S(2)}) async-start(bf16[8,32,768]{2,1,0:T(8,128)(2,1)} %bitcast.63), calls=%async_computation.2 | async-start | bytes 786432 | tf_op jit(solution)/shard_map/all_to_all | solution.py:241
  21.9 3.3 %copy-start.4 = (bf16[6144]{0:T(1024)(128)(2,1)S(1)}, bf16[6144]{0:T(1024)(128)(2,1)}, u32[]{:S(2)}) copy-start(bf16[6144]{0:T(1024)(128)(2,1)} %param.22) | copy-start | bytes 36868
  26.3 12.9 %all-to-all-start = ((bf16[8,32,768]{2,1,0:T(8,128)(2,1)}), bf16[8,32,768]{2,1,0:T(8,128)(2,1)S(1)}, u32[]{:S(2)}, u32[]{:S(2)}) async-start(bf16[8,32,768]{2,1,0:T(8,128)(2,1)} %bitcast.65), calls=%async_computation | async-start | bytes 786432 | tf_op jit(solution)/shard_map/all_to_all | solution.py:241
  39.2 10.1 %all-to-all-start.3 = ((bf16[8,16,768]{2,1,0:T(8,128)(2,1)}), bf16[8,16,768]{2,1,0:T(8,128)(2,1)S(1)}, u32[]{:S(2)}, u32[]{:S(2)}) async-start(bf16[8,16,768]{2,1,0:T(8,128)(2,1)} %bitcast.10), calls=%async_computation.3 | async-start | bytes 393216 | tf_op jit(solution)/shard_map/all_to_all | solution.py:246
  49.3 10.2 %all-to-all-start.1 = ((bf16[8,16,768]{2,1,0:T(8,128)(2,1)}), bf16[8,16,768]{2,1,0:T(8,128)(2,1)S(1)}, u32[]{:S(2)}, u32[]{:S(2)}) async-start(bf16[8,16,768]{2,1,0:T(8,128)(2,1)} %bitcast.4), calls=%async_computation.1 | async-start | bytes 393216 | tf_op jit(solution)/shard_map/all_to_all | solution.py:246
  59.8 6.9 %collective-permute-start = (bf16[16,6144]{1,0:T(8,128)(2,1)S(1)}, bf16[16,6144]{1,0:T(8,128)(2,1)S(1)}, u32[]{:S(2)}, u32[]{:S(2)}) collective-permute-start(bf16[16,6144]{1,0:T(8,128)(2,1)S(1)} %bitcast.74), channel_id=1, source_target_pairs={{0,8},{1,25},{8,0},{9,17},{16,24},{17,9},{24,16},{25,1},{2,10},{3,... | collective-permute-start | bytes 589832 | tf_op jit(solution)/shard_map/ppermute | solution.py:42
  63.7 5.9 %collective-permute-start.3 = (bf16[16,6144]{1,0:T(8,128)(2,1)S(1)}, bf16[16,6144]{1,0:T(8,128)(2,1)S(1)}, u32[]{:S(2)}, u32[]{:S(2)}) collective-permute-start(bf16[16,6144]{1,0:T(8,128)(2,1)S(1)} %bitcast.70), channel_id=1, source_target_pairs={{0,32},{1,97},{32,0},{33,65},{64,96},{65,33},{96,64},{97,1},{2,34}... | collective-permute-start | bytes 589832 | tf_op jit(solution)/shard_map/ppermute | solution.py:42
  66.7 10.0 %collective-permute-start.1 = (bf16[32,6144]{1,0:T(8,128)(2,1)S(1)}, bf16[32,6144]{1,0:T(8,128)(2,1)S(1)}, u32[]{:S(2)}, u32[]{:S(2)}) collective-permute-start(bf16[32,6144]{1,0:T(8,128)(2,1)S(1)} %pad_maximum_fusion), channel_id=1, source_target_pairs={{0,24},{1,9},{8,16},{9,1},{16,8},{17,25},{24,0},{25,17},{2,26},{3,... | collective-permute-start | bytes 1179656 | tf_op jit(solution)/shard_map/ppermute | solution.py:42
  69.6 7.0 %collective-permute-start.4 = (bf16[32,6144]{1,0:T(8,128)(2,1)S(1)}, bf16[32,6144]{1,0:T(8,128)(2,1)S(1)}, u32[]{:S(2)}, u32[]{:S(2)}) collective-permute-start(bf16[32,6144]{1,0:T(8,128)(2,1)S(1)} %pad_maximum_fusion.1), channel_id=1, source_target_pairs={{0,96},{1,33},{32,64},{33,1},{64,32},{65,97},{96,0},{97,65},{2,98}... | collective-permute-start | bytes 1179656 | tf_op jit(solution)/shard_map/ppermute | solution.py:42
  76.6 11.2 %collective-permute-start.5 = (bf16[64,6144]{1,0:T(8,128)(2,1)S(1)}, bf16[64,6144]{1,0:T(8,128)(2,1)S(1)}, u32[]{:S(2)}, u32[]{:S(2)}) collective-permute-start(bf16[64,6144]{1,0:T(8,128)(2,1)S(1)} %constant_dynamic-update-slice_fusion.3.second), channel_id=1, source_target_pairs={{0,8},{1,25},{8,16},{9,1},{16,24},{17,9},{24,0},{25,17},{2,10},{3,... | collective-permute-start | bytes 2359304 | tf_op jit(solution)/shard_map/ppermute | solution.py:33
  76.7 12.3 %collective-permute-start.2 = (bf16[64,6144]{1,0:T(8,128)(2,1)S(1)}, bf16[64,6144]{1,0:T(8,128)(2,1)S(1)}, u32[]{:S(2)}, u32[]{:S(2)}) collective-permute-start(bf16[64,6144]{1,0:T(8,128)(2,1)S(1)} %constant_dynamic-update-slice_fusion.first), channel_id=1, source_target_pairs={{0,32},{1,97},{32,64},{33,1},{64,96},{65,33},{96,0},{97,65},{2,34}... | collective-permute-start | bytes 2359304 | tf_op jit(solution)/shard_map/ppermute | solution.py:33
  87.8 22.0 %collective-permute-start.8 = (bf16[64,6144]{1,0:T(8,128)(2,1)S(1)}, bf16[64,6144]{1,0:T(8,128)(2,1)S(1)}, u32[]{:S(2)}, u32[]{:S(2)}) collective-permute-start(bf16[64,6144]{1,0:T(8,128)(2,1)S(1)} %collective-permute-done.5.second), channel_id=1, source_target_pairs={{0,8},{1,25},{8,16},{9,1},{16,24},{17,9},{24,0},{25,17},{2,10},{3,... | collective-permute-start | bytes 2359304 | tf_op jit(solution)/shard_map/ppermute | solution.py:33
  89.0 20.8 %collective-permute-start.7 = (bf16[64,6144]{1,0:T(8,128)(2,1)S(1)}, bf16[64,6144]{1,0:T(8,128)(2,1)S(1)}, u32[]{:S(2)}, u32[]{:S(2)}) collective-permute-start(bf16[64,6144]{1,0:T(8,128)(2,1)S(1)} %collective-permute-done.2.first), channel_id=1, source_target_pairs={{0,32},{1,97},{32,64},{33,1},{64,96},{65,33},{96,0},{97,65},{2,34}... | collective-permute-start | bytes 2359304 | tf_op jit(solution)/shard_map/ppermute | solution.py:33
  91.8 2.8 %copy-start.1 = (bf16[1,6144,512]{2,1,0:T(8,128)(2,1)S(1)}, bf16[1,6144,512]{2,1,0:T(8,128)(2,1)}, u32[]{:S(2)}) copy-start(bf16[1,6144,512]{2,1,0:T(8,128)(2,1)} %w_gate.7) | copy-start | bytes 18874372
  94.6 8.5 %copy-start.2 = (bf16[1,6144,512]{2,1,0:T(8,128)(2,1)S(1)}, bf16[1,6144,512]{2,1,0:T(8,128)(2,1)}, u32[]{:S(2)}) copy-start(bf16[1,6144,512]{2,1,0:T(8,128)(2,1)} %w_gate.7) | copy-start | bytes 18874372
  101.5 14.9 %collective-permute-start.15 = (bf16[64,6144]{1,0:T(8,128)(2,1)S(1)}, bf16[64,6144]{1,0:T(8,128)(2,1)S(1)}, u32[]{:S(2)}, u32[]{:S(2)}) collective-permute-start(bf16[64,6144]{1,0:T(8,128)(2,1)S(1)} %get-tuple-element.17), channel_id=1, source_target_pairs={{0,8},{1,25},{8,16},{9,1},{16,24},{17,9},{24,0},{25,17},{2,10},{3,... | collective-permute-start | bytes 2359304 | tf_op jit(solution)/shard_map/ppermute | solution.py:33
  109.7 11.2 %collective-permute-start.6 = (bf16[64,6144]{1,0:T(8,128)(2,1)S(1)}, bf16[64,6144]{1,0:T(8,128)(2,1)S(1)}, u32[]{:S(2)}, u32[]{:S(2)}) collective-permute-start(bf16[64,6144]{1,0:T(8,128)(2,1)S(1)} %get-tuple-element.13), channel_id=1, source_target_pairs={{0,32},{1,97},{32,64},{33,1},{64,96},{65,33},{96,0},{97,65},{2,34}... | collective-permute-start | bytes 2359304 | tf_op jit(solution)/shard_map/ppermute | solution.py:33
  116.6 26.3 %collective-permute-start.16 = (bf16[64,6144]{1,0:T(8,128)(2,1)S(1)}, bf16[64,6144]{1,0:T(8,128)(2,1)S(1)}, u32[]{:S(2)}, u32[]{:S(2)}) collective-permute-start(bf16[64,6144]{1,0:T(8,128)(2,1)S(1)} %add_convert_fusion.2), channel_id=1, source_target_pairs={{0,8},{1,25},{8,16},{9,1},{16,24},{17,9},{24,0},{25,17},{2,10},{3,... | collective-permute-start | bytes 2359304 | tf_op jit(solution)/shard_map/ppermute | solution.py:33
  116.8 19.4 %collective-permute-start.11 = (bf16[64,6144]{1,0:T(8,128)(2,1)S(1)}, bf16[64,6144]{1,0:T(8,128)(2,1)S(1)}, u32[]{:S(2)}, u32[]{:S(2)}) collective-permute-start(bf16[64,6144]{1,0:T(8,128)(2,1)S(1)} %collective-permute-done.8.second), channel_id=1, source_target_pairs={{0,8},{1,25},{8,16},{9,1},{16,24},{17,9},{24,0},{25,17},{2,10},{3,... | collective-permute-start | bytes 2359304 | tf_op jit(solution)/shard_map/ppermute | solution.py:33
  118.8 17.5 %collective-permute-start.10 = (bf16[64,6144]{1,0:T(8,128)(2,1)S(1)}, bf16[64,6144]{1,0:T(8,128)(2,1)S(1)}, u32[]{:S(2)}, u32[]{:S(2)}) collective-permute-start(bf16[64,6144]{1,0:T(8,128)(2,1)S(1)} %collective-permute-done.7.first), channel_id=1, source_target_pairs={{0,32},{1,97},{32,64},{33,1},{64,96},{65,33},{96,0},{97,65},{2,34}... | collective-permute-start | bytes 2359304 | tf_op jit(solution)/shard_map/ppermute | solution.py:33
  121.1 23.6 %collective-permute-start.9 = (bf16[64,6144]{1,0:T(8,128)(2,1)S(1)}, bf16[64,6144]{1,0:T(8,128)(2,1)S(1)}, u32[]{:S(2)}, u32[]{:S(2)}) collective-permute-start(bf16[64,6144]{1,0:T(8,128)(2,1)S(1)} %add_convert_fusion.5), channel_id=1, source_target_pairs={{0,32},{1,97},{32,64},{33,1},{64,96},{65,33},{96,0},{97,65},{2,34}... | collective-permute-start | bytes 2359304 | tf_op jit(solution)/shard_map/ppermute | solution.py:33
  143.1 11.4 %collective-permute-start.17 = (bf16[64,6144]{1,0:T(8,128)(2,1)S(1)}, bf16[64,6144]{1,0:T(8,128)(2,1)S(1)}, u32[]{:S(2)}, u32[]{:S(2)}) collective-permute-start(bf16[64,6144]{1,0:T(8,128)(2,1)S(1)} %add_convert_fusion.1), channel_id=1, source_target_pairs={{0,8},{1,25},{8,16},{9,1},{16,24},{17,9},{24,0},{25,17},{2,10},{3,... | collective-permute-start | bytes 2359304 | tf_op jit(solution)/shard_map/ppermute | solution.py:33
  144.9 11.3 %collective-permute-start.12 = (bf16[64,6144]{1,0:T(8,128)(2,1)S(1)}, bf16[64,6144]{1,0:T(8,128)(2,1)S(1)}, u32[]{:S(2)}, u32[]{:S(2)}) collective-permute-start(bf16[64,6144]{1,0:T(8,128)(2,1)S(1)} %add_convert_fusion.4), channel_id=1, source_target_pairs={{0,32},{1,97},{32,64},{33,1},{64,96},{65,33},{96,0},{97,65},{2,34}... | collective-permute-start | bytes 2359304 | tf_op jit(solution)/shard_map/ppermute | solution.py:33
  154.7 9.8 %collective-permute-start.18 = (bf16[32,6144]{1,0:T(8,128)(2,1)S(1)}, bf16[32,6144]{1,0:T(8,128)(2,1)S(1)}, u32[]{:S(2)}, u32[]{:S(2)}) collective-permute-start(bf16[32,6144]{1,0:T(8,128)(2,1)S(1)} %slice.121), channel_id=1, source_target_pairs={{0,96},{1,33},{32,64},{33,1},{64,32},{65,97},{96,0},{97,65},{2,98}... | collective-permute-start | bytes 1179656 | tf_op jit(solution)/shard_map/ppermute | solution.py:42
  156.4 9.8 %collective-permute-start.13 = (bf16[32,6144]{1,0:T(8,128)(2,1)S(1)}, bf16[32,6144]{1,0:T(8,128)(2,1)S(1)}, u32[]{:S(2)}, u32[]{:S(2)}) collective-permute-start(bf16[32,6144]{1,0:T(8,128)(2,1)S(1)} %slice.117), channel_id=1, source_target_pairs={{0,24},{1,9},{8,16},{9,1},{16,8},{17,25},{24,0},{25,17},{2,26},{3,... | collective-permute-start | bytes 1179656 | tf_op jit(solution)/shard_map/ppermute | solution.py:42
  164.6 7.4 %collective-permute-start.19 = (bf16[16,6144]{1,0:T(8,128)(2,1)S(1)}, bf16[16,6144]{1,0:T(8,128)(2,1)S(1)}, u32[]{:S(2)}, u32[]{:S(2)}) collective-permute-start(bf16[16,6144]{1,0:T(8,128)(2,1)S(1)} %slice.123), channel_id=1, source_target_pairs={{0,32},{1,97},{32,0},{33,65},{64,96},{65,33},{96,64},{97,1},{2,34}... | collective-permute-start | bytes 589832 | tf_op jit(solution)/shard_map/ppermute | solution.py:42
  166.3 15.0 %collective-permute-start.14 = (bf16[16,6144]{1,0:T(8,128)(2,1)S(1)}, bf16[16,6144]{1,0:T(8,128)(2,1)S(1)}, u32[]{:S(2)}, u32[]{:S(2)}) collective-permute-start(bf16[16,6144]{1,0:T(8,128)(2,1)S(1)} %slice.119), channel_id=1, source_target_pairs={{0,8},{1,25},{8,0},{9,17},{16,24},{17,9},{24,16},{25,1},{2,10},{3,... | collective-permute-start | bytes 589832 | tf_op jit(solution)/shard_map/ppermute | solution.py:42
  172.7 14.5 %all-to-all-start.5 = ((bf16[8,16,768]{2,1,0:T(8,128)(2,1)}), bf16[8,16,768]{2,1,0:T(8,128)(2,1)S(1)}, u32[]{:S(2)}, u32[]{:S(2)}) async-start(bf16[8,16,768]{2,1,0:T(8,128)(2,1)} %bitcast.67), calls=%async_computation.5 | async-start | bytes 393216 | tf_op jit(solution)/shard_map/all_to_all | solution.py:265
  187.3 10.2 %all-to-all-start.4 = ((bf16[8,16,768]{2,1,0:T(8,128)(2,1)}), bf16[8,16,768]{2,1,0:T(8,128)(2,1)S(1)}, u32[]{:S(2)}, u32[]{:S(2)}) async-start(bf16[8,16,768]{2,1,0:T(8,128)(2,1)} %bitcast.69), calls=%async_computation.4 | async-start | bytes 393216 | tf_op jit(solution)/shard_map/all_to_all | solution.py:265

commit v3 on v1

v3 whole, which is shorter than its diff:
```python
import math

import jax
import jax.numpy as jnp
from jax import lax
from jax.experimental import pallas as pl
from jax.experimental.pallas import tpu as pltpu
from jax.sharding import Mesh
from jax.sharding import PartitionSpec as P

HD = 128
TOP = 2
MICRO = 2
MB = 32
SIDE = 4
EXPERT_AXES = ("x", "c")
DEEP = 8
WIDE = 6
BLOCK = 32
EXPERT_VMEM = 8 * 1024 * 1024
VMEM = 60 * 1024 * 1024

epsilon = 1e-05


def shift(value, axis, step):
    return lax.ppermute(value, axis, [(i, (i + step) % SIDE) for i in range(SIDE)])


def ring(value, axis, turn):
    perm = []
    for i in range(SIDE):
        for core in range(2):
            to = (i + (1 if core == turn else -1)) % SIDE
            perm.append((2 * i + core, 2 * to + core))
    return lax.ppermute(value, (axis, "c"), perm)


def swap(value, axis, turn):
    perm = []
    for i in range(SIDE):
        for core in range(2):
            partner = i ^ 1 if core == turn else SIDE - 1 - i
            perm.append((2 * i + core, 2 * partner + core))
    return lax.ppermute(value, (axis, "c"), perm)


def gather_over(value, axis):
    half = jnp.concatenate([value, swap(value, axis, 0)], axis=0)
    return jnp.concatenate([half, swap(half, axis, 1)], axis=0)


def reduce_over(value, axis):
    rows = value.shape[0] // 2
    half = add(value[:rows], swap(value[rows:], axis, 1))
    rows = rows // 2
    return half[:rows].astype(jnp.float32) + swap(half[rows:], axis, 0).astype(jnp.float32)


def add(one, two):
    return (one.astype(jnp.float32) + two.astype(jnp.float32)).astype(jnp.bfloat16)


def expert_steps(first, second, weights, outs, scratch, arrive):
    w_gate, w_up, w_down = weights
    rows, gate, upper, out, in_sems, out_sems = scratch
    count, width = first.shape
    deep = width // DEEP
    wide = width // WIDE
    halves = [pl.ds(side * count, count) for side in range(2)]
    for side, source in enumerate((first, second)):
        pltpu.make_async_copy(source, rows.at[halves[side]], in_sems.at[side]).wait()
    for k in range(DEEP):
        arrive(k)
        part = pl.ds(k * deep, deep)
        more_gate = jnp.dot(rows[:, part], w_gate[part, :], preferred_element_type=jnp.float32)
        more_up = jnp.dot(rows[:, part], w_up[part, :], preferred_element_type=jnp.float32)
        if k == 0:
            gate[...] = more_gate
            upper[...] = more_up
        else:
            gate[...] += more_gate
            upper[...] += more_up
    value = gate[...]
    expanded = (value / (1.0 + jnp.exp(-value)) * upper[...]).astype(jnp.bfloat16)
    writes = []
    for n in range(WIDE):
        arrive(DEEP + n)
        part = pl.ds(n * wide, wide)
        out[:, part] = jnp.dot(
            expanded, w_down[:, part], preferred_element_type=jnp.float32
        ).astype(jnp.bfloat16)
        for side, target in enumerate(outs):
            write = pltpu.make_async_copy(
                out.at[halves[side], part], target.at[:, part], out_sems.at[2 * n + side]
            )
            write.start()
            writes.append(write)
    for write in writes:
        write.wait()


def start_rows(first, second, rows, in_sems):
    count = first.shape[0]
    for side, source in enumerate((first, second)):
        pltpu.make_async_copy(
            source, rows.at[pl.ds(side * count, count)], in_sems.at[side]
        ).start()


def expert_kernel(first, second, w_gate, w_up, w_down, first_out, second_out, *scratch):
    start_rows(first, second, scratch[0], scratch[4])
    expert_steps(
        first, second, (w_gate, w_up, w_down), (first_out, second_out), scratch, lambda k: None
    )


def first_expert_kernel(
    first, second, w_gate, w_up, w_down, first_out, second_out, kept_gate, kept_up, kept_down, *scratch
):
    deep = w_gate.shape[1] // DEEP
    wide = w_down.shape[2] // WIDE
    sems = scratch[6]
    groups = []
    for k in range(DEEP):
        part = pl.ds(k * deep, deep)
        groups.append(
            (
                pltpu.make_async_copy(w_gate.at[0, part], kept_gate.at[part], sems.at[2 * k]),
                pltpu.make_async_copy(w_up.at[0, part], kept_up.at[part], sems.at[2 * k + 1]),
            )
        )
    for n in range(WIDE):
        part = pl.ds(n * wide, wide)
        groups.append(
            (
                pltpu.make_async_copy(
                    w_down.at[0, :, part], kept_down.at[:, part], sems.at[2 * DEEP + n]
                ),
            )
        )
    start_rows(first, second, scratch[0], scratch[4])
    for group in groups:
        for copy in group:
            copy.start()

    def arrive(k):
        for copy in groups[k]:
            copy.wait()

    expert_steps(
        first, second, (kept_gate, kept_up, kept_down), (first_out, second_out), scratch[:6], arrive
    )


def expert_call(kernel, first, second, weights, hidden, kept):
    count, width = first.shape
    anywhere = pl.BlockSpec(memory_space=pl.ANY)
    near = pl.BlockSpec(memory_space=pltpu.VMEM)
    outs = [jax.ShapeDtypeStruct((count, width), jnp.bfloat16)] * 2
    scratch = [
        pltpu.VMEM((2 * count, width), jnp.bfloat16),
        pltpu.VMEM((2 * count, hidden), jnp.float32),
        pltpu.VMEM((2 * count, hidden), jnp.float32),
        pltpu.VMEM((2 * count, width), jnp.bfloat16),
        pltpu.SemaphoreType.DMA((2,)),
        pltpu.SemaphoreType.DMA((2 * WIDE,)),
    ]
    if kept:
        weights = [pltpu.with_memory_space_constraint(w, pltpu.VMEM) for w in weights]
    else:
        weights = [pltpu.with_memory_space_constraint(w, pltpu.HBM) for w in weights]
        outs += [pltpu.VMEM(w.shape[1:], w.dtype) for w in weights]
        scratch.append(pltpu.SemaphoreType.DMA((2 * DEEP + WIDE,)))
    return pl.pallas_call(
        kernel,
        out_shape=tuple(outs),
        in_specs=[anywhere] * 2 + [near if kept else anywhere] * 3,
        out_specs=(anywhere,) * 2 + (near,) * (len(outs) - 2),
        scratch_shapes=scratch,
        compiler_params=pltpu.CompilerParams(vmem_limit_bytes=EXPERT_VMEM),
        cost_estimate=pl.CostEstimate(flops=1000000, bytes_accessed=100000, transcendentals=0),
        name="expert_rows" if kept else "expert_rows_first",
    )(first, second, *weights)


def hold_kernel(*refs):
    pass


def hold(values, after):
    anywhere = pl.BlockSpec(memory_space=pl.ANY)
    return pl.pallas_call(
        hold_kernel,
        out_shape=tuple(jax.ShapeDtypeStruct(v.shape, v.dtype) for v in values),
        in_specs=[anywhere] * (len(values) + len(after)),
        out_specs=(anywhere,) * len(values),
        input_output_aliases={i: i for i in range(len(values))},
        compiler_params=pltpu.CompilerParams(vmem_limit_bytes=1024 * 1024),
        cost_estimate=pl.CostEstimate(flops=1000, bytes_accessed=1000, transcendentals=0),
        name="hold_rows",
    )(*values, *after)


def attend_kernel(
    where, queries, new_keys, new_values, cache_k, cache_v, lengths, out_proj, mine, theirs, heads, weights, sem
):
    step = pl.program_id(0)
    block = queries.shape[0]
    length = cache_k.shape[1]
    group = queries.shape[1] // HD
    half = 8
    copy = pltpu.make_async_copy(out_proj, weights, sem)

    @pl.when(step == 0)
    def _():
        copy.start()

    factor = 1.0 / math.sqrt(HD)
    column = lax.broadcasted_iota(jnp.int32, (group * half, half * length), 1)
    line = lax.broadcasted_iota(jnp.int32, (group * half, half * length), 0)
    same_row = column // length == line % half
    position = column % length
    turn = lax.broadcasted_iota(jnp.int32, (group * half, 1), 0) % half
    all_queries = queries[...].astype(jnp.float32)
    all_keys = new_keys[...].astype(jnp.float32)
    all_values = new_values[...].astype(jnp.float32)
    outs = []
    for part in range(block // half):
        rows = slice(part * half, (part + 1) * half)
        query = jnp.concatenate(
            [all_queries[rows, h * HD : (h + 1) * HD] for h in range(group)], axis=0
        )
        fresh_key = jnp.concatenate([all_keys[rows]] * group, axis=0)
        fresh_value = jnp.concatenate([all_values[rows]] * group, axis=0)
        used = jnp.zeros((group * half, 1), jnp.int32)
        for r in range(half):
            used = jnp.where(turn == r, lengths[step * block + part * half + r], used)
        keys = cache_k[rows].reshape(half * length, HD)
        values = cache_v[rows].reshape(half * length, HD)
        scores = (
            lax.dot_general(
                query.astype(jnp.bfloat16),
                keys,
                (((1,), (1,)), ((), ())),
                preferred_element_type=jnp.float32,
            )
            * factor
        )
        itself = jnp.sum(query * fresh_key, axis=1, keepdims=True) * factor
        masked = jnp.where(same_row & (position < used), scores, -jnp.inf)
        highest = jnp.maximum(jnp.max(masked, axis=1, keepdims=True), itself)
        spread = jnp.exp(masked - highest)
        own_exp = jnp.exp(itself - highest)
        inverse = 1.0 / (jnp.sum(spread, axis=1, keepdims=True) + own_exp)
        probs = (spread * inverse).astype(jnp.bfloat16)
        own_prob = (own_exp * inverse).astype(jnp.bfloat16).astype(jnp.float32)
        mixed = jnp.dot(probs, values, preferred_element_type=jnp.float32) + own_prob * fresh_value
        outs.append(
            jnp.concatenate([mixed[h * half : (h + 1) * half] for h in range(group)], axis=1)
        )
    heads[pl.ds(step * block, block), :] = jnp.concatenate(outs, axis=0).astype(jnp.bfloat16)

    @pl.when(step == pl.num_programs(0) - 1)
    def _():
        copy.wait()
        share = mine.shape[2]
        left = heads[...]
        for k in range(SIDE):
            chip = lax.rem(where[0] + k, SIDE)
            for core, target in ((where[1], mine), (1 - where[1], theirs)):
                part = pl.ds(pl.multiple_of((chip * 2 + core) * share, share), share)
                target[k] = jnp.dot(
                    left, weights[:, part], preferred_element_type=jnp.float32
                ).astype(jnp.bfloat16)


def attend(where, queries, new_keys, new_values, cache_k, cache_v, lengths, out_proj):
    count, width = queries.shape
    length = cache_k.shape[1]
    share = out_proj.shape[1] // (2 * SIDE)
    shape = jax.ShapeDtypeStruct((SIDE, count, share), jnp.bfloat16)
    whole = pl.BlockSpec((SIDE, count, share), lambda i: (0, 0, 0))
    return pl.pallas_call(
        attend_kernel,
        grid=(count // BLOCK,),
        out_shape=(shape, shape),
        in_specs=[
            pl.BlockSpec(memory_space=pltpu.SMEM),
            pl.BlockSpec((BLOCK, width), lambda i: (i, 0)),
            pl.BlockSpec((BLOCK, HD), lambda i: (i, 0)),
            pl.BlockSpec((BLOCK, HD), lambda i: (i, 0)),
            pl.BlockSpec((BLOCK, length, HD), lambda i: (i, 0, 0)),
            pl.BlockSpec((BLOCK, length, HD), lambda i: (i, 0, 0)),
            pl.BlockSpec(memory_space=pltpu.SMEM),
            pl.BlockSpec(memory_space=pl.ANY),
        ],
        out_specs=(whole, whole),
        scratch_shapes=[
            pltpu.VMEM((count, width), jnp.bfloat16),
            pltpu.VMEM(out_proj.shape, jnp.bfloat16),
            pltpu.SemaphoreType.DMA(()),
        ],
        compiler_params=pltpu.CompilerParams(vmem_limit_bytes=VMEM),
        cost_estimate=pl.CostEstimate(
            flops=2 * count * width * out_proj.shape[1],
            bytes_accessed=4 * count * length * HD,
            transcendentals=0,
        ),
        name="attend_rows",
    )(where, queries, new_keys, new_values, cache_k, cache_v, lengths, out_proj)


def slot_codes(route_ids, experts, capacity):
    routes = route_ids.reshape(MICRO, MB, TOP)
    onehot = (routes[..., None] == jnp.arange(experts, dtype=jnp.int32)).astype(jnp.int32)
    flat = onehot.reshape(MICRO, MB * TOP, experts)
    before = jnp.cumsum(flat, axis=1) - flat
    slots = jnp.sum(before * flat, axis=-1).reshape(MICRO, MB, TOP)
    batch = jnp.arange(MICRO, dtype=jnp.int32)[:, None, None]
    return ((routes * MICRO + batch) * capacity + slots).reshape(MICRO * MB, TOP)


def body(
    resid,
    queries,
    new_keys,
    new_values,
    cache_k,
    cache_v,
    lengths,
    out_proj,
    norm_gain,
    router,
    route_ids,
    w_gate,
    w_up,
    w_down,
):
    count, model_width = resid.shape
    experts = router.shape[1]
    capacity = 4 * MB // experts
    slots = MICRO * capacity
    share = model_width // experts
    mine = lax.axis_index(EXPERT_AXES)
    where = jnp.stack([lax.axis_index("x"), lax.axis_index("c")]).astype(jnp.int32)

    own, others = attend(
        where, queries, new_keys, new_values, cache_k, cache_v, lengths, out_proj
    )
    arrived = lax.ppermute(others, "c", [(0, 1), (1, 0)])
    sums = [add(own[k], arrived[k]) for k in range(SIDE)]
    sums = [sums[0]] + [shift(sums[k], "x", k) for k in range(1, SIDE)]

    route_ids, _ = lax.optimization_barrier((route_ids, own))
    codes = slot_codes(route_ids, experts, capacity)
    places = jnp.arange(experts * slots, dtype=jnp.int32)[:, None]
    dispatch = ((codes[None, :, 0] == places) | (codes[None, :, 1] == places)).astype(jnp.bfloat16)
    slot = jnp.arange(slots, dtype=jnp.int32)[:, None]
    hits = [(c // slots == mine)[None] & (c % slots == slot) for c in (codes[:, 0], codes[:, 1])]
    own_dispatch = (hits[0] | hits[1]).astype(jnp.bfloat16)
    expert_ids = jnp.arange(experts, dtype=jnp.int32)
    match = jnp.sum((route_ids[:, :, None] == expert_ids).astype(jnp.bfloat16), axis=1)
    both = jnp.dot(own_dispatch, match, preferred_element_type=jnp.float32)
    own_mask = (expert_ids == mine)[None, :]

    state = lax.dynamic_slice_in_dim(resid, mine * share, share, 1).astype(jnp.float32)
    for one in sums:
        state = state + one.astype(jnp.float32)
    sent = jnp.dot(dispatch, state.astype(jnp.bfloat16), preferred_element_type=jnp.float32)
    sent = sent.astype(jnp.bfloat16).reshape(experts, slots, share)
    rows = lax.all_to_all(sent, EXPERT_AXES, 0, 0, tiled=True).astype(jnp.float32)
    mean_square = jnp.sum(rows * rows, axis=(0, 2)) / model_width
    gain = norm_gain.astype(jnp.float32).reshape(experts, 1, share)
    normed = (rows * lax.rsqrt(mean_square + epsilon)[None, :, None] * gain).astype(jnp.bfloat16)
    normed = normed.transpose(1, 0, 2).reshape(slots, model_width)

    pieces = [(gather_over(normed[:capacity], "z"), gather_over(normed[capacity:], "y"))]
    (one, two), normed = lax.optimization_barrier((pieces[0], normed))

    logits = jnp.dot(normed, router, preferred_element_type=jnp.float32)
    own_logit = jnp.sum(jnp.where(own_mask, logits, 0.0), axis=1)
    other_logit = jnp.sum(jnp.where(own_mask, 0.0, logits * both), axis=1)
    gates = (1.0 / (1.0 + jnp.exp(other_logit - own_logit))).astype(jnp.bfloat16)

    def step(pair, turn):
        return ring(pair[0], "y", turn), ring(pair[1], "z", turn)

    hidden = w_gate.shape[2]

    def work(pair):
        return expert_call(expert_kernel, *pair, kept, hidden, True)

    def join(left, right):
        return add(left[0], right[0]), add(left[1], right[1])

    piece = (one, two)
    behind = step(piece, 0)
    *own_part, kept_gate, kept_up, kept_down = expert_call(
        first_expert_kernel, *piece, (w_gate, w_up, w_down), hidden, False
    )
    kept = (kept_gate, kept_up, kept_down)
    behind, own_part = lax.optimization_barrier((behind, own_part))
    far = step(behind, 0)
    behind_part = work(behind)
    ahead = step(hold(piece, far), 1)
    far_part = work(far)
    far_sum = step(far_part, 1)
    ahead, far_part = lax.optimization_barrier((ahead, far_part))
    ahead_part = work(ahead)
    from_behind = step(ahead_part, 0)
    far_sum, ahead_part = lax.optimization_barrier((far_sum, ahead_part))
    from_ahead = step(join(far_sum, behind_part), 1)

    def total(side):
        value = own_part[side].astype(jnp.float32) + from_behind[side].astype(jnp.float32)
        return (value + from_ahead[side].astype(jnp.float32)).astype(jnp.bfloat16)

    one, two = total(0), total(1)

    expert_out = jnp.concatenate([reduce_over(one, "z"), reduce_over(two, "y")], axis=0)
    weighted = (expert_out * gates.astype(jnp.float32)[:, None]).astype(jnp.bfloat16)
    weighted = weighted.reshape(slots, experts, share).transpose(1, 0, 2)
    back = lax.all_to_all(weighted, EXPERT_AXES, 0, 0, tiled=True)
    moe = lax.dot_general(
        dispatch,
        back.reshape(experts * slots, share),
        (((0,), (0,)), ((), ())),
        preferred_element_type=jnp.float32,
    )
    return (state + moe).astype(jnp.bfloat16)


def solution(mesh):
    fine = Mesh(mesh.devices.reshape(SIDE, SIDE, SIDE, 2), ("y", "z", "x", "c"))
    attn = ("y", "z")
    placed = (
        P(attn, None),
        P(attn, EXPERT_AXES),
        P(attn, EXPERT_AXES),
        P(attn, EXPERT_AXES),
        P(attn, None, EXPERT_AXES),
        P(attn, None, EXPERT_AXES),
        P(attn),
        P(EXPERT_AXES, None),
        P(),
        P(),
        P(attn, None),
        P(EXPERT_AXES, None, attn),
        P(EXPERT_AXES, None, attn),
        P(EXPERT_AXES, attn, None),
    )
    return jax.shard_map(
        body, mesh=fine, in_specs=placed, out_specs=P(attn, EXPERT_AXES), check_vma=False
    )
```

time: 183 us -> 163 us (0.89)
  matrix products: 49.1 us -> 2.24 us
  Pallas kernels: 0 us -> 28.8 us
  waiting for transfers between devices: 45.3 us -> 64.8 us
  local copies, waits for them, and re-layouts: 12.4 us -> 0.75 us
  starting transfers between devices: 47 us -> 38.1 us
  other arithmetic: 10.1 us -> 4.94 us
  blocking collectives: 18.3 us -> 22.3 us
    dot_general x12 -> x0, matrix products: 45 us -> none  [the longest x4 27.1 us: expert(): jnp.dot(expanded, down_weight, preferred_element_type=jnp.float32)]
    pallas_call x0 -> x6, Pallas kernels: none -> 28.8 us  [the longest x4 20 us: expert_call(): pl.pallas_call(kernel, out_shape=tuple(outs), in_specs=[anywhere] * 2 + [...]
    ppermute x0 -> x9, waiting for transfers between devices: none -> 23.3 us  [the longest x8 22.7 us: swap(): return lax.ppermute(value, (axis, 'c'), perm)]
    ppermute x12 -> x3, starting transfers between devices: 19.8 us -> 4.96 us  [shift(): lax.ppermute(value, axis, [(i, (i + step) % SIDE) for i in range(SIDE)])]
    ppermute x12, waiting for transfers between devices: 16.8 us -> 29.9 us  [ring(): return lax.ppermute(value, (axis, 'c'), perm)]
    ppermute x0 -> x9, starting transfers between devices: none -> 12.6 us  [the longest x8 11.1 us: swap(): return lax.ppermute(value, (axis, 'c'), perm)]
    all_to_all x1 -> x0, waiting for transfers between devices: 11.4 us -> none  [body(): sums = lax.all_to_all(partial_out, EXPERT_AXES, 0, 0, tiled=True)]
    unnamed x42 -> x9, local copies, waits for them, and re-layouts: 6.26 us -> 0.05 us
  transfers between devices with their start and end apart: 26 -> 25, of which waited for: 13 -> 18; matrix products, arithmetic and copies ran while one was open for 23% -> 2% of each run, Pallas kernels for 0% -> 12%
where the time goes in v3:
time: 163 us; the launch traced here: 162 us
  waiting for transfers between devices  64.8 us (40%)
  starting transfers between devices  38.1 us (23%)
  Pallas kernels  28.8 us (18%)
  blocking collectives  22.3 us (14%)
  other arithmetic  4.94 us (3%)
  matrix products  2.24 us (1%)
    ppermute x12, waiting for transfers between devices, ring(): return lax.ppermute(value, (axis, 'c'), perm)  29.9 us
    ppermute x8, waiting for transfers between devices, swap(): return lax.ppermute(value, (axis, 'c'), perm)  22.7 us
    all_to_all x1, blocking collectives, body(): back = lax.all_to_all(weighted, EXPERT_AXES, 0, 0, tiled=True)  22.3 us
    pallas_call x4, Pallas kernels, expert_call(): pl.pallas_call(kernel, out_shape=tuple(outs), in_specs=[anywhere] * 2 + [...  20 us
    ppermute x12, starting transfers between devices, ring(): return lax.ppermute(value, (axis, 'c'), perm)  15.5 us
    ppermute x8, starting transfers between devices, swap(): return lax.ppermute(value, (axis, 'c'), perm)  11.1 us
    pallas_call x1, Pallas kernels, attend(): pl.pallas_call(attend_kernel, grid=(count // BLOCK,), out_shape=(shape, s...  8.78 us
    all_to_all x1, waiting for transfers between devices, body(): lax.all_to_all(sent, EXPERT_AXES, 0, 0, tiled=True).astype(jnp.float32)  8.04 us
  transfers between devices with their start and end apart: 25, of which 18 were waited for; matrix products, arithmetic and copies ran while one was open for 2% of the time, Pallas kernels for 12%

profile of v3, /device:TPU:1, one launch (start us, length us, event | category | flops | bytes accessed | tf_op | source)
XLA Modules:
  0.0 162.3 jit_solution(15382242058876877967)
XLA Ops:
  0.0 0.6 pad_add_fusion.where
  0.6 8.8 %attend_rows.1 = (bf16[4,64,768]{2,1,0:T(8,128)(2,1)}, bf16[4,64,768]{2,1,0:T(8,128)(2,1)}) custom-call(s32[2]{0:T(128)} %pad_add_fusion.where, bf16[64,384]{1,0:T(8,128)(2,1)} %queries.1, bf16[64,128]{1,0:T(8,128)(2,1)} %new_keys.1, bf16[64,128]{1,0:T(8,128)(2,1)} %new_values.1, bf16[64,256,128]{2,1,0:T(8,128)(2,1)} %cache_k.1, ...), custom_call_target="tpu_custom_call" | custom-call | flops 301989888 | bytes 8388608 | tf_op jit(solution)/shard_map/attend_rows/pallas_call | solution.py:284
  9.4 1.5 collective-permute-start
  11.7 0.7 collective-permute-done
  12.4 1.1 fusion.17
  13.5 1.4 collective-permute-start.1
  14.8 2.5 %collective-permute-start.2 = (bf16[64,768]{1,0:T(8,128)(2,1)S(1)}, bf16[64,768]{1,0:T(8,128)(2,1)S(1)}, u32[]{:S(2)}, u32[]{:S(2)}) collective-permute-start(bf16[64,768]{1,0:T(8,128)(2,1)S(1)} %get-tuple-element.65), channel_id=1, source_target_pairs={{0,4},{2,6},{4,0},{6,2},{1,5},{3,7},{5,1},{7,3},{8,12},{10,14},{12... | collective-permute-start | bytes 294920 | tf_op jit(solution)/shard_map/ppermute | solution.py:27
  17.3 1.1 collective-permute-start.3
  18.4 0.3 collective-permute-done.1
  18.8 3.2 %collective-permute-done.2 = bf16[64,768]{1,0:T(8,128)(2,1)S(1)} collective-permute-done((bf16[64,768]{1,0:T(8,128)(2,1)S(1)}, bf16[64,768]{1,0:T(8,128)(2,1)S(1)}, u32[]{:S(2)}, u32[]{:S(2)}) %collective-permute-start.2) | collective-permute-done | bytes 98336 | tf_op jit(solution)/shard_map/ppermute | solution.py:27
  21.9 1.0 fusion.10
  23.0 1.0 convolution_convert_fusion
  24.0 5.1 %all-to-all-start = ((bf16[8,32,768]{2,1,0:T(8,128)(2,1)}), bf16[8,32,768]{2,1,0:T(8,128)(2,1)S(1)}, u32[]{:S(2)}, u32[]{:S(2)}) async-start(bf16[8,32,768]{2,1,0:T(8,128)(2,1)} %bitcast.8), calls=%async_computation | async-start | bytes 786432 | tf_op jit(solution)/shard_map/all_to_all | solution.py:372
  29.1 8.0 %all-to-all-done = bf16[8,32,768]{2,1,0:T(8,128)(2,1)S(1)} async-done(((bf16[8,32,768]{2,1,0:T(8,128)(2,1)}), bf16[8,32,768]{2,1,0:T(8,128)(2,1)S(1)}, u32[]{:S(2)}, u32[]{:S(2)}) %all-to-all-start) | async-done | bytes 393248 | tf_op jit(solution)/shard_map/all_to_all | solution.py:372
  37.6 2.8 %collective-permute-start.6 = (bf16[16,6144]{1,0:T(8,128)(2,1)S(1)}, bf16[16,6144]{1,0:T(8,128)(2,1)S(1)}, u32[]{:S(2)}, u32[]{:S(2)}) collective-permute-start(bf16[16,6144]{1,0:T(8,128)(2,1)S(1)} %bitcast.55), channel_id=1, source_target_pairs={{0,32},{1,97},{32,0},{33,65},{64,96},{65,33},{96,64},{97,1},{2,34}... | collective-permute-start | bytes 589832 | tf_op jit(solution)/shard_map/ppermute | solution.py:45
  40.5 3.8 %collective-permute-start.4 = (bf16[16,6144]{1,0:T(8,128)(2,1)S(1)}, bf16[16,6144]{1,0:T(8,128)(2,1)S(1)}, u32[]{:S(2)}, u32[]{:S(2)}) collective-permute-start(bf16[16,6144]{1,0:T(8,128)(2,1)S(1)} %bitcast.52), channel_id=1, source_target_pairs={{0,8},{1,25},{8,0},{9,17},{16,24},{17,9},{24,16},{25,1},{2,10},{3,... | collective-permute-start | bytes 589832 | tf_op jit(solution)/shard_map/ppermute | solution.py:45
  44.5 2.9 %collective-permute-done.4 = bf16[16,6144]{1,0:T(8,128)(2,1)S(1)} collective-permute-done((bf16[16,6144]{1,0:T(8,128)(2,1)S(1)}, bf16[16,6144]{1,0:T(8,128)(2,1)S(1)}, u32[]{:S(2)}, u32[]{:S(2)}) %collective-permute-start.4) | collective-permute-done | bytes 196640 | tf_op jit(solution)/shard_map/ppermute | solution.py:45
  47.5 3.9 %collective-permute-done.7 = bf16[32,6144]{1,0:T(8,128)(2,1)S(1)} collective-permute-done((bf16[32,6144]{1,0:T(8,128)(2,1)S(1)}, bf16[32,6144]{1,0:T(8,128)(2,1)S(1)}, u32[]{:S(2)}, u32[]{:S(2)}) %collective-permute-start.7) | collective-permute-done | bytes 393248 | tf_op jit(solution)/shard_map/ppermute | solution.py:45
  51.4 3.0 %collective-permute-done.5 = bf16[32,6144]{1,0:T(8,128)(2,1)S(1)} collective-permute-done((bf16[32,6144]{1,0:T(8,128)(2,1)S(1)}, bf16[32,6144]{1,0:T(8,128)(2,1)S(1)}, u32[]{:S(2)}, u32[]{:S(2)}) %collective-permute-start.5) | collective-permute-done | bytes 393248 | tf_op jit(solution)/shard_map/ppermute | solution.py:45
  54.5 2.7 %collective-permute-start.9 = (bf16[64,6144]{1,0:T(8,128)(2,1)S(1)}, bf16[64,6144]{1,0:T(8,128)(2,1)S(1)}, u32[]{:S(2)}, u32[]{:S(2)}) collective-permute-start(bf16[64,6144]{1,0:T(8,128)(2,1)S(1)} %pad_maximum_fusion.1.second.refs_1_), channel_id=1, source_target_pairs={{0,8},{1,25},{8,16},{9,1},{16,24},{17,9},{24,0},{25,17},{2,10},{3,... | collective-permute-start | bytes 2359304 | tf_op jit(solution)/shard_map/ppermute | solution.py:36
  57.3 7.6 %expert_rows_first.1 = (bf16[64,6144]{1,0:T(8,128)(2,1)S(1)}, bf16[64,6144]{1,0:T(8,128)(2,1)S(1)}, bf16[6144,512]{1,0:T(8,128)(2,1)S(1)}, bf16[6144,512]{1,0:T(8,128)(2,1)S(1)}, bf16[512,6144]{1,0:T(8,128)(2,1)S(1)}) custom-call(bf16[64,6144]{1,0:T(8,128)(2,1)S(1)} %pad_maximum_fusion.first.refs_0_, bf16[64,6144]{1,0:T(8,128)(2,1)S(1)} %pad_maximum_fusion.1.second.refs_1_, ...), custom_call_target="tpu_custom_call" | custom-call | flops 1000000 | bytes 100000 | tf_op jit(solution)/shard_map/expert_rows_first/pallas_call | solution.py:175
  64.8 0.8 collective-permute-done.8.first
  65.6 0.6 collective-permute-done.9.second
  66.2 1.4 collective-permute-start.10
  67.6 3.1 %collective-permute-start.11 = (bf16[64,6144]{1,0:T(8,128)(2,1)S(1)}, bf16[64,6144]{1,0:T(8,128)(2,1)S(1)}, u32[]{:S(2)}, u32[]{:S(2)}) collective-permute-start(bf16[64,6144]{1,0:T(8,128)(2,1)S(1)} %collective-permute-done.9.second), channel_id=1, source_target_pairs={{0,8},{1,25},{8,16},{9,1},{16,24},{17,9},{24,0},{25,17},{2,10},{3,... | collective-permute-start | bytes 2359304 | tf_op jit(solution)/shard_map/ppermute | solution.py:36
  70.7 6.6 %collective-permute-done.10.refs_2_.first = bf16[64,6144]{1,0:T(8,128)(2,1)S(1)} collective-permute-done((bf16[64,6144]{1,0:T(8,128)(2,1)S(1)}, bf16[64,6144]{1,0:T(8,128)(2,1)S(1)}, u32[]{:S(2)}, u32[]{:S(2)}) %collective-permute-start.10) | collective-permute-done | bytes 786464 | tf_op jit(solution)/shard_map/ppermute | solution.py:36
  77.3 2.3 %collective-permute-done.11.refs_3_.second = bf16[64,6144]{1,0:T(8,128)(2,1)S(1)} collective-permute-done((bf16[64,6144]{1,0:T(8,128)(2,1)S(1)}, bf16[64,6144]{1,0:T(8,128)(2,1)S(1)}, u32[]{:S(2)}, u32[]{:S(2)}) %collective-permute-start.11) | collective-permute-done | bytes 786464 | tf_op jit(solution)/shard_map/ppermute | solution.py:36
  79.6 0.4 collective-permute-start.12
  80.0 4.1 %expert_rows.3 = (bf16[64,6144]{1,0:T(8,128)(2,1)S(1)}, bf16[64,6144]{1,0:T(8,128)(2,1)S(1)}) custom-call(bf16[64,6144]{1,0:T(8,128)(2,1)S(1)} %collective-permute-done.10.refs_2_.first, bf16[64,6144]{1,0:T(8,128)(2,1)S(1)} %collective-permute-done.11.refs_3_.second, bf16[6144,512]{1,0:T(8,128)(2,1)S(1)} %get-tuple-element.44.w_gate, ...), custom_call_target="tpu_custom_call" | custom-call | flops 1000000 | bytes 100000 | tf_op jit(solution)/shard_map/expert_rows/pallas_call | solution.py:175
  84.2 1.2 collective-permute-start.15
  85.3 1.6 collective-permute-start.16
  87.3 4.2 %expert_rows.5 = (bf16[64,6144]{1,0:T(8,128)(2,1)S(1)}, bf16[64,6144]{1,0:T(8,128)(2,1)S(1)}) custom-call(bf16[64,6144]{1,0:T(8,128)(2,1)S(1)} %collective-permute-done.8.first, bf16[64,6144]{1,0:T(8,128)(2,1)S(1)} %collective-permute-done.9.second, bf16[6144,512]{1,0:T(8,128)(2,1)S(1)} %get-tuple-element.44.w_gate, ...), custom_call_target="tpu_custom_call" | custom-call | flops 1000000 | bytes 100000 | tf_op jit(solution)/shard_map/expert_rows/pallas_call | solution.py:175
  91.7 1.2 collective-permute-done.13.second
  92.9 4.1 %expert_rows.4 = (bf16[64,6144]{1,0:T(8,128)(2,1)S(1)}, bf16[64,6144]{1,0:T(8,128)(2,1)S(1)}) custom-call(bf16[64,6144]{1,0:T(8,128)(2,1)S(1)} %collective-permute-done.12.first, bf16[64,6144]{1,0:T(8,128)(2,1)S(1)} %collective-permute-done.13.second, bf16[6144,512]{1,0:T(8,128)(2,1)S(1)} %get-tuple-element.44.w_gate, ...), custom_call_target="tpu_custom_call" | custom-call | flops 1000000 | bytes 100000 | tf_op jit(solution)/shard_map/expert_rows/pallas_call | solution.py:175
  97.1 2.5 %collective-permute-start.14 = (bf16[64,6144]{1,0:T(8,128)(2,1)S(1)}, bf16[64,6144]{1,0:T(8,128)(2,1)S(1)}, u32[]{:S(2)}, u32[]{:S(2)}) collective-permute-start(bf16[64,6144]{1,0:T(8,128)(2,1)S(1)} %get-tuple-element.51), channel_id=1, source_target_pairs={{0,32},{1,97},{32,64},{33,1},{64,96},{65,33},{96,0},{97,65},{2,34}... | collective-permute-start | bytes 2359304 | tf_op jit(solution)/shard_map/ppermute | solution.py:36
  99.6 1.5 collective-permute-start.20
  101.6 0.7 collective-permute-start.17
  102.5 0.3 collective-permute-start.21
  102.8 16.5 %collective-permute-done.17 = bf16[64,6144]{1,0:T(8,128)(2,1)S(1)} collective-permute-done((bf16[64,6144]{1,0:T(8,128)(2,1)S(1)}, bf16[64,6144]{1,0:T(8,128)(2,1)S(1)}, u32[]{:S(2)}, u32[]{:S(2)}) %collective-permute-start.17) | collective-permute-done | bytes 786464 | tf_op jit(solution)/shard_map/ppermute | solution.py:36
  119.3 0.3 add_convert_fusion.2
  119.7 1.4 collective-permute-done.21
  121.4 2.4 %collective-permute-start.22 = (bf16[32,6144]{1,0:T(8,128)(2,1)S(1)}, bf16[32,6144]{1,0:T(8,128)(2,1)S(1)}, u32[]{:S(2)}, u32[]{:S(2)}) collective-permute-start(bf16[32,6144]{1,0:T(8,128)(2,1)S(1)} %slice.101), channel_id=1, source_target_pairs={{0,96},{1,33},{32,64},{33,1},{64,32},{65,97},{96,0},{97,65},{2,98}... | collective-permute-start | bytes 1179656 | tf_op jit(solution)/shard_map/ppermute | solution.py:45
  123.9 6.6 %collective-permute-done.18 = bf16[32,6144]{1,0:T(8,128)(2,1)S(1)} collective-permute-done((bf16[32,6144]{1,0:T(8,128)(2,1)S(1)}, bf16[32,6144]{1,0:T(8,128)(2,1)S(1)}, u32[]{:S(2)}, u32[]{:S(2)}) %collective-permute-start.18) | collective-permute-done | bytes 393248 | tf_op jit(solution)/shard_map/ppermute | solution.py:45
  130.6 1.2 collective-permute-start.19
  131.9 0.5 collective-permute-start.23
  132.5 6.3 %collective-permute-done.19 = bf16[16,6144]{1,0:T(8,128)(2,1)S(1)} collective-permute-done((bf16[16,6144]{1,0:T(8,128)(2,1)S(1)}, bf16[16,6144]{1,0:T(8,128)(2,1)S(1)}, u32[]{:S(2)}, u32[]{:S(2)}) %collective-permute-start.19) | collective-permute-done | bytes 196640 | tf_op jit(solution)/shard_map/ppermute | solution.py:45
  139.1 22.3 %all_to_all.10 = bf16[8,32,768]{2,1,0:T(8,128)(2,1)S(1)} all-to-all(bf16[8,32,768]{2,1,0:T(8,128)(2,1)S(1)} %fusion.7), channel_id=1, replica_groups=mesh['y'=4,'z'=4,'x'=4,'c'=2] {'x','c'}, dimensions={0} | all-to-all | bytes 786432 | tf_op jit(solution)/shard_map/all_to_all | solution.py:424
  161.4 0.9 fusion
  (66 shorter events, 4.0 us)
Async XLA Ops:
  0.0 86.9 %copy-start = (bf16[6144,8]{0,1:T(8,128)(2,1)S(1)}, bf16[6144,8]{0,1:T(8,128)(2,1)}, u32[]{:S(2)}) copy-start(bf16[6144,8]{0,1:T(8,128)(2,1)} %param.23) | copy-start | bytes 294916
  0.6 10.3 %copy-start.3 = (s32[64,2]{0,1:T(2,128)S(1)}, s32[64,2]{0,1:T(2,128)}, u32[]{:S(2)}) copy-start(s32[64,2]{0,1:T(2,128)} %param.24) | copy-start | bytes 1540
  9.4 3.0 %collective-permute-start = (bf16[4,64,768]{2,1,0:T(8,128)(2,1)}, bf16[4,64,768]{2,1,0:T(8,128)(2,1)S(1)}, u32[]{:S(2)}, u32[]{:S(2)}) collective-permute-start(bf16[4,64,768]{2,1,0:T(8,128)(2,1)} %get-tuple-element.33), channel_id=1, source_target_pairs={{0,1},{1,0},{2,3},{3,2},{4,5},{5,4},{6,7},{7,6},{8,9},{9,8},{10,11... | collective-permute-start | bytes 1179656 | tf_op jit(solution)/shard_map/ppermute | solution.py:351
  11.4 17.6 %copy-start.2 = (bf16[6144]{0:T(1024)(128)(2,1)S(1)}, bf16[6144]{0:T(1024)(128)(2,1)}, u32[]{:S(2)}) copy-start(bf16[6144]{0:T(1024)(128)(2,1)} %param.22) | copy-start | bytes 36868
  13.5 5.3 %collective-permute-start.1 = (bf16[64,768]{1,0:T(8,128)(2,1)S(1)}, bf16[64,768]{1,0:T(8,128)(2,1)S(1)}, u32[]{:S(2)}, u32[]{:S(2)}) collective-permute-start(bf16[64,768]{1,0:T(8,128)(2,1)S(1)} %get-tuple-element.63), channel_id=1, source_target_pairs={{0,2},{2,4},{4,6},{6,0},{1,3},{3,5},{5,7},{7,1},{8,10},{10,12},{12... | collective-permute-start | bytes 294920 | tf_op jit(solution)/shard_map/ppermute | solution.py:27
  14.8 7.1 %collective-permute-start.2 = (bf16[64,768]{1,0:T(8,128)(2,1)S(1)}, bf16[64,768]{1,0:T(8,128)(2,1)S(1)}, u32[]{:S(2)}, u32[]{:S(2)}) collective-permute-start(bf16[64,768]{1,0:T(8,128)(2,1)S(1)} %get-tuple-element.65), channel_id=1, source_target_pairs={{0,4},{2,6},{4,0},{6,2},{1,5},{3,7},{5,1},{7,3},{8,12},{10,14},{12... | collective-permute-start | bytes 294920 | tf_op jit(solution)/shard_map/ppermute | solution.py:27
  17.3 4.7 %collective-permute-start.3 = (bf16[64,768]{1,0:T(8,128)(2,1)S(1)}, bf16[64,768]{1,0:T(8,128)(2,1)S(1)}, u32[]{:S(2)}, u32[]{:S(2)}) collective-permute-start(bf16[64,768]{1,0:T(8,128)(2,1)S(1)} %get-tuple-element.64), channel_id=1, source_target_pairs={{0,6},{2,0},{4,2},{6,4},{1,7},{3,1},{5,3},{7,5},{8,14},{10,8},{12,... | collective-permute-start | bytes 294920 | tf_op jit(solution)/shard_map/ppermute | solution.py:27
  24.0 13.2 %all-to-all-start = ((bf16[8,32,768]{2,1,0:T(8,128)(2,1)}), bf16[8,32,768]{2,1,0:T(8,128)(2,1)S(1)}, u32[]{:S(2)}, u32[]{:S(2)}) async-start(bf16[8,32,768]{2,1,0:T(8,128)(2,1)} %bitcast.8), calls=%async_computation | async-start | bytes 786432 | tf_op jit(solution)/shard_map/all_to_all | solution.py:372
  37.6 6.7 %collective-permute-start.6 = (bf16[16,6144]{1,0:T(8,128)(2,1)S(1)}, bf16[16,6144]{1,0:T(8,128)(2,1)S(1)}, u32[]{:S(2)}, u32[]{:S(2)}) collective-permute-start(bf16[16,6144]{1,0:T(8,128)(2,1)S(1)} %bitcast.55), channel_id=1, source_target_pairs={{0,32},{1,97},{32,0},{33,65},{64,96},{65,33},{96,64},{97,1},{2,34}... | collective-permute-start | bytes 589832 | tf_op jit(solution)/shard_map/ppermute | solution.py:45
  40.5 6.9 %collective-permute-start.4 = (bf16[16,6144]{1,0:T(8,128)(2,1)S(1)}, bf16[16,6144]{1,0:T(8,128)(2,1)S(1)}, u32[]{:S(2)}, u32[]{:S(2)}) collective-permute-start(bf16[16,6144]{1,0:T(8,128)(2,1)S(1)} %bitcast.52), channel_id=1, source_target_pairs={{0,8},{1,25},{8,0},{9,17},{16,24},{17,9},{24,16},{25,1},{2,10},{3,... | collective-permute-start | bytes 589832 | tf_op jit(solution)/shard_map/ppermute | solution.py:45
  44.4 7.0 %collective-permute-start.7 = (bf16[32,6144]{1,0:T(8,128)(2,1)S(1)}, bf16[32,6144]{1,0:T(8,128)(2,1)S(1)}, u32[]{:S(2)}, u32[]{:S(2)}) collective-permute-start(bf16[32,6144]{1,0:T(8,128)(2,1)S(1)} %pad_maximum_fusion.3), channel_id=1, source_target_pairs={{0,96},{1,33},{32,64},{33,1},{64,32},{65,97},{96,0},{97,65},{2,98}... | collective-permute-start | bytes 1179656 | tf_op jit(solution)/shard_map/ppermute | solution.py:45
  47.4 7.0 %collective-permute-start.5 = (bf16[32,6144]{1,0:T(8,128)(2,1)S(1)}, bf16[32,6144]{1,0:T(8,128)(2,1)S(1)}, u32[]{:S(2)}, u32[]{:S(2)}) collective-permute-start(bf16[32,6144]{1,0:T(8,128)(2,1)S(1)} %pad_maximum_fusion.2), channel_id=1, source_target_pairs={{0,24},{1,9},{8,16},{9,1},{16,8},{17,25},{24,0},{25,17},{2,26},{3,... | collective-permute-start | bytes 1179656 | tf_op jit(solution)/shard_map/ppermute | solution.py:45
  54.4 11.2 %collective-permute-start.8 = (bf16[64,6144]{1,0:T(8,128)(2,1)S(1)}, bf16[64,6144]{1,0:T(8,128)(2,1)S(1)}, u32[]{:S(2)}, u32[]{:S(2)}) collective-permute-start(bf16[64,6144]{1,0:T(8,128)(2,1)S(1)} %pad_maximum_fusion.first.refs_0_), channel_id=1, source_target_pairs={{0,32},{1,97},{32,64},{33,1},{64,96},{65,33},{96,0},{97,65},{2,34}... | collective-permute-start | bytes 2359304 | tf_op jit(solution)/shard_map/ppermute | solution.py:36
  54.5 11.7 %collective-permute-start.9 = (bf16[64,6144]{1,0:T(8,128)(2,1)S(1)}, bf16[64,6144]{1,0:T(8,128)(2,1)S(1)}, u32[]{:S(2)}, u32[]{:S(2)}) collective-permute-start(bf16[64,6144]{1,0:T(8,128)(2,1)S(1)} %pad_maximum_fusion.1.second.refs_1_), channel_id=1, source_target_pairs={{0,8},{1,25},{8,16},{9,1},{16,24},{17,9},{24,0},{25,17},{2,10},{3,... | collective-permute-start | bytes 2359304 | tf_op jit(solution)/shard_map/ppermute | solution.py:36
  66.2 11.1 %collective-permute-start.10 = (bf16[64,6144]{1,0:T(8,128)(2,1)S(1)}, bf16[64,6144]{1,0:T(8,128)(2,1)S(1)}, u32[]{:S(2)}, u32[]{:S(2)}) collective-permute-start(bf16[64,6144]{1,0:T(8,128)(2,1)S(1)} %collective-permute-done.8.first), channel_id=1, source_target_pairs={{0,32},{1,97},{32,64},{33,1},{64,96},{65,33},{96,0},{97,65},{2,34}... | collective-permute-start | bytes 2359304 | tf_op jit(solution)/shard_map/ppermute | solution.py:36
  67.6 12.1 %collective-permute-start.11 = (bf16[64,6144]{1,0:T(8,128)(2,1)S(1)}, bf16[64,6144]{1,0:T(8,128)(2,1)S(1)}, u32[]{:S(2)}, u32[]{:S(2)}) collective-permute-start(bf16[64,6144]{1,0:T(8,128)(2,1)S(1)} %collective-permute-done.9.second), channel_id=1, source_target_pairs={{0,8},{1,25},{8,16},{9,1},{16,24},{17,9},{24,0},{25,17},{2,10},{3,... | collective-permute-start | bytes 2359304 | tf_op jit(solution)/shard_map/ppermute | solution.py:36
  79.6 12.1 %collective-permute-start.12 = (bf16[64,6144]{1,0:T(8,128)(2,1)S(1)}, bf16[64,6144]{1,0:T(8,128)(2,1)S(1)}, u32[]{:S(2)}, u32[]{:S(2)}) collective-permute-start(bf16[64,6144]{1,0:T(8,128)(2,1)S(1)} %get-tuple-element.42), channel_id=1, source_target_pairs={{0,96},{1,33},{32,0},{33,65},{64,32},{65,97},{96,64},{97,1},{2,98}... | collective-permute-start | bytes 2359304 | tf_op jit(solution)/shard_map/ppermute | solution.py:36
  80.0 12.9 %collective-permute-start.13 = (bf16[64,6144]{1,0:T(8,128)(2,1)S(1)}, bf16[64,6144]{1,0:T(8,128)(2,1)S(1)}, u32[]{:S(2)}, u32[]{:S(2)}) collective-permute-start(bf16[64,6144]{1,0:T(8,128)(2,1)S(1)} %get-tuple-element.43), channel_id=1, source_target_pairs={{0,24},{1,9},{8,0},{9,17},{16,8},{17,25},{24,16},{25,1},{2,26},{3,... | collective-permute-start | bytes 2359304 | tf_op jit(solution)/shard_map/ppermute | solution.py:36
  84.2 16.9 %collective-permute-start.15 = (bf16[64,6144]{1,0:T(8,128)(2,1)S(1)}, bf16[64,6144]{1,0:T(8,128)(2,1)S(1)}, u32[]{:S(2)}, u32[]{:S(2)}) collective-permute-start(bf16[64,6144]{1,0:T(8,128)(2,1)S(1)} %get-tuple-element.47), channel_id=1, source_target_pairs={{0,96},{1,33},{32,0},{33,65},{64,32},{65,97},{96,64},{97,1},{2,98}... | collective-permute-start | bytes 2359304 | tf_op jit(solution)/shard_map/ppermute | solution.py:36
  85.3 16.0 %collective-permute-start.16 = (bf16[64,6144]{1,0:T(8,128)(2,1)S(1)}, bf16[64,6144]{1,0:T(8,128)(2,1)S(1)}, u32[]{:S(2)}, u32[]{:S(2)}) collective-permute-start(bf16[64,6144]{1,0:T(8,128)(2,1)S(1)} %get-tuple-element.48), channel_id=1, source_target_pairs={{0,24},{1,9},{8,0},{9,17},{16,8},{17,25},{24,16},{25,1},{2,26},{3,... | collective-permute-start | bytes 2359304 | tf_op jit(solution)/shard_map/ppermute | solution.py:36
  97.1 22.2 %collective-permute-start.14 = (bf16[64,6144]{1,0:T(8,128)(2,1)S(1)}, bf16[64,6144]{1,0:T(8,128)(2,1)S(1)}, u32[]{:S(2)}, u32[]{:S(2)}) collective-permute-start(bf16[64,6144]{1,0:T(8,128)(2,1)S(1)} %get-tuple-element.51), channel_id=1, source_target_pairs={{0,32},{1,97},{32,64},{33,1},{64,96},{65,33},{96,0},{97,65},{2,34}... | collective-permute-start | bytes 2359304 | tf_op jit(solution)/shard_map/ppermute | solution.py:36
  99.6 21.5 %collective-permute-start.20 = (bf16[64,6144]{1,0:T(8,128)(2,1)S(1)}, bf16[64,6144]{1,0:T(8,128)(2,1)S(1)}, u32[]{:S(2)}, u32[]{:S(2)}) collective-permute-start(bf16[64,6144]{1,0:T(8,128)(2,1)S(1)} %get-tuple-element.52), channel_id=1, source_target_pairs={{0,8},{1,25},{8,16},{9,1},{16,24},{17,9},{24,0},{25,17},{2,10},{3,... | collective-permute-start | bytes 2359304 | tf_op jit(solution)/shard_map/ppermute | solution.py:36
  101.6 17.8 %collective-permute-start.17 = (bf16[64,6144]{1,0:T(8,128)(2,1)S(1)}, bf16[64,6144]{1,0:T(8,128)(2,1)S(1)}, u32[]{:S(2)}, u32[]{:S(2)}) collective-permute-start(bf16[64,6144]{1,0:T(8,128)(2,1)S(1)} %add_convert_fusion.3), channel_id=1, source_target_pairs={{0,96},{1,33},{32,0},{33,65},{64,32},{65,97},{96,64},{97,1},{2,98}... | collective-permute-start | bytes 2359304 | tf_op jit(solution)/shard_map/ppermute | solution.py:36
  102.5 18.7 %collective-permute-start.21 = (bf16[64,6144]{1,0:T(8,128)(2,1)S(1)}, bf16[64,6144]{1,0:T(8,128)(2,1)S(1)}, u32[]{:S(2)}, u32[]{:S(2)}) collective-permute-start(bf16[64,6144]{1,0:T(8,128)(2,1)S(1)} %add_convert_fusion.1), channel_id=1, source_target_pairs={{0,24},{1,9},{8,0},{9,17},{16,8},{17,25},{24,16},{25,1},{2,26},{3,... | collective-permute-start | bytes 2359304 | tf_op jit(solution)/shard_map/ppermute | solution.py:36
  119.6 10.8 %collective-permute-start.18 = (bf16[32,6144]{1,0:T(8,128)(2,1)S(1)}, bf16[32,6144]{1,0:T(8,128)(2,1)S(1)}, u32[]{:S(2)}, u32[]{:S(2)}) collective-permute-start(bf16[32,6144]{1,0:T(8,128)(2,1)S(1)} %slice.97), channel_id=1, source_target_pairs={{0,24},{1,9},{8,16},{9,1},{16,8},{17,25},{24,0},{25,17},{2,26},{3,... | collective-permute-start | bytes 1179656 | tf_op jit(solution)/shard_map/ppermute | solution.py:45
  121.4 10.4 %collective-permute-start.22 = (bf16[32,6144]{1,0:T(8,128)(2,1)S(1)}, bf16[32,6144]{1,0:T(8,128)(2,1)S(1)}, u32[]{:S(2)}, u32[]{:S(2)}) collective-permute-start(bf16[32,6144]{1,0:T(8,128)(2,1)S(1)} %slice.101), channel_id=1, source_target_pairs={{0,96},{1,33},{32,64},{33,1},{64,32},{65,97},{96,0},{97,65},{2,98}... | collective-permute-start | bytes 1179656 | tf_op jit(solution)/shard_map/ppermute | solution.py:45
  130.6 8.2 %collective-permute-start.19 = (bf16[16,6144]{1,0:T(8,128)(2,1)S(1)}, bf16[16,6144]{1,0:T(8,128)(2,1)S(1)}, u32[]{:S(2)}, u32[]{:S(2)}) collective-permute-start(bf16[16,6144]{1,0:T(8,128)(2,1)S(1)} %slice.99), channel_id=1, source_target_pairs={{0,8},{1,25},{8,0},{9,17},{16,24},{17,9},{24,16},{25,1},{2,10},{3,... | collective-permute-start | bytes 589832 | tf_op jit(solution)/shard_map/ppermute | solution.py:45
  131.9 6.9 %collective-permute-start.23 = (bf16[16,6144]{1,0:T(8,128)(2,1)S(1)}, bf16[16,6144]{1,0:T(8,128)(2,1)S(1)}, u32[]{:S(2)}, u32[]{:S(2)}) collective-permute-start(bf16[16,6144]{1,0:T(8,128)(2,1)S(1)} %slice.103), channel_id=1, source_target_pairs={{0,32},{1,97},{32,0},{33,65},{64,96},{65,33},{96,64},{97,1},{2,34}... | collective-permute-start | bytes 589832 | tf_op jit(solution)/shard_map/ppermute | solution.py:45
  138.9 23.4 %copy-start.1 = (bf16[6144,8]{0,1:T(8,128)(2,1)S(1)}, bf16[6144,8]{0,1:T(8,128)(2,1)}, u32[]{:S(2)}) copy-start(bf16[6144,8]{0,1:T(8,128)(2,1)} %param.23) | copy-start | bytes 294916

commit v4 on v3

--- a/solution.py
+++ b/solution.py
@@ -1,3 +1,4 @@
+import functools
 import math
 
 import jax
@@ -45,33 +46,64 @@
     return lax.ppermute(value, (axis, "c"), perm)
 
 
-def gather_over(value, axis):
-    half = jnp.concatenate([value, swap(value, axis, 0)], axis=0)
-    return jnp.concatenate([half, swap(half, axis, 1)], axis=0)
-
-
-def reduce_over(value, axis):
-    rows = value.shape[0] // 2
-    half = add(value[:rows], swap(value[rows:], axis, 1))
-    rows = rows // 2
-    return half[:rows].astype(jnp.float32) + swap(half[rows:], axis, 0).astype(jnp.float32)
-
-
 def add(one, two):
     return (one.astype(jnp.float32) + two.astype(jnp.float32)).astype(jnp.bfloat16)
 
 
-def expert_steps(first, second, weights, outs, scratch, arrive):
-    w_gate, w_up, w_down = weights
-    rows, gate, upper, out, in_sems, out_sems = scratch
-    count, width = first.shape
+def expert_kernel(taken, given, kept, waits, *refs):
+    sources, refs = refs[: len(taken)], refs[len(taken) :]
+    weights, refs = refs[:3], refs[3 + waits :]
+    targets, refs = refs[: len(given)], refs[len(given) :]
+    if not kept:
+        near, refs = refs[:3], refs[3:]
+        weight_sems, refs = refs[-1], refs[:-1]
+    rows, gate, upper, out, in_sems, out_sems = refs
+    width = rows.shape[1]
     deep = width // DEEP
     wide = width // WIDE
-    halves = [pl.ds(side * count, count) for side in range(2)]
-    for side, source in enumerate((first, second)):
-        pltpu.make_async_copy(source, rows.at[halves[side]], in_sems.at[side]).wait()
+
+    arrivals = []
+    place = 0
+    for index, (source, count) in enumerate(zip(sources, taken)):
+        arrivals.append(
+            pltpu.make_async_copy(source, rows.at[pl.ds(place, count)], in_sems.at[index])
+        )
+        place += count
+    for copy in arrivals:
+        copy.start()
+    groups = [()] * (DEEP + WIDE)
+    if not kept:
+        groups = []
+        for k in range(DEEP):
+            part = pl.ds(k * deep, deep)
+            groups.append(
+                tuple(
+                    pltpu.make_async_copy(
+                        weights[w].at[0, part], near[w].at[part], weight_sems.at[2 * k + w]
+                    )
+                    for w in range(2)
+                )
+            )
+        for n in range(WIDE):
+            part = pl.ds(n * wide, wide)
+            groups.append(
+                (
+                    pltpu.make_async_copy(
+                        weights[2].at[0, :, part], near[2].at[:, part], weight_sems.at[2 * DEEP + n]
+                    ),
+                )
+            )
+        for group in groups:
+            for copy in group:
+                copy.start()
+        weights = near
+    w_gate, w_up, w_down = weights
+    for copy in arrivals:
+        copy.wait()
+
     for k in range(DEEP):
-        arrive(k)
+        for copy in groups[k]:
+            copy.wait()
         part = pl.ds(k * deep, deep)
         more_gate = jnp.dot(rows[:, part], w_gate[part, :], preferred_element_type=jnp.float32)
         more_up = jnp.dot(rows[:, part], w_up[part, :], preferred_element_type=jnp.float32)
@@ -85,86 +117,40 @@
     expanded = (value / (1.0 + jnp.exp(-value)) * upper[...]).astype(jnp.bfloat16)
     writes = []
     for n in range(WIDE):
-        arrive(DEEP + n)
+        for copy in groups[DEEP + n]:
+            copy.wait()
         part = pl.ds(n * wide, wide)
         out[:, part] = jnp.dot(
             expanded, w_down[:, part], preferred_element_type=jnp.float32
         ).astype(jnp.bfloat16)
-        for side, target in enumerate(outs):
+        place = 0
+        for index, (target, count) in enumerate(zip(targets, given)):
             write = pltpu.make_async_copy(
-                out.at[halves[side], part], target.at[:, part], out_sems.at[2 * n + side]
+                out.at[pl.ds(place, count), part],
+                target.at[:, part],
+                out_sems.at[n * len(given) + index],
             )
             write.start()
             writes.append(write)
+            place += count
     for write in writes:
         write.wait()
 
 
-def start_rows(first, second, rows, in_sems):
-    count = first.shape[0]
-    for side, source in enumerate((first, second)):
-        pltpu.make_async_copy(
-            source, rows.at[pl.ds(side * count, count)], in_sems.at[side]
-        ).start()
-
-
-def expert_kernel(first, second, w_gate, w_up, w_down, first_out, second_out, *scratch):
-    start_rows(first, second, scratch[0], scratch[4])
-    expert_steps(
-        first, second, (w_gate, w_up, w_down), (first_out, second_out), scratch, lambda k: None
-    )
-
-
-def first_expert_kernel(
-    first, second, w_gate, w_up, w_down, first_out, second_out, kept_gate, kept_up, kept_down, *scratch
-):
-    deep = w_gate.shape[1] // DEEP
-    wide = w_down.shape[2] // WIDE
-    sems = scratch[6]
-    groups = []
-    for k in range(DEEP):
-        part = pl.ds(k * deep, deep)
-        groups.append(
-            (
-                pltpu.make_async_copy(w_gate.at[0, part], kept_gate.at[part], sems.at[2 * k]),
-                pltpu.make_async_copy(w_up.at[0, part], kept_up.at[part], sems.at[2 * k + 1]),
-            )
-        )
-    for n in range(WIDE):
-        part = pl.ds(n * wide, wide)
-        groups.append(
-            (
-                pltpu.make_async_copy(
-                    w_down.at[0, :, part], kept_down.at[:, part], sems.at[2 * DEEP + n]
-                ),
-            )
-        )
-    start_rows(first, second, scratch[0], scratch[4])
-    for group in groups:
-        for copy in group:
-            copy.start()
-
-    def arrive(k):
-        for copy in groups[k]:
-            copy.wait()
-
-    expert_steps(
-        first, second, (kept_gate, kept_up, kept_down), (first_out, second_out), scratch[:6], arrive
-    )
-
-
-def expert_call(kernel, first, second, weights, hidden, kept):
-    count, width = first.shape
+def expert_call(pieces, given, weights, kept, after=()):
+    taken = tuple(p.shape[0] for p in pieces)
+    total, width = sum(taken), pieces[0].shape[1]
+    hidden = weights[2].shape[-2]
     anywhere = pl.BlockSpec(memory_space=pl.ANY)
     near = pl.BlockSpec(memory_space=pltpu.VMEM)
-    outs = [jax.ShapeDtypeStruct((count, width), jnp.bfloat16)] * 2
+    outs = [jax.ShapeDtypeStruct((count, width), jnp.bfloat16) for count in given]
     scratch = [
-        pltpu.VMEM((2 * count, width), jnp.bfloat16),
-        pltpu.VMEM((2 * count, hidden), jnp.float32),
-        pltpu.VMEM((2 * count, hidden), jnp.float32),
-        pltpu.VMEM((2 * count, width), jnp.bfloat16),
-        pltpu.SemaphoreType.DMA((2,)),
-        pltpu.SemaphoreType.DMA((2 * WIDE,)),
+        pltpu.VMEM((total, width), jnp.bfloat16),
+        pltpu.VMEM((total, hidden), jnp.float32),
+        pltpu.VMEM((total, hidden), jnp.float32),
+        pltpu.VMEM((total, width), jnp.bfloat16),
+        pltpu.SemaphoreType.DMA((len(taken),)),
+        pltpu.SemaphoreType.DMA((len(given) * WIDE,)),
     ]
     if kept:
         weights = [pltpu.with_memory_space_constraint(w, pltpu.VMEM) for w in weights]
@@ -172,34 +158,48 @@
         weights = [pltpu.with_memory_space_constraint(w, pltpu.HBM) for w in weights]
         outs += [pltpu.VMEM(w.shape[1:], w.dtype) for w in weights]
         scratch.append(pltpu.SemaphoreType.DMA((2 * DEEP + WIDE,)))
-    return pl.pallas_call(
-        kernel,
+    results = pl.pallas_call(
+        functools.partial(expert_kernel, taken, given, kept, len(after)),
         out_shape=tuple(outs),
-        in_specs=[anywhere] * 2 + [near if kept else anywhere] * 3,
-        out_specs=(anywhere,) * 2 + (near,) * (len(outs) - 2),
+        in_specs=[anywhere] * len(taken)
+        + [near if kept else anywhere] * 3
+        + [anywhere] * len(after),
+        out_specs=(anywhere,) * len(given) + (near,) * (len(outs) - len(given)),
         scratch_shapes=scratch,
         compiler_params=pltpu.CompilerParams(vmem_limit_bytes=EXPERT_VMEM),
         cost_estimate=pl.CostEstimate(flops=1000000, bytes_accessed=100000, transcendentals=0),
         name="expert_rows" if kept else "expert_rows_first",
-    )(first, second, *weights)
-
-
-def hold_kernel(*refs):
-    pass
-
-
-def hold(values, after):
+    )(*pieces, *weights, *after)
+    return results[: len(given)], results[len(given) :]
+
+
+def lay_kernel(count, *refs):
+    pieces, outs, sems = refs[:count], refs[-1 - count // 2 : -1], refs[-1]
+    copies = []
+    for index, piece in enumerate(pieces):
+        rows = piece.shape[0]
+        target = outs[index // 2].at[pl.ds(index % 2 * rows, rows)]
+        copies.append(pltpu.make_async_copy(piece, target, sems.at[index]))
+    for copy in copies:
+        copy.start()
+    for copy in copies:
+        copy.wait()
+
+
+def lay(pieces, after):
     anywhere = pl.BlockSpec(memory_space=pl.ANY)
+    rows, width = pieces[0].shape
+    shape = jax.ShapeDtypeStruct((2 * rows, width), pieces[0].dtype)
     return pl.pallas_call(
-        hold_kernel,
-        out_shape=tuple(jax.ShapeDtypeStruct(v.shape, v.dtype) for v in values),
-        in_specs=[anywhere] * (len(values) + len(after)),
-        out_specs=(anywhere,) * len(values),
-        input_output_aliases={i: i for i in range(len(values))},
+        functools.partial(lay_kernel, len(pieces)),
+        out_shape=(shape,) * (len(pieces) // 2),
+        in_specs=[anywhere] * (len(pieces) + len(after)),
+        out_specs=(anywhere,) * (len(pieces) // 2),
+        scratch_shapes=[pltpu.SemaphoreType.DMA((len(pieces),))],
         compiler_params=pltpu.CompilerParams(vmem_limit_bytes=1024 * 1024),
         cost_estimate=pl.CostEstimate(flops=1000, bytes_accessed=1000, transcendentals=0),
-        name="hold_rows",
-    )(*values, *after)
+        name="lay_rows",
+    )(*pieces, *after)
 
 
 def attend_kernel(
@@ -375,9 +375,6 @@
     normed = (rows * lax.rsqrt(mean_square + epsilon)[None, :, None] * gain).astype(jnp.bfloat16)
     normed = normed.transpose(1, 0, 2).reshape(slots, model_width)
 
-    pieces = [(gather_over(normed[:capacity], "z"), gather_over(normed[capacity:], "y"))]
-    (one, two), normed = lax.optimization_barrier((pieces[0], normed))
-
     logits = jnp.dot(normed, router, preferred_element_type=jnp.float32)
     own_logit = jnp.sum(jnp.where(own_mask, logits, 0.0), axis=1)
     other_logit = jnp.sum(jnp.where(own_mask, 0.0, logits * both), axis=1)
@@ -386,39 +383,43 @@
     def step(pair, turn):
         return ring(pair[0], "y", turn), ring(pair[1], "z", turn)
 
-    hidden = w_gate.shape[2]
-
-    def work(pair):
-        return expert_call(expert_kernel, *pair, kept, hidden, True)
+    def turn_over(pair, turn):
+        return swap(pair[0], "z", turn), swap(pair[1], "y", turn)
 
     def join(left, right):
         return add(left[0], right[0]), add(left[1], right[1])
 
-    piece = (one, two)
-    behind = step(piece, 0)
-    *own_part, kept_gate, kept_up, kept_down = expert_call(
-        first_expert_kernel, *piece, (w_gate, w_up, w_down), hidden, False
-    )
-    kept = (kept_gate, kept_up, kept_down)
-    behind, own_part = lax.optimization_barrier((behind, own_part))
-    far = step(behind, 0)
-    behind_part = work(behind)
-    ahead = step(hold(piece, far), 1)
-    far_part = work(far)
+    start = (normed[:capacity], normed[capacity:])
+    partner = turn_over(start, 0)
+    near = tuple(jnp.concatenate(both, axis=0) for both in zip(start, partner))
+    apart = turn_over(near, 1)
+    whole = (4 * capacity,) * 2
+
+    def pieces(one, two):
+        return one[0], two[0], one[1], two[1]
+
+    behind = step(near, 0), step(apart, 0)
+    far = step(behind[0], 0), step(behind[1], 0)
+    own_part, kept = expert_call(pieces(near, apart), whole, (w_gate, w_up, w_down), False)
+    ahead = step(lay(pieces(near, apart), far[0]), 1)
+    far_part, _ = expert_call(pieces(*far), whole, kept, True)
     far_sum = step(far_part, 1)
-    ahead, far_part = lax.optimization_barrier((ahead, far_part))
-    ahead_part = work(ahead)
+    behind_part, _ = expert_call(pieces(*behind), whole, kept, True, far_part)
+    ahead_part, _ = expert_call(ahead, whole, kept, True)
     from_behind = step(ahead_part, 0)
-    far_sum, ahead_part = lax.optimization_barrier((far_sum, ahead_part))
     from_ahead = step(join(far_sum, behind_part), 1)
 
-    def total(side):
+    def collect(side, axis):
         value = own_part[side].astype(jnp.float32) + from_behind[side].astype(jnp.float32)
-        return (value + from_ahead[side].astype(jnp.float32)).astype(jnp.bfloat16)
-
-    one, two = total(0), total(1)
-
-    expert_out = jnp.concatenate([reduce_over(one, "z"), reduce_over(two, "y")], axis=0)
+        value = value + from_ahead[side].astype(jnp.float32)
+        value = value.reshape(SIDE, capacity, model_width)
+        sent = value[1:].astype(jnp.bfloat16)
+        total = value[0] + swap(sent[0], axis, 0).astype(jnp.float32)
+        total = total + swap(sent[1], axis, 1).astype(jnp.float32)
+        return total + shift(sent[2], axis, 2).astype(jnp.float32)
+
+    expert_out = jnp.concatenate([collect(0, "z"), collect(1, "y")], axis=0)
+
     weighted = (expert_out * gates.astype(jnp.float32)[:, None]).astype(jnp.bfloat16)
     weighted = weighted.reshape(slots, experts, share).transpose(1, 0, 2)
     back = lax.all_to_all(weighted, EXPERT_AXES, 0, 0, tiled=True)

time: 163 us -> 151 us (0.926)
  waiting for transfers between devices: 64.8 us -> 45.2 us
  starting transfers between devices: 38.1 us -> 43.5 us
  Pallas kernels: 28.8 us -> 31.6 us
    ppermute x12 -> x16, waiting for transfers between devices: 29.9 us -> 17.1 us  [ring(): return lax.ppermute(value, (axis, 'c'), perm)]
    ppermute x8, waiting for transfers between devices: 22.7 us -> 15.8 us  [swap(): return lax.ppermute(value, (axis, 'c'), perm)]
    ppermute x12 -> x16, starting transfers between devices: 15.5 us -> 20.4 us  [ring(): return lax.ppermute(value, (axis, 'c'), perm)]
    pallas_call x5, Pallas kernels: 20 us -> 22.8 us  [the longest x4 22 us: expert_call(): pl.pallas_call(functools.partial(expert_kernel, taken, given, kept, len(a...]
    ppermute x3 -> x5, starting transfers between devices: 4.96 us -> 6.84 us  [shift(): lax.ppermute(value, axis, [(i, (i + step) % SIDE) for i in range(SIDE)])]
    ppermute x3 -> x5, waiting for transfers between devices: 3.51 us -> 3.56 us  [shift(): lax.ppermute(value, axis, [(i, (i + step) % SIDE) for i in range(SIDE)])]
  transfers between devices with their start and end apart: 25 -> 31, of which waited for: 18 -> 13; matrix products, arithmetic and copies ran while one was open for 2% -> 2% of each run, Pallas kernels for 12% -> 15%
where the time goes in v4:
time: 151 us; the launch traced here: 150 us
  waiting for transfers between devices  45.2 us (30%)
  starting transfers between devices  43.5 us (29%)
  Pallas kernels  31.6 us (21%)
  blocking collectives  22 us (15%)
  other arithmetic  4.7 us (3%)
  matrix products  2.24 us (1%)
    pallas_call x4, Pallas kernels, expert_call(): pl.pallas_call(functools.partial(expert_kernel, taken, given, kept, len(a...  22 us
    all_to_all x1, blocking collectives, body(): back = lax.all_to_all(weighted, EXPERT_AXES, 0, 0, tiled=True)  22 us
    ppermute x16, starting transfers between devices, ring(): return lax.ppermute(value, (axis, 'c'), perm)  20.4 us
    ppermute x16, waiting for transfers between devices, ring(): return lax.ppermute(value, (axis, 'c'), perm)  17.1 us
    ppermute x8, waiting for transfers between devices, swap(): return lax.ppermute(value, (axis, 'c'), perm)  15.8 us
    ppermute x8, starting transfers between devices, swap(): return lax.ppermute(value, (axis, 'c'), perm)  9.54 us
    pallas_call x1, Pallas kernels, attend(): pl.pallas_call(attend_kernel, grid=(count // BLOCK,), out_shape=(shape, s...  8.78 us
    all_to_all x1, waiting for transfers between devices, body(): lax.all_to_all(sent, EXPERT_AXES, 0, 0, tiled=True).astype(jnp.float32)  8.06 us
  transfers between devices with their start and end apart: 31, of which 13 were waited for; matrix products, arithmetic and copies ran while one was open for 2% of the time, Pallas kernels for 15%

profile of v4, /device:TPU:1, one launch (start us, length us, event | category | flops | bytes accessed | tf_op | source)
XLA Modules:
  0.0 150.4 jit_solution(8236380259179675890)
XLA Ops:
  0.0 0.6 pad_add_fusion.where
  0.6 8.8 %attend_rows.1 = (bf16[4,64,768]{2,1,0:T(8,128)(2,1)}, bf16[4,64,768]{2,1,0:T(8,128)(2,1)}) custom-call(s32[2]{0:T(128)} %pad_add_fusion.where, bf16[64,384]{1,0:T(8,128)(2,1)} %queries.1, bf16[64,128]{1,0:T(8,128)(2,1)} %new_keys.1, bf16[64,128]{1,0:T(8,128)(2,1)} %new_values.1, bf16[64,256,128]{2,1,0:T(8,128)(2,1)} %cache_k.1, ...), custom_call_target="tpu_custom_call" | custom-call | flops 301989888 | bytes 8388608 | tf_op jit(solution)/shard_map/attend_rows/pallas_call | solution.py:284
  9.4 1.5 collective-permute-start
  11.7 0.7 collective-permute-done
  12.4 1.1 fusion.21
  13.4 1.4 collective-permute-start.1
  14.8 1.4 collective-permute-start.3
  16.2 1.6 %collective-permute-start.2 = (bf16[64,768]{1,0:T(8,128)(2,1)S(1)}, bf16[64,768]{1,0:T(8,128)(2,1)S(1)}, u32[]{:S(2)}, u32[]{:S(2)}) collective-permute-start(bf16[64,768]{1,0:T(8,128)(2,1)S(1)} %get-tuple-element.53), channel_id=1, source_target_pairs={{0,4},{2,6},{4,0},{6,2},{1,5},{3,7},{5,1},{7,3},{8,12},{10,14},{12... | collective-permute-start | bytes 294920 | tf_op jit(solution)/shard_map/ppermute | solution.py:28
  17.8 0.9 collective-permute-done.1
  18.7 2.6 %collective-permute-done.2 = bf16[64,768]{1,0:T(8,128)(2,1)S(1)} collective-permute-done((bf16[64,768]{1,0:T(8,128)(2,1)S(1)}, bf16[64,768]{1,0:T(8,128)(2,1)S(1)}, u32[]{:S(2)}, u32[]{:S(2)}) %collective-permute-start.2) | collective-permute-done | bytes 98336 | tf_op jit(solution)/shard_map/ppermute | solution.py:28
  21.4 1.0 fusion.14
  22.4 1.0 convolution_convert_fusion
  23.4 5.2 %all-to-all-start = ((bf16[8,32,768]{2,1,0:T(8,128)(2,1)}), bf16[8,32,768]{2,1,0:T(8,128)(2,1)S(1)}, u32[]{:S(2)}, u32[]{:S(2)}) async-start(bf16[8,32,768]{2,1,0:T(8,128)(2,1)} %bitcast.8), calls=%async_computation | async-start | bytes 786432 | tf_op jit(solution)/shard_map/all_to_all | solution.py:372
  28.6 8.1 %all-to-all-done = bf16[8,32,768]{2,1,0:T(8,128)(2,1)S(1)} async-done(((bf16[8,32,768]{2,1,0:T(8,128)(2,1)}), bf16[8,32,768]{2,1,0:T(8,128)(2,1)S(1)}, u32[]{:S(2)}, u32[]{:S(2)}) %all-to-all-start) | async-done | bytes 393248 | tf_op jit(solution)/shard_map/all_to_all | solution.py:372
  37.2 3.9 %collective-permute-start.4 = (bf16[16,6144]{1,0:T(8,128)(2,1)S(1)}, bf16[16,6144]{1,0:T(8,128)(2,1)S(1)}, u32[]{:S(2)}, u32[]{:S(2)}) collective-permute-start(bf16[16,6144]{1,0:T(8,128)(2,1)S(1)} %bitcast.55), channel_id=1, source_target_pairs={{0,8},{1,25},{8,0},{9,17},{16,24},{17,9},{24,16},{25,1},{2,10},{3,... | collective-permute-start | bytes 589832 | tf_op jit(solution)/shard_map/ppermute | solution.py:46
  41.1 2.8 %collective-permute-start.6 = (bf16[16,6144]{1,0:T(8,128)(2,1)S(1)}, bf16[16,6144]{1,0:T(8,128)(2,1)S(1)}, u32[]{:S(2)}, u32[]{:S(2)}) collective-permute-start(bf16[16,6144]{1,0:T(8,128)(2,1)S(1)} %bitcast.57), channel_id=1, source_target_pairs={{0,32},{1,97},{32,0},{33,65},{64,96},{65,33},{96,64},{97,1},{2,34}... | collective-permute-start | bytes 589832 | tf_op jit(solution)/shard_map/ppermute | solution.py:46
  44.0 3.0 %collective-permute-done.6 = bf16[16,6144]{1,0:T(8,128)(2,1)S(1)} collective-permute-done((bf16[16,6144]{1,0:T(8,128)(2,1)S(1)}, bf16[16,6144]{1,0:T(8,128)(2,1)S(1)}, u32[]{:S(2)}, u32[]{:S(2)}) %collective-permute-start.6) | collective-permute-done | bytes 196640 | tf_op jit(solution)/shard_map/ppermute | solution.py:46
  47.2 0.4 collective-permute-start.10
  47.7 2.4 %collective-permute-start.8 = (bf16[32,6144]{1,0:T(8,128)(2,1)S(1)}, bf16[32,6144]{1,0:T(8,128)(2,1)S(1)}, u32[]{:S(2)}, u32[]{:S(2)}) collective-permute-start(bf16[32,6144]{1,0:T(8,128)(2,1)S(1)} %constant_dynamic-update-slice_fusion.refs_0_), channel_id=1, source_target_pairs={{0,32},{1,97},{32,64},{33,1},{64,96},{65,33},{96,0},{97,65},{2,34}... | collective-permute-start | bytes 1179656 | tf_op jit(solution)/shard_map/ppermute | solution.py:37
  50.1 4.0 %collective-permute-done.7.refs_3_ = bf16[32,6144]{1,0:T(8,128)(2,1)S(1)} collective-permute-done((bf16[32,6144]{1,0:T(8,128)(2,1)S(1)}, bf16[32,6144]{1,0:T(8,128)(2,1)S(1)}, u32[]{:S(2)}, u32[]{:S(2)}) %collective-permute-start.7) | collective-permute-done | bytes 393248 | tf_op jit(solution)/shard_map/ppermute | solution.py:46
  54.1 3.4 %collective-permute-start.15 = (bf16[32,6144]{1,0:T(8,128)(2,1)S(1)}, bf16[32,6144]{1,0:T(8,128)(2,1)S(1)}, u32[]{:S(2)}, u32[]{:S(2)}) collective-permute-start(bf16[32,6144]{1,0:T(8,128)(2,1)S(1)} %collective-permute-done.5.refs_1_), channel_id=1, source_target_pairs={{0,32},{1,97},{32,64},{33,1},{64,96},{65,33},{96,0},{97,65},{2,34}... | collective-permute-start | bytes 1179656 | tf_op jit(solution)/shard_map/ppermute | solution.py:37
  57.5 0.8 collective-permute-done.10.refs_2_
  58.4 3.1 %collective-permute-start.9 = (bf16[32,6144]{1,0:T(8,128)(2,1)S(1)}, bf16[32,6144]{1,0:T(8,128)(2,1)S(1)}, u32[]{:S(2)}, u32[]{:S(2)}) collective-permute-start(bf16[32,6144]{1,0:T(8,128)(2,1)S(1)} %collective-permute-done.8.refs_0_), channel_id=1, source_target_pairs={{0,32},{1,97},{32,64},{33,1},{64,96},{65,33},{96,0},{97,65},{2,34}... | collective-permute-start | bytes 1179656 | tf_op jit(solution)/shard_map/ppermute | solution.py:37
  61.5 1.0 collective-permute-done.17.refs_3_
  62.6 1.4 collective-permute-start.18
  63.9 2.4 %collective-permute-start.16 = (bf16[32,6144]{1,0:T(8,128)(2,1)S(1)}, bf16[32,6144]{1,0:T(8,128)(2,1)S(1)}, u32[]{:S(2)}, u32[]{:S(2)}) collective-permute-start(bf16[32,6144]{1,0:T(8,128)(2,1)S(1)} %collective-permute-done.15.refs_1_), channel_id=1, source_target_pairs={{0,32},{1,97},{32,64},{33,1},{64,96},{65,33},{96,0},{97,65},{2,34}... | collective-permute-start | bytes 1179656 | tf_op jit(solution)/shard_map/ppermute | solution.py:37
  66.3 8.2 %expert_rows_first.1 = (bf16[64,6144]{1,0:T(8,128)(2,1)S(1)}, bf16[64,6144]{1,0:T(8,128)(2,1)S(1)}, bf16[6144,512]{1,0:T(8,128)(2,1)S(1)}, bf16[6144,512]{1,0:T(8,128)(2,1)S(1)}, bf16[512,6144]{1,0:T(8,128)(2,1)S(1)}) custom-call(bf16[32,6144]{1,0:T(8,128)(2,1)S(1)} %constant_dynamic-update-slice_fusion.refs_0_, ...), custom_call_target="tpu_custom_call" | custom-call | flops 1000000 | bytes 100000 | tf_op jit(solution)/shard_map/expert_rows_first/pallas_call | solution.py:161
  74.6 0.8 lay_rows.1
  75.7 0.6 collective-permute-start.13
  76.3 4.8 %expert_rows.4 = (bf16[64,6144]{1,0:T(8,128)(2,1)S(1)}, bf16[64,6144]{1,0:T(8,128)(2,1)S(1)}) custom-call(bf16[32,6144]{1,0:T(8,128)(2,1)S(1)} %collective-permute-done.9.refs_4_.refs_0_, bf16[32,6144]{1,0:T(8,128)(2,1)S(1)} %collective-permute-done.16.refs_1_, bf16[32,6144]{1,0:T(8,128)(2,1)S(1)} %collective-permute-done.11.refs_5_.refs_2_, ...), custom_call_target="tpu_custom_call" | custom-call | flops 1000000 | bytes 100000 | tf_op jit(solution)/shard_map/expert_rows/pallas_call | solution.py:161
  81.1 0.7 collective-permute-start.19
  82.2 1.1 collective-permute-start.25
  83.3 4.8 %expert_rows.5 = (bf16[64,6144]{1,0:T(8,128)(2,1)S(1)}, bf16[64,6144]{1,0:T(8,128)(2,1)S(1)}) custom-call(bf16[32,6144]{1,0:T(8,128)(2,1)S(1)} %collective-permute-done.8.refs_0_, bf16[32,6144]{1,0:T(8,128)(2,1)S(1)} %collective-permute-done.15.refs_1_, bf16[32,6144]{1,0:T(8,128)(2,1)S(1)} %collective-permute-done.10.refs_2_, ...), custom_call_target="tpu_custom_call" | custom-call | flops 1000000 | bytes 100000 | tf_op jit(solution)/shard_map/expert_rows/pallas_call | solution.py:161
  88.1 4.2 %expert_rows.3 = (bf16[64,6144]{1,0:T(8,128)(2,1)S(1)}, bf16[64,6144]{1,0:T(8,128)(2,1)S(1)}) custom-call(bf16[64,6144]{1,0:T(8,128)(2,1)S(1)} %collective-permute-done.12.refs_0_, bf16[64,6144]{1,0:T(8,128)(2,1)S(1)} %collective-permute-done.13.refs_1_, bf16[6144,512]{1,0:T(8,128)(2,1)S(1)} %get-tuple-element.27.refs_2_.refs_4_, ...), custom_call_target="tpu_custom_call" | custom-call | flops 1000000 | bytes 100000 | tf_op jit(solution)/shard_map/expert_rows/pallas_call | solution.py:161
  92.3 2.7 %collective-permute-start.14 = (bf16[64,6144]{1,0:T(8,128)(2,1)S(1)}, bf16[64,6144]{1,0:T(8,128)(2,1)S(1)}, u32[]{:S(2)}, u32[]{:S(2)}) collective-permute-start(bf16[64,6144]{1,0:T(8,128)(2,1)S(1)} %get-tuple-element.30), channel_id=1, source_target_pairs={{0,32},{1,97},{32,64},{33,1},{64,96},{65,33},{96,0},{97,65},{2,34}... | collective-permute-start | bytes 2359304 | tf_op jit(solution)/shard_map/ppermute | solution.py:37
  95.0 1.1 collective-permute-start.24
  96.6 0.8 collective-permute-start.26
  97.4 11.7 %collective-permute-done.14 = bf16[64,6144]{1,0:T(8,128)(2,1)S(1)} collective-permute-done((bf16[64,6144]{1,0:T(8,128)(2,1)S(1)}, bf16[64,6144]{1,0:T(8,128)(2,1)S(1)}, u32[]{:S(2)}, u32[]{:S(2)}) %collective-permute-start.14) | collective-permute-done | bytes 786464 | tf_op jit(solution)/shard_map/ppermute | solution.py:37
  109.2 3.5 %collective-permute-done.20 = bf16[64,6144]{1,0:T(8,128)(2,1)S(1)} collective-permute-done((bf16[64,6144]{1,0:T(8,128)(2,1)S(1)}, bf16[64,6144]{1,0:T(8,128)(2,1)S(1)}, u32[]{:S(2)}, u32[]{:S(2)}) %collective-permute-start.20) | collective-permute-done | bytes 786464 | tf_op jit(solution)/shard_map/ppermute | solution.py:37
  112.6 0.3 fusion.43
  113.0 2.3 %collective-permute-start.21 = (bf16[16,6144]{1,0:T(8,128)(2,1)S(1)}, bf16[16,6144]{1,0:T(8,128)(2,1)S(1)}, u32[]{:S(2)}, u32[]{:S(2)}) collective-permute-start(bf16[16,6144]{1,0:T(8,128)(2,1)S(1)} %get-tuple-element.45), channel_id=1, source_target_pairs={{0,8},{1,25},{8,0},{9,17},{16,24},{17,9},{24,16},{25,1},{2,10},{3,... | collective-permute-start | bytes 589832 | tf_op jit(solution)/shard_map/ppermute | solution.py:46
  115.3 2.5 %collective-permute-start.23 = (bf16[16,6144]{1,0:T(8,128)(2,1)S(1)}, bf16[16,6144]{1,0:T(8,128)(2,1)S(1)}, u32[]{:S(2)}, u32[]{:S(2)}) collective-permute-start(bf16[16,6144]{1,0:T(8,128)(2,1)S(1)} %get-tuple-element.46), channel_id=1, source_target_pairs={{0,16},{8,24},{16,0},{24,8},{1,17},{9,25},{17,1},{25,9},{2,18},{10... | collective-permute-start | bytes 589832 | tf_op jit(solution)/shard_map/ppermute | solution.py:28
  117.8 0.3 fusion.44
  118.2 0.3 collective-permute-start.27
  118.4 3.6 %collective-permute-done.21 = bf16[16,6144]{1,0:T(8,128)(2,1)S(1)} collective-permute-done((bf16[16,6144]{1,0:T(8,128)(2,1)S(1)}, bf16[16,6144]{1,0:T(8,128)(2,1)S(1)}, u32[]{:S(2)}, u32[]{:S(2)}) %collective-permute-start.21) | collective-permute-done | bytes 196640 | tf_op jit(solution)/shard_map/ppermute | solution.py:46
  122.0 5.1 %collective-permute-done.22 = bf16[16,6144]{1,0:T(8,128)(2,1)S(1)} collective-permute-done((bf16[16,6144]{1,0:T(8,128)(2,1)S(1)}, bf16[16,6144]{1,0:T(8,128)(2,1)S(1)}, u32[]{:S(2)}, u32[]{:S(2)}) %collective-permute-start.22) | collective-permute-done | bytes 196640 | tf_op jit(solution)/shard_map/ppermute | solution.py:46
  127.6 22.0 %all_to_all.10 = bf16[8,32,768]{2,1,0:T(8,128)(2,1)S(1)} all-to-all(bf16[8,32,768]{2,1,0:T(8,128)(2,1)S(1)} %fusion.7), channel_id=1, replica_groups=mesh['y'=4,'z'=4,'x'=4,'c'=2] {'x','c'}, dimensions={0} | all-to-all | bytes 786432 | tf_op jit(solution)/shard_map/all_to_all | solution.py:425
  149.5 0.9 fusion
  (74 shorter events, 3.5 us)
Async XLA Ops:
  0.0 81.8 %copy-start = (bf16[6144,8]{0,1:T(8,128)(2,1)S(1)}, bf16[6144,8]{0,1:T(8,128)(2,1)}, u32[]{:S(2)}) copy-start(bf16[6144,8]{0,1:T(8,128)(2,1)} %param.23) | copy-start | bytes 294916
  0.6 10.3 %copy-start.3 = (s32[64,2]{0,1:T(2,128)S(1)}, s32[64,2]{0,1:T(2,128)}, u32[]{:S(2)}) copy-start(s32[64,2]{0,1:T(2,128)} %param.24) | copy-start | bytes 1540
  9.4 3.0 %collective-permute-start = (bf16[4,64,768]{2,1,0:T(8,128)(2,1)}, bf16[4,64,768]{2,1,0:T(8,128)(2,1)S(1)}, u32[]{:S(2)}, u32[]{:S(2)}) collective-permute-start(bf16[4,64,768]{2,1,0:T(8,128)(2,1)} %get-tuple-element.22), channel_id=1, source_target_pairs={{0,1},{1,0},{2,3},{3,2},{4,5},{5,4},{6,7},{7,6},{8,9},{9,8},{10,11... | collective-permute-start | bytes 1179656 | tf_op jit(solution)/shard_map/ppermute | solution.py:351
  11.5 17.1 %copy-start.2 = (bf16[6144]{0:T(1024)(128)(2,1)S(1)}, bf16[6144]{0:T(1024)(128)(2,1)}, u32[]{:S(2)}) copy-start(bf16[6144]{0:T(1024)(128)(2,1)} %param.22) | copy-start | bytes 36868
  13.4 5.3 %collective-permute-start.1 = (bf16[64,768]{1,0:T(8,128)(2,1)S(1)}, bf16[64,768]{1,0:T(8,128)(2,1)S(1)}, u32[]{:S(2)}, u32[]{:S(2)}) collective-permute-start(bf16[64,768]{1,0:T(8,128)(2,1)S(1)} %get-tuple-element.51), channel_id=1, source_target_pairs={{0,2},{2,4},{4,6},{6,0},{1,3},{3,5},{5,7},{7,1},{8,10},{10,12},{12... | collective-permute-start | bytes 294920 | tf_op jit(solution)/shard_map/ppermute | solution.py:28
  14.8 3.9 %collective-permute-start.3 = (bf16[64,768]{1,0:T(8,128)(2,1)S(1)}, bf16[64,768]{1,0:T(8,128)(2,1)S(1)}, u32[]{:S(2)}, u32[]{:S(2)}) collective-permute-start(bf16[64,768]{1,0:T(8,128)(2,1)S(1)} %get-tuple-element.52), channel_id=1, source_target_pairs={{0,6},{2,0},{4,2},{6,4},{1,7},{3,1},{5,3},{7,5},{8,14},{10,8},{12,... | collective-permute-start | bytes 294920 | tf_op jit(solution)/shard_map/ppermute | solution.py:28
  16.2 5.2 %collective-permute-start.2 = (bf16[64,768]{1,0:T(8,128)(2,1)S(1)}, bf16[64,768]{1,0:T(8,128)(2,1)S(1)}, u32[]{:S(2)}, u32[]{:S(2)}) collective-permute-start(bf16[64,768]{1,0:T(8,128)(2,1)S(1)} %get-tuple-element.53), channel_id=1, source_target_pairs={{0,4},{2,6},{4,0},{6,2},{1,5},{3,7},{5,1},{7,3},{8,12},{10,14},{12... | collective-permute-start | bytes 294920 | tf_op jit(solution)/shard_map/ppermute | solution.py:28
  23.4 13.3 %all-to-all-start = ((bf16[8,32,768]{2,1,0:T(8,128)(2,1)}), bf16[8,32,768]{2,1,0:T(8,128)(2,1)S(1)}, u32[]{:S(2)}, u32[]{:S(2)}) async-start(bf16[8,32,768]{2,1,0:T(8,128)(2,1)} %bitcast.8), calls=%async_computation | async-start | bytes 786432 | tf_op jit(solution)/shard_map/all_to_all | solution.py:372
  37.2 10.0 %collective-permute-start.4 = (bf16[16,6144]{1,0:T(8,128)(2,1)S(1)}, bf16[16,6144]{1,0:T(8,128)(2,1)S(1)}, u32[]{:S(2)}, u32[]{:S(2)}) collective-permute-start(bf16[16,6144]{1,0:T(8,128)(2,1)S(1)} %bitcast.55), channel_id=1, source_target_pairs={{0,8},{1,25},{8,0},{9,17},{16,24},{17,9},{24,16},{25,1},{2,10},{3,... | collective-permute-start | bytes 589832 | tf_op jit(solution)/shard_map/ppermute | solution.py:46
  41.1 5.9 %collective-permute-start.6 = (bf16[16,6144]{1,0:T(8,128)(2,1)S(1)}, bf16[16,6144]{1,0:T(8,128)(2,1)S(1)}, u32[]{:S(2)}, u32[]{:S(2)}) collective-permute-start(bf16[16,6144]{1,0:T(8,128)(2,1)S(1)} %bitcast.57), channel_id=1, source_target_pairs={{0,32},{1,97},{32,0},{33,65},{64,96},{65,33},{96,64},{97,1},{2,34}... | collective-permute-start | bytes 589832 | tf_op jit(solution)/shard_map/ppermute | solution.py:46
  47.0 7.0 %collective-permute-start.7 = (bf16[32,6144]{1,0:T(8,128)(2,1)S(1)}, bf16[32,6144]{1,0:T(8,128)(2,1)S(1)}, u32[]{:S(2)}, u32[]{:S(2)}) collective-permute-start(bf16[32,6144]{1,0:T(8,128)(2,1)S(1)} %constant_dynamic-update-slice_fusion.2.refs_2_), channel_id=1, source_target_pairs={{0,96},{1,33},{32,64},{33,1},{64,32},{65,97},{96,0},{97,65},{2,98}... | collective-permute-start | bytes 1179656 | tf_op jit(solution)/shard_map/ppermute | solution.py:46
  47.1 7.0 %collective-permute-start.5 = (bf16[32,6144]{1,0:T(8,128)(2,1)S(1)}, bf16[32,6144]{1,0:T(8,128)(2,1)S(1)}, u32[]{:S(2)}, u32[]{:S(2)}) collective-permute-start(bf16[32,6144]{1,0:T(8,128)(2,1)S(1)} %constant_dynamic-update-slice_fusion.refs_0_), channel_id=1, source_target_pairs={{0,24},{1,9},{8,16},{9,1},{16,8},{17,25},{24,0},{25,17},{2,26},{3,... | collective-permute-start | bytes 1179656 | tf_op jit(solution)/shard_map/ppermute | solution.py:46
  47.2 11.1 %collective-permute-start.10 = (bf16[32,6144]{1,0:T(8,128)(2,1)S(1)}, bf16[32,6144]{1,0:T(8,128)(2,1)S(1)}, u32[]{:S(2)}, u32[]{:S(2)}) collective-permute-start(bf16[32,6144]{1,0:T(8,128)(2,1)S(1)} %constant_dynamic-update-slice_fusion.2.refs_2_), channel_id=1, source_target_pairs={{0,8},{1,25},{8,16},{9,1},{16,24},{17,9},{24,0},{25,17},{2,10},{3,... | collective-permute-start | bytes 1179656 | tf_op jit(solution)/shard_map/ppermute | solution.py:37
  47.7 10.7 %collective-permute-start.8 = (bf16[32,6144]{1,0:T(8,128)(2,1)S(1)}, bf16[32,6144]{1,0:T(8,128)(2,1)S(1)}, u32[]{:S(2)}, u32[]{:S(2)}) collective-permute-start(bf16[32,6144]{1,0:T(8,128)(2,1)S(1)} %constant_dynamic-update-slice_fusion.refs_0_), channel_id=1, source_target_pairs={{0,32},{1,97},{32,64},{33,1},{64,96},{65,33},{96,0},{97,65},{2,34}... | collective-permute-start | bytes 1179656 | tf_op jit(solution)/shard_map/ppermute | solution.py:37
  54.0 8.6 %collective-permute-start.17 = (bf16[32,6144]{1,0:T(8,128)(2,1)S(1)}, bf16[32,6144]{1,0:T(8,128)(2,1)S(1)}, u32[]{:S(2)}, u32[]{:S(2)}) collective-permute-start(bf16[32,6144]{1,0:T(8,128)(2,1)S(1)} %collective-permute-done.7.refs_3_), channel_id=1, source_target_pairs={{0,8},{1,25},{8,16},{9,1},{16,24},{17,9},{24,0},{25,17},{2,10},{3,... | collective-permute-start | bytes 1179656 | tf_op jit(solution)/shard_map/ppermute | solution.py:37
  54.1 9.8 %collective-permute-start.15 = (bf16[32,6144]{1,0:T(8,128)(2,1)S(1)}, bf16[32,6144]{1,0:T(8,128)(2,1)S(1)}, u32[]{:S(2)}, u32[]{:S(2)}) collective-permute-start(bf16[32,6144]{1,0:T(8,128)(2,1)S(1)} %collective-permute-done.5.refs_1_), channel_id=1, source_target_pairs={{0,32},{1,97},{32,64},{33,1},{64,96},{65,33},{96,0},{97,65},{2,34}... | collective-permute-start | bytes 1179656 | tf_op jit(solution)/shard_map/ppermute | solution.py:37
  58.4 16.2 %collective-permute-start.11 = (bf16[32,6144]{1,0:T(8,128)(2,1)S(1)}, bf16[32,6144]{1,0:T(8,128)(2,1)S(1)}, u32[]{:S(2)}, u32[]{:S(2)}) collective-permute-start(bf16[32,6144]{1,0:T(8,128)(2,1)S(1)} %collective-permute-done.10.refs_2_), channel_id=1, source_target_pairs={{0,8},{1,25},{8,16},{9,1},{16,24},{17,9},{24,0},{25,17},{2,10},{3,... | collective-permute-start | bytes 1179656 | tf_op jit(solution)/shard_map/ppermute | solution.py:37
  58.4 16.2 %collective-permute-start.9 = (bf16[32,6144]{1,0:T(8,128)(2,1)S(1)}, bf16[32,6144]{1,0:T(8,128)(2,1)S(1)}, u32[]{:S(2)}, u32[]{:S(2)}) collective-permute-start(bf16[32,6144]{1,0:T(8,128)(2,1)S(1)} %collective-permute-done.8.refs_0_), channel_id=1, source_target_pairs={{0,32},{1,97},{32,64},{33,1},{64,96},{65,33},{96,0},{97,65},{2,34}... | collective-permute-start | bytes 1179656 | tf_op jit(solution)/shard_map/ppermute | solution.py:37
  62.6 13.7 %collective-permute-start.18 = (bf16[32,6144]{1,0:T(8,128)(2,1)S(1)}, bf16[32,6144]{1,0:T(8,128)(2,1)S(1)}, u32[]{:S(2)}, u32[]{:S(2)}) collective-permute-start(bf16[32,6144]{1,0:T(8,128)(2,1)S(1)} %collective-permute-done.17.refs_3_), channel_id=1, source_target_pairs={{0,8},{1,25},{8,16},{9,1},{16,24},{17,9},{24,0},{25,17},{2,10},{3,... | collective-permute-start | bytes 1179656 | tf_op jit(solution)/shard_map/ppermute | solution.py:37
  63.9 12.3 %collective-permute-start.16 = (bf16[32,6144]{1,0:T(8,128)(2,1)S(1)}, bf16[32,6144]{1,0:T(8,128)(2,1)S(1)}, u32[]{:S(2)}, u32[]{:S(2)}) collective-permute-start(bf16[32,6144]{1,0:T(8,128)(2,1)S(1)} %collective-permute-done.15.refs_1_), channel_id=1, source_target_pairs={{0,32},{1,97},{32,64},{33,1},{64,96},{65,33},{96,0},{97,65},{2,34}... | collective-permute-start | bytes 1179656 | tf_op jit(solution)/shard_map/ppermute | solution.py:37
  75.4 12.7 %collective-permute-start.12 = (bf16[64,6144]{1,0:T(8,128)(2,1)S(1)}, bf16[64,6144]{1,0:T(8,128)(2,1)S(1)}, u32[]{:S(2)}, u32[]{:S(2)}) collective-permute-start(bf16[64,6144]{1,0:T(8,128)(2,1)S(1)} %get-tuple-element.25), channel_id=1, source_target_pairs={{0,96},{1,33},{32,0},{33,65},{64,32},{65,97},{96,64},{97,1},{2,98}... | collective-permute-start | bytes 2359304 | tf_op jit(solution)/shard_map/ppermute | solution.py:37
  75.7 12.4 %collective-permute-start.13 = (bf16[64,6144]{1,0:T(8,128)(2,1)S(1)}, bf16[64,6144]{1,0:T(8,128)(2,1)S(1)}, u32[]{:S(2)}, u32[]{:S(2)}) collective-permute-start(bf16[64,6144]{1,0:T(8,128)(2,1)S(1)} %get-tuple-element.26), channel_id=1, source_target_pairs={{0,24},{1,9},{8,0},{9,17},{16,8},{17,25},{24,16},{25,1},{2,26},{3,... | collective-permute-start | bytes 2359304 | tf_op jit(solution)/shard_map/ppermute | solution.py:37
  81.1 15.0 %collective-permute-start.19 = (bf16[64,6144]{1,0:T(8,128)(2,1)S(1)}, bf16[64,6144]{1,0:T(8,128)(2,1)S(1)}, u32[]{:S(2)}, u32[]{:S(2)}) collective-permute-start(bf16[64,6144]{1,0:T(8,128)(2,1)S(1)} %get-tuple-element.31.refs_7_), channel_id=1, source_target_pairs={{0,96},{1,33},{32,0},{33,65},{64,32},{65,97},{96,64},{97,1},{2,98}... | collective-permute-start | bytes 2359304 | tf_op jit(solution)/shard_map/ppermute | solution.py:37
  82.2 14.2 %collective-permute-start.25 = (bf16[64,6144]{1,0:T(8,128)(2,1)S(1)}, bf16[64,6144]{1,0:T(8,128)(2,1)S(1)}, u32[]{:S(2)}, u32[]{:S(2)}) collective-permute-start(bf16[64,6144]{1,0:T(8,128)(2,1)S(1)} %get-tuple-element.32.refs_8_), channel_id=1, source_target_pairs={{0,24},{1,9},{8,0},{9,17},{16,8},{17,25},{24,16},{25,1},{2,26},{3,... | collective-permute-start | bytes 2359304 | tf_op jit(solution)/shard_map/ppermute | solution.py:37
  92.3 16.9 %collective-permute-start.14 = (bf16[64,6144]{1,0:T(8,128)(2,1)S(1)}, bf16[64,6144]{1,0:T(8,128)(2,1)S(1)}, u32[]{:S(2)}, u32[]{:S(2)}) collective-permute-start(bf16[64,6144]{1,0:T(8,128)(2,1)S(1)} %get-tuple-element.30), channel_id=1, source_target_pairs={{0,32},{1,97},{32,64},{33,1},{64,96},{65,33},{96,0},{97,65},{2,34}... | collective-permute-start | bytes 2359304 | tf_op jit(solution)/shard_map/ppermute | solution.py:37
  95.0 22.8 %collective-permute-start.24 = (bf16[64,6144]{1,0:T(8,128)(2,1)S(1)}, bf16[64,6144]{1,0:T(8,128)(2,1)S(1)}, u32[]{:S(2)}, u32[]{:S(2)}) collective-permute-start(bf16[64,6144]{1,0:T(8,128)(2,1)S(1)} %get-tuple-element.35), channel_id=1, source_target_pairs={{0,8},{1,25},{8,16},{9,1},{16,24},{17,9},{24,0},{25,17},{2,10},{3,... | collective-permute-start | bytes 2359304 | tf_op jit(solution)/shard_map/ppermute | solution.py:37
  96.3 16.3 %collective-permute-start.20 = (bf16[64,6144]{1,0:T(8,128)(2,1)S(1)}, bf16[64,6144]{1,0:T(8,128)(2,1)S(1)}, u32[]{:S(2)}, u32[]{:S(2)}) collective-permute-start(bf16[64,6144]{1,0:T(8,128)(2,1)S(1)} %add_convert_fusion.1), channel_id=1, source_target_pairs={{0,96},{1,33},{32,0},{33,65},{64,32},{65,97},{96,64},{97,1},{2,98}... | collective-permute-start | bytes 2359304 | tf_op jit(solution)/shard_map/ppermute | solution.py:37
  96.6 21.2 %collective-permute-start.26 = (bf16[64,6144]{1,0:T(8,128)(2,1)S(1)}, bf16[64,6144]{1,0:T(8,128)(2,1)S(1)}, u32[]{:S(2)}, u32[]{:S(2)}) collective-permute-start(bf16[64,6144]{1,0:T(8,128)(2,1)S(1)} %add_convert_fusion), channel_id=1, source_target_pairs={{0,24},{1,9},{8,0},{9,17},{16,8},{17,25},{24,16},{25,1},{2,26},{3,... | collective-permute-start | bytes 2359304 | tf_op jit(solution)/shard_map/ppermute | solution.py:37
  113.0 9.1 %collective-permute-start.21 = (bf16[16,6144]{1,0:T(8,128)(2,1)S(1)}, bf16[16,6144]{1,0:T(8,128)(2,1)S(1)}, u32[]{:S(2)}, u32[]{:S(2)}) collective-permute-start(bf16[16,6144]{1,0:T(8,128)(2,1)S(1)} %get-tuple-element.45), channel_id=1, source_target_pairs={{0,8},{1,25},{8,0},{9,17},{16,24},{17,9},{24,16},{25,1},{2,10},{3,... | collective-permute-start | bytes 589832 | tf_op jit(solution)/shard_map/ppermute | solution.py:46
  115.3 6.7 %collective-permute-start.23 = (bf16[16,6144]{1,0:T(8,128)(2,1)S(1)}, bf16[16,6144]{1,0:T(8,128)(2,1)S(1)}, u32[]{:S(2)}, u32[]{:S(2)}) collective-permute-start(bf16[16,6144]{1,0:T(8,128)(2,1)S(1)} %get-tuple-element.46), channel_id=1, source_target_pairs={{0,16},{8,24},{16,0},{24,8},{1,17},{9,25},{17,1},{25,9},{2,18},{10... | collective-permute-start | bytes 589832 | tf_op jit(solution)/shard_map/ppermute | solution.py:28
  117.8 9.3 %collective-permute-start.22 = (bf16[16,6144]{1,0:T(8,128)(2,1)S(1)}, bf16[16,6144]{1,0:T(8,128)(2,1)S(1)}, u32[]{:S(2)}, u32[]{:S(2)}) collective-permute-start(bf16[16,6144]{1,0:T(8,128)(2,1)S(1)} %get-tuple-element.47), channel_id=1, source_target_pairs={{0,24},{1,9},{8,16},{9,1},{16,8},{17,25},{24,0},{25,17},{2,26},{3,... | collective-permute-start | bytes 589832 | tf_op jit(solution)/shard_map/ppermute | solution.py:46
  118.2 9.1 %collective-permute-start.27 = (bf16[16,6144]{1,0:T(8,128)(2,1)S(1)}, bf16[16,6144]{1,0:T(8,128)(2,1)S(1)}, u32[]{:S(2)}, u32[]{:S(2)}) collective-permute-start(bf16[16,6144]{1,0:T(8,128)(2,1)S(1)} %get-tuple-element.48), channel_id=1, source_target_pairs={{0,32},{1,97},{32,0},{33,65},{64,96},{65,33},{96,64},{97,1},{2,34}... | collective-permute-start | bytes 589832 | tf_op jit(solution)/shard_map/ppermute | solution.py:46
  118.4 8.8 %collective-permute-start.29 = (bf16[16,6144]{1,0:T(8,128)(2,1)S(1)}, bf16[16,6144]{1,0:T(8,128)(2,1)S(1)}, u32[]{:S(2)}, u32[]{:S(2)}) collective-permute-start(bf16[16,6144]{1,0:T(8,128)(2,1)S(1)} %get-tuple-element.49), channel_id=1, source_target_pairs={{0,64},{32,96},{64,0},{96,32},{1,65},{33,97},{65,1},{97,33},{2,66}... | collective-permute-start | bytes 589832 | tf_op jit(solution)/shard_map/ppermute | solution.py:28
  122.0 5.2 %collective-permute-start.28 = (bf16[16,6144]{1,0:T(8,128)(2,1)S(1)}, bf16[16,6144]{1,0:T(8,128)(2,1)S(1)}, u32[]{:S(2)}, u32[]{:S(2)}) collective-permute-start(bf16[16,6144]{1,0:T(8,128)(2,1)S(1)} %get-tuple-element.50), channel_id=1, source_target_pairs={{0,96},{1,33},{32,64},{33,1},{64,32},{65,97},{96,0},{97,65},{2,98}... | collective-permute-start | bytes 589832 | tf_op jit(solution)/shard_map/ppermute | solution.py:46
  127.3 23.1 %copy-start.1 = (bf16[6144,8]{0,1:T(8,128)(2,1)S(1)}, bf16[6144,8]{0,1:T(8,128)(2,1)}, u32[]{:S(2)}) copy-start(bf16[6144,8]{0,1:T(8,128)(2,1)} %param.23) | copy-start | bytes 294916

commit v5 on v4

--- a/solution.py
+++ b/solution.py
@@ -17,7 +17,8 @@
 EXPERT_AXES = ("x", "c")
 DEEP = 8
 WIDE = 6
-BLOCK = 32
+BLOCK = 8
+PARTS = 8
 EXPERT_VMEM = 8 * 1024 * 1024
 VMEM = 60 * 1024 * 1024
 
@@ -203,103 +204,138 @@
 
 
 def attend_kernel(
-    where, queries, new_keys, new_values, cache_k, cache_v, lengths, out_proj, mine, theirs, heads, weights, sem
+    lengths, queries, new_keys, new_values, cache_k, cache_v, out_proj, mine, theirs, near_lengths, near_queries, near_keys, near_values, keys, values, heads, weights, sums, sems, out_sems
 ):
-    step = pl.program_id(0)
-    block = queries.shape[0]
-    length = cache_k.shape[1]
-    group = queries.shape[1] // HD
-    half = 8
-    copy = pltpu.make_async_copy(out_proj, weights, sem)
-
-    @pl.when(step == 0)
-    def _():
-        copy.start()
+    count, length, _ = cache_k.shape
+    share = mine.shape[2]
+    width = queries.shape[1]
+    group = width // HD
+    blocks = count // BLOCK
+    copies = []
+    small = []
+    for index, (source, target) in enumerate(
+        (
+            (lengths, near_lengths),
+            (queries, near_queries),
+            (new_keys, near_keys),
+            (new_values, near_values),
+        )
+    ):
+        small.append(pltpu.make_async_copy(source, target, sems.at[2 * blocks + PARTS + index]))
+        small[-1].start()
+    for g in range(blocks):
+        part = pl.ds(g * BLOCK, BLOCK)
+        copies.append(
+            (
+                pltpu.make_async_copy(cache_k.at[part], keys.at[part], sems.at[2 * g]),
+                pltpu.make_async_copy(cache_v.at[part], values.at[part], sems.at[2 * g + 1]),
+            )
+        )
+    rows = width // PARTS
+    last = []
+    for k in range(PARTS):
+        part = pl.ds(k * rows, rows)
+        last.append(
+            pltpu.make_async_copy(out_proj.at[part], weights.at[part], sems.at[2 * blocks + k])
+        )
+    copies.append(tuple(last))
+    for pair in copies:
+        for copy in pair:
+            copy.start()
 
     factor = 1.0 / math.sqrt(HD)
-    column = lax.broadcasted_iota(jnp.int32, (group * half, half * length), 1)
-    line = lax.broadcasted_iota(jnp.int32, (group * half, half * length), 0)
-    same_row = column // length == line % half
-    position = column % length
-    turn = lax.broadcasted_iota(jnp.int32, (group * half, 1), 0) % half
-    all_queries = queries[...].astype(jnp.float32)
-    all_keys = new_keys[...].astype(jnp.float32)
-    all_values = new_values[...].astype(jnp.float32)
+    lines = 8
+    position = lax.broadcasted_iota(jnp.int32, (BLOCK, lines, length), 2)
+    turn = lax.broadcasted_iota(jnp.int32, (BLOCK, lines, 1), 0)
+    for copy in small:
+        copy.wait()
+    all_queries = near_queries[...].astype(jnp.float32)
+    all_keys = near_keys[...].astype(jnp.float32)
+    all_values = near_values[...].astype(jnp.float32)
     outs = []
-    for part in range(block // half):
-        rows = slice(part * half, (part + 1) * half)
-        query = jnp.concatenate(
-            [all_queries[rows, h * HD : (h + 1) * HD] for h in range(group)], axis=0
-        )
-        fresh_key = jnp.concatenate([all_keys[rows]] * group, axis=0)
-        fresh_value = jnp.concatenate([all_values[rows]] * group, axis=0)
-        used = jnp.zeros((group * half, 1), jnp.int32)
-        for r in range(half):
-            used = jnp.where(turn == r, lengths[step * block + part * half + r], used)
-        keys = cache_k[rows].reshape(half * length, HD)
-        values = cache_v[rows].reshape(half * length, HD)
+    for g in range(blocks):
+        rows = slice(g * BLOCK, (g + 1) * BLOCK)
+        heads_in = [all_queries[rows, h * HD : (h + 1) * HD][:, None, :] for h in range(group)]
+        empty = jnp.zeros((BLOCK, lines - group, HD), jnp.float32)
+        query = jnp.concatenate(heads_in + [empty], axis=1)
+        fresh_key = all_keys[rows][:, None, :]
+        fresh_value = all_values[rows][:, None, :]
+        used = jnp.zeros((BLOCK, lines, 1), jnp.int32)
+        for r in range(BLOCK):
+            used = jnp.where(turn == r, near_lengths[g * BLOCK + r], used)
+        itself = jnp.sum(query * fresh_key, axis=2, keepdims=True) * factor
+        for copy in copies[g]:
+            copy.wait()
         scores = (
-            lax.dot_general(
+            jnp.einsum(
+                "rhd,rld->rhl",
                 query.astype(jnp.bfloat16),
-                keys,
-                (((1,), (1,)), ((), ())),
+                keys[rows],
                 preferred_element_type=jnp.float32,
             )
             * factor
         )
-        itself = jnp.sum(query * fresh_key, axis=1, keepdims=True) * factor
-        masked = jnp.where(same_row & (position < used), scores, -jnp.inf)
-        highest = jnp.maximum(jnp.max(masked, axis=1, keepdims=True), itself)
+        masked = jnp.where(position < used, scores, -jnp.inf)
+        highest = jnp.maximum(jnp.max(masked, axis=2, keepdims=True), itself)
         spread = jnp.exp(masked - highest)
         own_exp = jnp.exp(itself - highest)
-        inverse = 1.0 / (jnp.sum(spread, axis=1, keepdims=True) + own_exp)
+        inverse = 1.0 / (jnp.sum(spread, axis=2, keepdims=True) + own_exp)
         probs = (spread * inverse).astype(jnp.bfloat16)
         own_prob = (own_exp * inverse).astype(jnp.bfloat16).astype(jnp.float32)
-        mixed = jnp.dot(probs, values, preferred_element_type=jnp.float32) + own_prob * fresh_value
-        outs.append(
-            jnp.concatenate([mixed[h * half : (h + 1) * half] for h in range(group)], axis=1)
-        )
-    heads[pl.ds(step * block, block), :] = jnp.concatenate(outs, axis=0).astype(jnp.bfloat16)
-
-    @pl.when(step == pl.num_programs(0) - 1)
-    def _():
+        mixed = jnp.einsum(
+            "rhl,rld->rhd", probs, values[rows], preferred_element_type=jnp.float32
+        )
+        mixed = mixed + own_prob * fresh_value
+        outs.append(jnp.concatenate([mixed[:, h, :] for h in range(group)], axis=1))
+        if g % 2 == 1:
+            heads[pl.ds((g - 1) * BLOCK, 2 * BLOCK), :] = jnp.concatenate(
+                outs[-2:], axis=0
+            ).astype(jnp.bfloat16)
+
+    for copy in copies[-1]:
         copy.wait()
-        share = mine.shape[2]
-        left = heads[...]
+    left = heads[...]
+    chip_here, core_here = lax.axis_index("x"), lax.axis_index("c")
+    writes = []
+    for side, (core, target) in enumerate(((1 - core_here, theirs), (core_here, mine))):
         for k in range(SIDE):
-            chip = lax.rem(where[0] + k, SIDE)
-            for core, target in ((where[1], mine), (1 - where[1], theirs)):
-                part = pl.ds(pl.multiple_of((chip * 2 + core) * share, share), share)
-                target[k] = jnp.dot(
-                    left, weights[:, part], preferred_element_type=jnp.float32
-                ).astype(jnp.bfloat16)
-
-
-def attend(where, queries, new_keys, new_values, cache_k, cache_v, lengths, out_proj):
+            chip = lax.rem(chip_here + k, SIDE)
+            part = pl.ds(pl.multiple_of((chip * 2 + core) * share, share), share)
+            place = side * SIDE + k
+            sums[place] = jnp.dot(
+                left, weights[:, part], preferred_element_type=jnp.float32
+            ).astype(jnp.bfloat16)
+            writes.append(
+                pltpu.make_async_copy(sums.at[place], target.at[k], out_sems.at[place])
+            )
+            writes[-1].start()
+    for write in writes:
+        write.wait()
+
+
+def attend(queries, new_keys, new_values, cache_k, cache_v, lengths, out_proj):
     count, width = queries.shape
     length = cache_k.shape[1]
     share = out_proj.shape[1] // (2 * SIDE)
     shape = jax.ShapeDtypeStruct((SIDE, count, share), jnp.bfloat16)
-    whole = pl.BlockSpec((SIDE, count, share), lambda i: (0, 0, 0))
+    anywhere = pl.BlockSpec(memory_space=pl.ANY)
     return pl.pallas_call(
         attend_kernel,
-        grid=(count // BLOCK,),
         out_shape=(shape, shape),
-        in_specs=[
-            pl.BlockSpec(memory_space=pltpu.SMEM),
-            pl.BlockSpec((BLOCK, width), lambda i: (i, 0)),
-            pl.BlockSpec((BLOCK, HD), lambda i: (i, 0)),
-            pl.BlockSpec((BLOCK, HD), lambda i: (i, 0)),
-            pl.BlockSpec((BLOCK, length, HD), lambda i: (i, 0, 0)),
-            pl.BlockSpec((BLOCK, length, HD), lambda i: (i, 0, 0)),
-            pl.BlockSpec(memory_space=pltpu.SMEM),
-            pl.BlockSpec(memory_space=pl.ANY),
-        ],
-        out_specs=(whole, whole),
+        in_specs=[anywhere] * 7,
+        out_specs=(anywhere, anywhere),
         scratch_shapes=[
+            pltpu.SMEM(lengths.shape, jnp.int32),
+            pltpu.VMEM(queries.shape, jnp.bfloat16),
+            pltpu.VMEM(new_keys.shape, jnp.bfloat16),
+            pltpu.VMEM(new_values.shape, jnp.bfloat16),
+            pltpu.VMEM(cache_k.shape, jnp.bfloat16),
+            pltpu.VMEM(cache_v.shape, jnp.bfloat16),
             pltpu.VMEM((count, width), jnp.bfloat16),
             pltpu.VMEM(out_proj.shape, jnp.bfloat16),
-            pltpu.SemaphoreType.DMA(()),
+            pltpu.VMEM((2 * SIDE, count, share), jnp.bfloat16),
+            pltpu.SemaphoreType.DMA((2 * count // BLOCK + PARTS + 4,)),
+            pltpu.SemaphoreType.DMA((2 * SIDE,)),
         ],
         compiler_params=pltpu.CompilerParams(vmem_limit_bytes=VMEM),
         cost_estimate=pl.CostEstimate(
@@ -308,7 +344,7 @@
             transcendentals=0,
         ),
         name="attend_rows",
-    )(where, queries, new_keys, new_values, cache_k, cache_v, lengths, out_proj)
+    )(lengths, queries, new_keys, new_values, cache_k, cache_v, out_proj)
 
 
 def slot_codes(route_ids, experts, capacity):
@@ -343,11 +379,8 @@
     slots = MICRO * capacity
     share = model_width // experts
     mine = lax.axis_index(EXPERT_AXES)
-    where = jnp.stack([lax.axis_index("x"), lax.axis_index("c")]).astype(jnp.int32)
-
-    own, others = attend(
-        where, queries, new_keys, new_values, cache_k, cache_v, lengths, out_proj
-    )
+
+    own, others = attend(queries, new_keys, new_values, cache_k, cache_v, lengths, out_proj)
     arrived = lax.ppermute(others, "c", [(0, 1), (1, 0)])
     sums = [add(own[k], arrived[k]) for k in range(SIDE)]
     sums = [sums[0]] + [shift(sums[k], "x", k) for k in range(1, SIDE)]

time: 151 us -> 149 us (0.987)
  no operation moved by 1% of the time
where the time goes in v5:
time: 149 us; the launch traced here: 148 us
  waiting for transfers between devices  45.1 us (30%)
  starting transfers between devices  43.3 us (29%)
  Pallas kernels  30.5 us (20%)
  blocking collectives  22 us (15%)
  other arithmetic  4.14 us (3%)
  matrix products  2.24 us (2%)
    pallas_call x4, Pallas kernels, expert_call(): pl.pallas_call(functools.partial(expert_kernel, taken, given, kept, len(a...  22 us
    all_to_all x1, blocking collectives, body(): back = lax.all_to_all(weighted, EXPERT_AXES, 0, 0, tiled=True)  22 us
    ppermute x16, starting transfers between devices, ring(): return lax.ppermute(value, (axis, 'c'), perm)  20.1 us
    ppermute x16, waiting for transfers between devices, ring(): return lax.ppermute(value, (axis, 'c'), perm)  17.4 us
    ppermute x8, waiting for transfers between devices, swap(): return lax.ppermute(value, (axis, 'c'), perm)  15.3 us
    ppermute x8, starting transfers between devices, swap(): return lax.ppermute(value, (axis, 'c'), perm)  9.78 us
    all_to_all x1, waiting for transfers between devices, body(): lax.all_to_all(sent, EXPERT_AXES, 0, 0, tiled=True).astype(jnp.float32)  8.06 us
    pallas_call x1, Pallas kernels, attend(): pl.pallas_call(attend_kernel, out_shape=(shape, shape), in_specs=[anywher...  7.66 us
  transfers between devices with their start and end apart: 31, of which 13 were waited for; matrix products, arithmetic and copies ran while one was open for 2% of the time, Pallas kernels for 15%

profile of v5, /device:TPU:1, one launch (start us, length us, event | category | flops | bytes accessed | tf_op | source)
XLA Modules:
  0.0 148.4 jit_solution(2177400159122678388)
XLA Ops:
  0.0 7.7 %attend_rows.1 = (bf16[4,64,768]{2,1,0:T(8,128)(2,1)}, bf16[4,64,768]{2,1,0:T(8,128)(2,1)}) custom-call(s32[64]{0:T(128)} %lengths.1, bf16[64,384]{1,0:T(8,128)(2,1)} %queries.1, bf16[64,128]{1,0:T(8,128)(2,1)} %new_keys.1, bf16[64,128]{1,0:T(8,128)(2,1)} %new_values.1, bf16[64,256,128]{2,1,0:T(8,128)(2,1)} %cache_k.1, bf16[64,256,128]{2,1,0:T(8,128)(2,1)} %cache_v.1, ...), custom_call_target="tpu_custom_call" | custom-call | flops 301989888 | bytes 8388608 | tf_op jit(solution)/shard_map/attend_rows/pallas_call | solution.py:322
  7.7 1.5 %collective-permute-start = (bf16[4,64,768]{2,1,0:T(8,128)(2,1)}, bf16[4,64,768]{2,1,0:T(8,128)(2,1)S(1)}, u32[]{:S(2)}, u32[]{:S(2)}) collective-permute-start(bf16[4,64,768]{2,1,0:T(8,128)(2,1)} %get-tuple-element.22), channel_id=1, source_target_pairs={{0,1},{1,0},{2,3},{3,2},{4,5},{5,4},{6,7},{7,6},{8,9},{9,8},{10,11... | collective-permute-start | bytes 1179656 | tf_op jit(solution)/shard_map/ppermute | solution.py:384
  10.0 0.7 collective-permute-done
  10.7 1.1 fusion.21
  11.8 1.4 collective-permute-start.1
  13.2 1.4 collective-permute-start.3
  14.5 1.6 %collective-permute-start.2 = (bf16[64,768]{1,0:T(8,128)(2,1)S(1)}, bf16[64,768]{1,0:T(8,128)(2,1)S(1)}, u32[]{:S(2)}, u32[]{:S(2)}) collective-permute-start(bf16[64,768]{1,0:T(8,128)(2,1)S(1)} %get-tuple-element.53), channel_id=1, source_target_pairs={{0,4},{2,6},{4,0},{6,2},{1,5},{3,7},{5,1},{7,3},{8,12},{10,14},{12... | collective-permute-start | bytes 294920 | tf_op jit(solution)/shard_map/ppermute | solution.py:29
  16.2 0.9 collective-permute-done.1
  17.1 2.6 %collective-permute-done.2 = bf16[64,768]{1,0:T(8,128)(2,1)S(1)} collective-permute-done((bf16[64,768]{1,0:T(8,128)(2,1)S(1)}, bf16[64,768]{1,0:T(8,128)(2,1)S(1)}, u32[]{:S(2)}, u32[]{:S(2)}) %collective-permute-start.2) | collective-permute-done | bytes 98336 | tf_op jit(solution)/shard_map/ppermute | solution.py:29
  19.7 1.0 fusion.14
  20.7 1.0 convolution_convert_fusion
  21.7 5.2 %all-to-all-start = ((bf16[8,32,768]{2,1,0:T(8,128)(2,1)}), bf16[8,32,768]{2,1,0:T(8,128)(2,1)S(1)}, u32[]{:S(2)}, u32[]{:S(2)}) async-start(bf16[8,32,768]{2,1,0:T(8,128)(2,1)} %bitcast.6), calls=%async_computation | async-start | bytes 786432 | tf_op jit(solution)/shard_map/all_to_all | solution.py:405
  27.0 8.1 %all-to-all-done = bf16[8,32,768]{2,1,0:T(8,128)(2,1)S(1)} async-done(((bf16[8,32,768]{2,1,0:T(8,128)(2,1)}), bf16[8,32,768]{2,1,0:T(8,128)(2,1)S(1)}, u32[]{:S(2)}, u32[]{:S(2)}) %all-to-all-start) | async-done | bytes 393248 | tf_op jit(solution)/shard_map/all_to_all | solution.py:405
  35.5 3.9 %collective-permute-start.4 = (bf16[16,6144]{1,0:T(8,128)(2,1)S(1)}, bf16[16,6144]{1,0:T(8,128)(2,1)S(1)}, u32[]{:S(2)}, u32[]{:S(2)}) collective-permute-start(bf16[16,6144]{1,0:T(8,128)(2,1)S(1)} %bitcast.53), channel_id=1, source_target_pairs={{0,8},{1,25},{8,0},{9,17},{16,24},{17,9},{24,16},{25,1},{2,10},{3,... | collective-permute-start | bytes 589832 | tf_op jit(solution)/shard_map/ppermute | solution.py:47
  39.5 2.8 %collective-permute-start.6 = (bf16[16,6144]{1,0:T(8,128)(2,1)S(1)}, bf16[16,6144]{1,0:T(8,128)(2,1)S(1)}, u32[]{:S(2)}, u32[]{:S(2)}) collective-permute-start(bf16[16,6144]{1,0:T(8,128)(2,1)S(1)} %bitcast.55), channel_id=1, source_target_pairs={{0,32},{1,97},{32,0},{33,65},{64,96},{65,33},{96,64},{97,1},{2,34}... | collective-permute-start | bytes 589832 | tf_op jit(solution)/shard_map/ppermute | solution.py:47
  42.3 3.0 %collective-permute-done.6 = bf16[16,6144]{1,0:T(8,128)(2,1)S(1)} collective-permute-done((bf16[16,6144]{1,0:T(8,128)(2,1)S(1)}, bf16[16,6144]{1,0:T(8,128)(2,1)S(1)}, u32[]{:S(2)}, u32[]{:S(2)}) %collective-permute-start.6) | collective-permute-done | bytes 196640 | tf_op jit(solution)/shard_map/ppermute | solution.py:47
  45.6 0.4 collective-permute-start.10
  46.0 2.4 %collective-permute-start.8 = (bf16[32,6144]{1,0:T(8,128)(2,1)S(1)}, bf16[32,6144]{1,0:T(8,128)(2,1)S(1)}, u32[]{:S(2)}, u32[]{:S(2)}) collective-permute-start(bf16[32,6144]{1,0:T(8,128)(2,1)S(1)} %constant_dynamic-update-slice_fusion.refs_0_), channel_id=1, source_target_pairs={{0,32},{1,97},{32,64},{33,1},{64,96},{65,33},{96,0},{97,65},{2,34}... | collective-permute-start | bytes 1179656 | tf_op jit(solution)/shard_map/ppermute | solution.py:38
  48.4 4.0 %collective-permute-done.7.refs_3_ = bf16[32,6144]{1,0:T(8,128)(2,1)S(1)} collective-permute-done((bf16[32,6144]{1,0:T(8,128)(2,1)S(1)}, bf16[32,6144]{1,0:T(8,128)(2,1)S(1)}, u32[]{:S(2)}, u32[]{:S(2)}) %collective-permute-start.7) | collective-permute-done | bytes 393248 | tf_op jit(solution)/shard_map/ppermute | solution.py:47
  52.5 3.4 %collective-permute-start.15 = (bf16[32,6144]{1,0:T(8,128)(2,1)S(1)}, bf16[32,6144]{1,0:T(8,128)(2,1)S(1)}, u32[]{:S(2)}, u32[]{:S(2)}) collective-permute-start(bf16[32,6144]{1,0:T(8,128)(2,1)S(1)} %collective-permute-done.5.refs_1_), channel_id=1, source_target_pairs={{0,32},{1,97},{32,64},{33,1},{64,96},{65,33},{96,0},{97,65},{2,34}... | collective-permute-start | bytes 1179656 | tf_op jit(solution)/shard_map/ppermute | solution.py:38
  55.9 0.8 collective-permute-done.10.refs_2_
  56.8 3.1 %collective-permute-start.9 = (bf16[32,6144]{1,0:T(8,128)(2,1)S(1)}, bf16[32,6144]{1,0:T(8,128)(2,1)S(1)}, u32[]{:S(2)}, u32[]{:S(2)}) collective-permute-start(bf16[32,6144]{1,0:T(8,128)(2,1)S(1)} %collective-permute-done.8.refs_0_), channel_id=1, source_target_pairs={{0,32},{1,97},{32,64},{33,1},{64,96},{65,33},{96,0},{97,65},{2,34}... | collective-permute-start | bytes 1179656 | tf_op jit(solution)/shard_map/ppermute | solution.py:38
  59.9 1.0 collective-permute-done.17.refs_3_
  60.9 1.3 collective-permute-start.18
  62.3 2.4 %collective-permute-start.16 = (bf16[32,6144]{1,0:T(8,128)(2,1)S(1)}, bf16[32,6144]{1,0:T(8,128)(2,1)S(1)}, u32[]{:S(2)}, u32[]{:S(2)}) collective-permute-start(bf16[32,6144]{1,0:T(8,128)(2,1)S(1)} %collective-permute-done.15.refs_1_), channel_id=1, source_target_pairs={{0,32},{1,97},{32,64},{33,1},{64,96},{65,33},{96,0},{97,65},{2,34}... | collective-permute-start | bytes 1179656 | tf_op jit(solution)/shard_map/ppermute | solution.py:38
  64.7 8.2 %expert_rows_first.1 = (bf16[64,6144]{1,0:T(8,128)(2,1)S(1)}, bf16[64,6144]{1,0:T(8,128)(2,1)S(1)}, bf16[6144,512]{1,0:T(8,128)(2,1)S(1)}, bf16[6144,512]{1,0:T(8,128)(2,1)S(1)}, bf16[512,6144]{1,0:T(8,128)(2,1)S(1)}) custom-call(bf16[32,6144]{1,0:T(8,128)(2,1)S(1)} %constant_dynamic-update-slice_fusion.refs_0_, ...), custom_call_target="tpu_custom_call" | custom-call | flops 1000000 | bytes 100000 | tf_op jit(solution)/shard_map/expert_rows_first/pallas_call | solution.py:162
  73.0 0.8 lay_rows.1
  73.8 0.6 collective-permute-start.13
  74.5 4.8 %expert_rows.4 = (bf16[64,6144]{1,0:T(8,128)(2,1)S(1)}, bf16[64,6144]{1,0:T(8,128)(2,1)S(1)}) custom-call(bf16[32,6144]{1,0:T(8,128)(2,1)S(1)} %collective-permute-done.9.refs_4_.refs_0_, bf16[32,6144]{1,0:T(8,128)(2,1)S(1)} %collective-permute-done.16.refs_1_, bf16[32,6144]{1,0:T(8,128)(2,1)S(1)} %collective-permute-done.11.refs_5_.refs_2_, ...), custom_call_target="tpu_custom_call" | custom-call | flops 1000000 | bytes 100000 | tf_op jit(solution)/shard_map/expert_rows/pallas_call | solution.py:162
  79.3 0.7 collective-permute-start.19
  80.0 0.2 select_reduce_fusion.1
  80.4 1.3 collective-permute-start.25
  81.7 4.8 %expert_rows.5 = (bf16[64,6144]{1,0:T(8,128)(2,1)S(1)}, bf16[64,6144]{1,0:T(8,128)(2,1)S(1)}) custom-call(bf16[32,6144]{1,0:T(8,128)(2,1)S(1)} %collective-permute-done.8.refs_0_, bf16[32,6144]{1,0:T(8,128)(2,1)S(1)} %collective-permute-done.15.refs_1_, bf16[32,6144]{1,0:T(8,128)(2,1)S(1)} %collective-permute-done.10.refs_2_, ...), custom_call_target="tpu_custom_call" | custom-call | flops 1000000 | bytes 100000 | tf_op jit(solution)/shard_map/expert_rows/pallas_call | solution.py:162
  86.5 4.2 %expert_rows.3 = (bf16[64,6144]{1,0:T(8,128)(2,1)S(1)}, bf16[64,6144]{1,0:T(8,128)(2,1)S(1)}) custom-call(bf16[64,6144]{1,0:T(8,128)(2,1)S(1)} %collective-permute-done.12.refs_0_, bf16[64,6144]{1,0:T(8,128)(2,1)S(1)} %collective-permute-done.13.refs_1_, bf16[6144,512]{1,0:T(8,128)(2,1)S(1)} %get-tuple-element.27.refs_2_.refs_4_, ...), custom_call_target="tpu_custom_call" | custom-call | flops 1000000 | bytes 100000 | tf_op jit(solution)/shard_map/expert_rows/pallas_call | solution.py:162
  90.7 2.7 %collective-permute-start.14 = (bf16[64,6144]{1,0:T(8,128)(2,1)S(1)}, bf16[64,6144]{1,0:T(8,128)(2,1)S(1)}, u32[]{:S(2)}, u32[]{:S(2)}) collective-permute-start(bf16[64,6144]{1,0:T(8,128)(2,1)S(1)} %get-tuple-element.30), channel_id=1, source_target_pairs={{0,32},{1,97},{32,64},{33,1},{64,96},{65,33},{96,0},{97,65},{2,34}... | collective-permute-start | bytes 2359304 | tf_op jit(solution)/shard_map/ppermute | solution.py:38
  93.4 1.1 collective-permute-start.24
  95.0 0.5 collective-permute-start.26
  95.4 11.9 %collective-permute-done.14 = bf16[64,6144]{1,0:T(8,128)(2,1)S(1)} collective-permute-done((bf16[64,6144]{1,0:T(8,128)(2,1)S(1)}, bf16[64,6144]{1,0:T(8,128)(2,1)S(1)}, u32[]{:S(2)}, u32[]{:S(2)}) %collective-permute-start.14) | collective-permute-done | bytes 786464 | tf_op jit(solution)/shard_map/ppermute | solution.py:38
  107.3 3.7 %collective-permute-done.20 = bf16[64,6144]{1,0:T(8,128)(2,1)S(1)} collective-permute-done((bf16[64,6144]{1,0:T(8,128)(2,1)S(1)}, bf16[64,6144]{1,0:T(8,128)(2,1)S(1)}, u32[]{:S(2)}, u32[]{:S(2)}) %collective-permute-start.20) | collective-permute-done | bytes 786464 | tf_op jit(solution)/shard_map/ppermute | solution.py:38
  111.0 0.3 fusion.43
  111.4 2.1 %collective-permute-start.21 = (bf16[16,6144]{1,0:T(8,128)(2,1)S(1)}, bf16[16,6144]{1,0:T(8,128)(2,1)S(1)}, u32[]{:S(2)}, u32[]{:S(2)}) collective-permute-start(bf16[16,6144]{1,0:T(8,128)(2,1)S(1)} %get-tuple-element.45), channel_id=1, source_target_pairs={{0,8},{1,25},{8,0},{9,17},{16,24},{17,9},{24,16},{25,1},{2,10},{3,... | collective-permute-start | bytes 589832 | tf_op jit(solution)/shard_map/ppermute | solution.py:47
  113.5 2.3 %collective-permute-start.23 = (bf16[16,6144]{1,0:T(8,128)(2,1)S(1)}, bf16[16,6144]{1,0:T(8,128)(2,1)S(1)}, u32[]{:S(2)}, u32[]{:S(2)}) collective-permute-start(bf16[16,6144]{1,0:T(8,128)(2,1)S(1)} %get-tuple-element.46), channel_id=1, source_target_pairs={{0,16},{8,24},{16,0},{24,8},{1,17},{9,25},{17,1},{25,9},{2,18},{10... | collective-permute-start | bytes 589832 | tf_op jit(solution)/shard_map/ppermute | solution.py:29
  115.8 0.3 fusion.44
  116.1 0.8 collective-permute-start.27
  116.9 3.4 %collective-permute-done.21 = bf16[16,6144]{1,0:T(8,128)(2,1)S(1)} collective-permute-done((bf16[16,6144]{1,0:T(8,128)(2,1)S(1)}, bf16[16,6144]{1,0:T(8,128)(2,1)S(1)}, u32[]{:S(2)}, u32[]{:S(2)}) %collective-permute-start.21) | collective-permute-done | bytes 196640 | tf_op jit(solution)/shard_map/ppermute | solution.py:47
  120.2 4.8 %collective-permute-done.22 = bf16[16,6144]{1,0:T(8,128)(2,1)S(1)} collective-permute-done((bf16[16,6144]{1,0:T(8,128)(2,1)S(1)}, bf16[16,6144]{1,0:T(8,128)(2,1)S(1)}, u32[]{:S(2)}, u32[]{:S(2)}) %collective-permute-start.22) | collective-permute-done | bytes 196640 | tf_op jit(solution)/shard_map/ppermute | solution.py:47
  125.5 22.0 %all_to_all.10 = bf16[8,32,768]{2,1,0:T(8,128)(2,1)S(1)} all-to-all(bf16[8,32,768]{2,1,0:T(8,128)(2,1)S(1)} %fusion.7), channel_id=1, replica_groups=mesh['y'=4,'z'=4,'x'=4,'c'=2] {'x','c'}, dimensions={0} | all-to-all | bytes 786432 | tf_op jit(solution)/shard_map/all_to_all | solution.py:458
  147.5 0.9 fusion
  (73 shorter events, 3.0 us)
Async XLA Ops:
  0.0 80.0 %copy-start = (bf16[6144,8]{0,1:T(8,128)(2,1)S(1)}, bf16[6144,8]{0,1:T(8,128)(2,1)}, u32[]{:S(2)}) copy-start(bf16[6144,8]{0,1:T(8,128)(2,1)} %param.23) | copy-start | bytes 294916
  0.0 9.2 %copy-start.3 = (s32[64,2]{0,1:T(2,128)S(1)}, s32[64,2]{0,1:T(2,128)}, u32[]{:S(2)}) copy-start(s32[64,2]{0,1:T(2,128)} %param.24) | copy-start | bytes 1540
  7.7 3.1 %collective-permute-start = (bf16[4,64,768]{2,1,0:T(8,128)(2,1)}, bf16[4,64,768]{2,1,0:T(8,128)(2,1)S(1)}, u32[]{:S(2)}, u32[]{:S(2)}) collective-permute-start(bf16[4,64,768]{2,1,0:T(8,128)(2,1)} %get-tuple-element.22), channel_id=1, source_target_pairs={{0,1},{1,0},{2,3},{3,2},{4,5},{5,4},{6,7},{7,6},{8,9},{9,8},{10,11... | collective-permute-start | bytes 1179656 | tf_op jit(solution)/shard_map/ppermute | solution.py:384
  9.8 17.1 %copy-start.2 = (bf16[6144]{0:T(1024)(128)(2,1)S(1)}, bf16[6144]{0:T(1024)(128)(2,1)}, u32[]{:S(2)}) copy-start(bf16[6144]{0:T(1024)(128)(2,1)} %param.22) | copy-start | bytes 36868
  11.8 5.3 %collective-permute-start.1 = (bf16[64,768]{1,0:T(8,128)(2,1)S(1)}, bf16[64,768]{1,0:T(8,128)(2,1)S(1)}, u32[]{:S(2)}, u32[]{:S(2)}) collective-permute-start(bf16[64,768]{1,0:T(8,128)(2,1)S(1)} %get-tuple-element.51), channel_id=1, source_target_pairs={{0,2},{2,4},{4,6},{6,0},{1,3},{3,5},{5,7},{7,1},{8,10},{10,12},{12... | collective-permute-start | bytes 294920 | tf_op jit(solution)/shard_map/ppermute | solution.py:29
  13.2 3.9 %collective-permute-start.3 = (bf16[64,768]{1,0:T(8,128)(2,1)S(1)}, bf16[64,768]{1,0:T(8,128)(2,1)S(1)}, u32[]{:S(2)}, u32[]{:S(2)}) collective-permute-start(bf16[64,768]{1,0:T(8,128)(2,1)S(1)} %get-tuple-element.52), channel_id=1, source_target_pairs={{0,6},{2,0},{4,2},{6,4},{1,7},{3,1},{5,3},{7,5},{8,14},{10,8},{12,... | collective-permute-start | bytes 294920 | tf_op jit(solution)/shard_map/ppermute | solution.py:29
  14.5 5.2 %collective-permute-start.2 = (bf16[64,768]{1,0:T(8,128)(2,1)S(1)}, bf16[64,768]{1,0:T(8,128)(2,1)S(1)}, u32[]{:S(2)}, u32[]{:S(2)}) collective-permute-start(bf16[64,768]{1,0:T(8,128)(2,1)S(1)} %get-tuple-element.53), channel_id=1, source_target_pairs={{0,4},{2,6},{4,0},{6,2},{1,5},{3,7},{5,1},{7,3},{8,12},{10,14},{12... | collective-permute-start | bytes 294920 | tf_op jit(solution)/shard_map/ppermute | solution.py:29
  21.7 13.3 %all-to-all-start = ((bf16[8,32,768]{2,1,0:T(8,128)(2,1)}), bf16[8,32,768]{2,1,0:T(8,128)(2,1)S(1)}, u32[]{:S(2)}, u32[]{:S(2)}) async-start(bf16[8,32,768]{2,1,0:T(8,128)(2,1)} %bitcast.6), calls=%async_computation | async-start | bytes 786432 | tf_op jit(solution)/shard_map/all_to_all | solution.py:405
  35.5 10.0 %collective-permute-start.4 = (bf16[16,6144]{1,0:T(8,128)(2,1)S(1)}, bf16[16,6144]{1,0:T(8,128)(2,1)S(1)}, u32[]{:S(2)}, u32[]{:S(2)}) collective-permute-start(bf16[16,6144]{1,0:T(8,128)(2,1)S(1)} %bitcast.53), channel_id=1, source_target_pairs={{0,8},{1,25},{8,0},{9,17},{16,24},{17,9},{24,16},{25,1},{2,10},{3,... | collective-permute-start | bytes 589832 | tf_op jit(solution)/shard_map/ppermute | solution.py:47
  39.5 5.9 %collective-permute-start.6 = (bf16[16,6144]{1,0:T(8,128)(2,1)S(1)}, bf16[16,6144]{1,0:T(8,128)(2,1)S(1)}, u32[]{:S(2)}, u32[]{:S(2)}) collective-permute-start(bf16[16,6144]{1,0:T(8,128)(2,1)S(1)} %bitcast.55), channel_id=1, source_target_pairs={{0,32},{1,97},{32,0},{33,65},{64,96},{65,33},{96,64},{97,1},{2,34}... | collective-permute-start | bytes 589832 | tf_op jit(solution)/shard_map/ppermute | solution.py:47
  45.4 7.0 %collective-permute-start.7 = (bf16[32,6144]{1,0:T(8,128)(2,1)S(1)}, bf16[32,6144]{1,0:T(8,128)(2,1)S(1)}, u32[]{:S(2)}, u32[]{:S(2)}) collective-permute-start(bf16[32,6144]{1,0:T(8,128)(2,1)S(1)} %constant_dynamic-update-slice_fusion.2.refs_2_), channel_id=1, source_target_pairs={{0,96},{1,33},{32,64},{33,1},{64,32},{65,97},{96,0},{97,65},{2,98}... | collective-permute-start | bytes 1179656 | tf_op jit(solution)/shard_map/ppermute | solution.py:47
  45.5 7.0 %collective-permute-start.5 = (bf16[32,6144]{1,0:T(8,128)(2,1)S(1)}, bf16[32,6144]{1,0:T(8,128)(2,1)S(1)}, u32[]{:S(2)}, u32[]{:S(2)}) collective-permute-start(bf16[32,6144]{1,0:T(8,128)(2,1)S(1)} %constant_dynamic-update-slice_fusion.refs_0_), channel_id=1, source_target_pairs={{0,24},{1,9},{8,16},{9,1},{16,8},{17,25},{24,0},{25,17},{2,26},{3,... | collective-permute-start | bytes 1179656 | tf_op jit(solution)/shard_map/ppermute | solution.py:47
  45.6 11.1 %collective-permute-start.10 = (bf16[32,6144]{1,0:T(8,128)(2,1)S(1)}, bf16[32,6144]{1,0:T(8,128)(2,1)S(1)}, u32[]{:S(2)}, u32[]{:S(2)}) collective-permute-start(bf16[32,6144]{1,0:T(8,128)(2,1)S(1)} %constant_dynamic-update-slice_fusion.2.refs_2_), channel_id=1, source_target_pairs={{0,8},{1,25},{8,16},{9,1},{16,24},{17,9},{24,0},{25,17},{2,10},{3,... | collective-permute-start | bytes 1179656 | tf_op jit(solution)/shard_map/ppermute | solution.py:38
  46.0 10.8 %collective-permute-start.8 = (bf16[32,6144]{1,0:T(8,128)(2,1)S(1)}, bf16[32,6144]{1,0:T(8,128)(2,1)S(1)}, u32[]{:S(2)}, u32[]{:S(2)}) collective-permute-start(bf16[32,6144]{1,0:T(8,128)(2,1)S(1)} %constant_dynamic-update-slice_fusion.refs_0_), channel_id=1, source_target_pairs={{0,32},{1,97},{32,64},{33,1},{64,96},{65,33},{96,0},{97,65},{2,34}... | collective-permute-start | bytes 1179656 | tf_op jit(solution)/shard_map/ppermute | solution.py:38
  52.4 8.6 %collective-permute-start.17 = (bf16[32,6144]{1,0:T(8,128)(2,1)S(1)}, bf16[32,6144]{1,0:T(8,128)(2,1)S(1)}, u32[]{:S(2)}, u32[]{:S(2)}) collective-permute-start(bf16[32,6144]{1,0:T(8,128)(2,1)S(1)} %collective-permute-done.7.refs_3_), channel_id=1, source_target_pairs={{0,8},{1,25},{8,16},{9,1},{16,24},{17,9},{24,0},{25,17},{2,10},{3,... | collective-permute-start | bytes 1179656 | tf_op jit(solution)/shard_map/ppermute | solution.py:38
  52.5 9.8 %collective-permute-start.15 = (bf16[32,6144]{1,0:T(8,128)(2,1)S(1)}, bf16[32,6144]{1,0:T(8,128)(2,1)S(1)}, u32[]{:S(2)}, u32[]{:S(2)}) collective-permute-start(bf16[32,6144]{1,0:T(8,128)(2,1)S(1)} %collective-permute-done.5.refs_1_), channel_id=1, source_target_pairs={{0,32},{1,97},{32,64},{33,1},{64,96},{65,33},{96,0},{97,65},{2,34}... | collective-permute-start | bytes 1179656 | tf_op jit(solution)/shard_map/ppermute | solution.py:38
  56.7 16.2 %collective-permute-start.11 = (bf16[32,6144]{1,0:T(8,128)(2,1)S(1)}, bf16[32,6144]{1,0:T(8,128)(2,1)S(1)}, u32[]{:S(2)}, u32[]{:S(2)}) collective-permute-start(bf16[32,6144]{1,0:T(8,128)(2,1)S(1)} %collective-permute-done.10.refs_2_), channel_id=1, source_target_pairs={{0,8},{1,25},{8,16},{9,1},{16,24},{17,9},{24,0},{25,17},{2,10},{3,... | collective-permute-start | bytes 1179656 | tf_op jit(solution)/shard_map/ppermute | solution.py:38
  56.8 16.2 %collective-permute-start.9 = (bf16[32,6144]{1,0:T(8,128)(2,1)S(1)}, bf16[32,6144]{1,0:T(8,128)(2,1)S(1)}, u32[]{:S(2)}, u32[]{:S(2)}) collective-permute-start(bf16[32,6144]{1,0:T(8,128)(2,1)S(1)} %collective-permute-done.8.refs_0_), channel_id=1, source_target_pairs={{0,32},{1,97},{32,64},{33,1},{64,96},{65,33},{96,0},{97,65},{2,34}... | collective-permute-start | bytes 1179656 | tf_op jit(solution)/shard_map/ppermute | solution.py:38
  60.9 13.5 %collective-permute-start.18 = (bf16[32,6144]{1,0:T(8,128)(2,1)S(1)}, bf16[32,6144]{1,0:T(8,128)(2,1)S(1)}, u32[]{:S(2)}, u32[]{:S(2)}) collective-permute-start(bf16[32,6144]{1,0:T(8,128)(2,1)S(1)} %collective-permute-done.17.refs_3_), channel_id=1, source_target_pairs={{0,8},{1,25},{8,16},{9,1},{16,24},{17,9},{24,0},{25,17},{2,10},{3,... | collective-permute-start | bytes 1179656 | tf_op jit(solution)/shard_map/ppermute | solution.py:38
  62.3 12.2 %collective-permute-start.16 = (bf16[32,6144]{1,0:T(8,128)(2,1)S(1)}, bf16[32,6144]{1,0:T(8,128)(2,1)S(1)}, u32[]{:S(2)}, u32[]{:S(2)}) collective-permute-start(bf16[32,6144]{1,0:T(8,128)(2,1)S(1)} %collective-permute-done.15.refs_1_), channel_id=1, source_target_pairs={{0,32},{1,97},{32,64},{33,1},{64,96},{65,33},{96,0},{97,65},{2,34}... | collective-permute-start | bytes 1179656 | tf_op jit(solution)/shard_map/ppermute | solution.py:38
  73.8 12.7 %collective-permute-start.12 = (bf16[64,6144]{1,0:T(8,128)(2,1)S(1)}, bf16[64,6144]{1,0:T(8,128)(2,1)S(1)}, u32[]{:S(2)}, u32[]{:S(2)}) collective-permute-start(bf16[64,6144]{1,0:T(8,128)(2,1)S(1)} %get-tuple-element.25), channel_id=1, source_target_pairs={{0,96},{1,33},{32,0},{33,65},{64,32},{65,97},{96,64},{97,1},{2,98}... | collective-permute-start | bytes 2359304 | tf_op jit(solution)/shard_map/ppermute | solution.py:38
  73.8 12.7 %collective-permute-start.13 = (bf16[64,6144]{1,0:T(8,128)(2,1)S(1)}, bf16[64,6144]{1,0:T(8,128)(2,1)S(1)}, u32[]{:S(2)}, u32[]{:S(2)}) collective-permute-start(bf16[64,6144]{1,0:T(8,128)(2,1)S(1)} %get-tuple-element.26), channel_id=1, source_target_pairs={{0,24},{1,9},{8,0},{9,17},{16,8},{17,25},{24,16},{25,1},{2,26},{3,... | collective-permute-start | bytes 2359304 | tf_op jit(solution)/shard_map/ppermute | solution.py:38
  79.3 15.2 %collective-permute-start.19 = (bf16[64,6144]{1,0:T(8,128)(2,1)S(1)}, bf16[64,6144]{1,0:T(8,128)(2,1)S(1)}, u32[]{:S(2)}, u32[]{:S(2)}) collective-permute-start(bf16[64,6144]{1,0:T(8,128)(2,1)S(1)} %get-tuple-element.31.refs_7_), channel_id=1, source_target_pairs={{0,96},{1,33},{32,0},{33,65},{64,32},{65,97},{96,64},{97,1},{2,98}... | collective-permute-start | bytes 2359304 | tf_op jit(solution)/shard_map/ppermute | solution.py:38
  80.4 14.4 %collective-permute-start.25 = (bf16[64,6144]{1,0:T(8,128)(2,1)S(1)}, bf16[64,6144]{1,0:T(8,128)(2,1)S(1)}, u32[]{:S(2)}, u32[]{:S(2)}) collective-permute-start(bf16[64,6144]{1,0:T(8,128)(2,1)S(1)} %get-tuple-element.32.refs_8_), channel_id=1, source_target_pairs={{0,24},{1,9},{8,0},{9,17},{16,8},{17,25},{24,16},{25,1},{2,26},{3,... | collective-permute-start | bytes 2359304 | tf_op jit(solution)/shard_map/ppermute | solution.py:38
  90.7 16.6 %collective-permute-start.14 = (bf16[64,6144]{1,0:T(8,128)(2,1)S(1)}, bf16[64,6144]{1,0:T(8,128)(2,1)S(1)}, u32[]{:S(2)}, u32[]{:S(2)}) collective-permute-start(bf16[64,6144]{1,0:T(8,128)(2,1)S(1)} %get-tuple-element.30), channel_id=1, source_target_pairs={{0,32},{1,97},{32,64},{33,1},{64,96},{65,33},{96,0},{97,65},{2,34}... | collective-permute-start | bytes 2359304 | tf_op jit(solution)/shard_map/ppermute | solution.py:38
  93.4 22.3 %collective-permute-start.24 = (bf16[64,6144]{1,0:T(8,128)(2,1)S(1)}, bf16[64,6144]{1,0:T(8,128)(2,1)S(1)}, u32[]{:S(2)}, u32[]{:S(2)}) collective-permute-start(bf16[64,6144]{1,0:T(8,128)(2,1)S(1)} %get-tuple-element.35), channel_id=1, source_target_pairs={{0,8},{1,25},{8,16},{9,1},{16,24},{17,9},{24,0},{25,17},{2,10},{3,... | collective-permute-start | bytes 2359304 | tf_op jit(solution)/shard_map/ppermute | solution.py:38
  94.7 16.3 %collective-permute-start.20 = (bf16[64,6144]{1,0:T(8,128)(2,1)S(1)}, bf16[64,6144]{1,0:T(8,128)(2,1)S(1)}, u32[]{:S(2)}, u32[]{:S(2)}) collective-permute-start(bf16[64,6144]{1,0:T(8,128)(2,1)S(1)} %add_convert_fusion.1), channel_id=1, source_target_pairs={{0,96},{1,33},{32,0},{33,65},{64,32},{65,97},{96,64},{97,1},{2,98}... | collective-permute-start | bytes 2359304 | tf_op jit(solution)/shard_map/ppermute | solution.py:38
  95.0 20.8 %collective-permute-start.26 = (bf16[64,6144]{1,0:T(8,128)(2,1)S(1)}, bf16[64,6144]{1,0:T(8,128)(2,1)S(1)}, u32[]{:S(2)}, u32[]{:S(2)}) collective-permute-start(bf16[64,6144]{1,0:T(8,128)(2,1)S(1)} %add_convert_fusion), channel_id=1, source_target_pairs={{0,24},{1,9},{8,0},{9,17},{16,8},{17,25},{24,16},{25,1},{2,26},{3,... | collective-permute-start | bytes 2359304 | tf_op jit(solution)/shard_map/ppermute | solution.py:38
  111.4 8.8 %collective-permute-start.21 = (bf16[16,6144]{1,0:T(8,128)(2,1)S(1)}, bf16[16,6144]{1,0:T(8,128)(2,1)S(1)}, u32[]{:S(2)}, u32[]{:S(2)}) collective-permute-start(bf16[16,6144]{1,0:T(8,128)(2,1)S(1)} %get-tuple-element.45), channel_id=1, source_target_pairs={{0,8},{1,25},{8,0},{9,17},{16,24},{17,9},{24,16},{25,1},{2,10},{3,... | collective-permute-start | bytes 589832 | tf_op jit(solution)/shard_map/ppermute | solution.py:47
  113.5 6.8 %collective-permute-start.23 = (bf16[16,6144]{1,0:T(8,128)(2,1)S(1)}, bf16[16,6144]{1,0:T(8,128)(2,1)S(1)}, u32[]{:S(2)}, u32[]{:S(2)}) collective-permute-start(bf16[16,6144]{1,0:T(8,128)(2,1)S(1)} %get-tuple-element.46), channel_id=1, source_target_pairs={{0,16},{8,24},{16,0},{24,8},{1,17},{9,25},{17,1},{25,9},{2,18},{10... | collective-permute-start | bytes 589832 | tf_op jit(solution)/shard_map/ppermute | solution.py:29
  115.7 9.3 %collective-permute-start.22 = (bf16[16,6144]{1,0:T(8,128)(2,1)S(1)}, bf16[16,6144]{1,0:T(8,128)(2,1)S(1)}, u32[]{:S(2)}, u32[]{:S(2)}) collective-permute-start(bf16[16,6144]{1,0:T(8,128)(2,1)S(1)} %get-tuple-element.47), channel_id=1, source_target_pairs={{0,24},{1,9},{8,16},{9,1},{16,8},{17,25},{24,0},{25,17},{2,26},{3,... | collective-permute-start | bytes 589832 | tf_op jit(solution)/shard_map/ppermute | solution.py:47
  116.1 9.1 %collective-permute-start.27 = (bf16[16,6144]{1,0:T(8,128)(2,1)S(1)}, bf16[16,6144]{1,0:T(8,128)(2,1)S(1)}, u32[]{:S(2)}, u32[]{:S(2)}) collective-permute-start(bf16[16,6144]{1,0:T(8,128)(2,1)S(1)} %get-tuple-element.48), channel_id=1, source_target_pairs={{0,32},{1,97},{32,0},{33,65},{64,96},{65,33},{96,64},{97,1},{2,34}... | collective-permute-start | bytes 589832 | tf_op jit(solution)/shard_map/ppermute | solution.py:47
  116.9 8.3 %collective-permute-start.29 = (bf16[16,6144]{1,0:T(8,128)(2,1)S(1)}, bf16[16,6144]{1,0:T(8,128)(2,1)S(1)}, u32[]{:S(2)}, u32[]{:S(2)}) collective-permute-start(bf16[16,6144]{1,0:T(8,128)(2,1)S(1)} %get-tuple-element.49), channel_id=1, source_target_pairs={{0,64},{32,96},{64,0},{96,32},{1,65},{33,97},{65,1},{97,33},{2,66}... | collective-permute-start | bytes 589832 | tf_op jit(solution)/shard_map/ppermute | solution.py:29
  120.2 5.0 %collective-permute-start.28 = (bf16[16,6144]{1,0:T(8,128)(2,1)S(1)}, bf16[16,6144]{1,0:T(8,128)(2,1)S(1)}, u32[]{:S(2)}, u32[]{:S(2)}) collective-permute-start(bf16[16,6144]{1,0:T(8,128)(2,1)S(1)} %get-tuple-element.50), channel_id=1, source_target_pairs={{0,96},{1,33},{32,64},{33,1},{64,32},{65,97},{96,0},{97,65},{2,98}... | collective-permute-start | bytes 589832 | tf_op jit(solution)/shard_map/ppermute | solution.py:47
  125.3 23.1 %copy-start.1 = (bf16[6144,8]{0,1:T(8,128)(2,1)S(1)}, bf16[6144,8]{0,1:T(8,128)(2,1)}, u32[]{:S(2)}) copy-start(bf16[6144,8]{0,1:T(8,128)(2,1)} %param.23) | copy-start | bytes 294916

commit v6 on v5

--- a/solution.py
+++ b/solution.py
@@ -17,7 +17,7 @@
 EXPERT_AXES = ("x", "c")
 DEEP = 8
 WIDE = 6
-BLOCK = 8
+BLOCK = 16
 PARTS = 8
 EXPERT_VMEM = 8 * 1024 * 1024
 VMEM = 60 * 1024 * 1024

time: 149 us -> 148 us (level)
  no operation moved by 1% of the time
where the time goes in v6:
time: 148 us; the launch traced here: 147 us
  waiting for transfers between devices  45.1 us (30%)
  starting transfers between devices  43.3 us (29%)
  Pallas kernels  29.5 us (20%)
  blocking collectives  21.9 us (15%)
  other arithmetic  4.14 us (3%)
  matrix products  2.24 us (2%)
    pallas_call x4, Pallas kernels, expert_call(): pl.pallas_call(functools.partial(expert_kernel, taken, given, kept, len(a...  22 us
    all_to_all x1, blocking collectives, body(): back = lax.all_to_all(weighted, EXPERT_AXES, 0, 0, tiled=True)  21.9 us
    ppermute x16, starting transfers between devices, ring(): return lax.ppermute(value, (axis, 'c'), perm)  20.1 us
    ppermute x16, waiting for transfers between devices, ring(): return lax.ppermute(value, (axis, 'c'), perm)  17.4 us
    ppermute x8, waiting for transfers between devices, swap(): return lax.ppermute(value, (axis, 'c'), perm)  15.4 us
    ppermute x8, starting transfers between devices, swap(): return lax.ppermute(value, (axis, 'c'), perm)  9.81 us
    all_to_all x1, waiting for transfers between devices, body(): lax.all_to_all(sent, EXPERT_AXES, 0, 0, tiled=True).astype(jnp.float32)  8.06 us
    pallas_call x1, Pallas kernels, attend(): pl.pallas_call(attend_kernel, out_shape=(shape, shape), in_specs=[anywher...  6.72 us
  transfers between devices with their start and end apart: 31, of which 13 were waited for; matrix products, arithmetic and copies ran while one was open for 2% of the time, Pallas kernels for 15%

profile of v6, /device:TPU:1, one launch (start us, length us, event | category | flops | bytes accessed | tf_op | source)
XLA Modules:
  0.0 147.4 jit_solution(4437047307183004800)
XLA Ops:
  0.0 6.7 %attend_rows.1 = (bf16[4,64,768]{2,1,0:T(8,128)(2,1)}, bf16[4,64,768]{2,1,0:T(8,128)(2,1)}) custom-call(s32[64]{0:T(128)} %lengths.1, bf16[64,384]{1,0:T(8,128)(2,1)} %queries.1, bf16[64,128]{1,0:T(8,128)(2,1)} %new_keys.1, bf16[64,128]{1,0:T(8,128)(2,1)} %new_values.1, bf16[64,256,128]{2,1,0:T(8,128)(2,1)} %cache_k.1, bf16[64,256,128]{2,1,0:T(8,128)(2,1)} %cache_v.1, ...), custom_call_target="tpu_custom_call" | custom-call | flops 301989888 | bytes 8388608 | tf_op jit(solution)/shard_map/attend_rows/pallas_call | solution.py:322
  6.7 1.5 %collective-permute-start = (bf16[4,64,768]{2,1,0:T(8,128)(2,1)}, bf16[4,64,768]{2,1,0:T(8,128)(2,1)S(1)}, u32[]{:S(2)}, u32[]{:S(2)}) collective-permute-start(bf16[4,64,768]{2,1,0:T(8,128)(2,1)} %get-tuple-element.22), channel_id=1, source_target_pairs={{0,1},{1,0},{2,3},{3,2},{4,5},{5,4},{6,7},{7,6},{8,9},{9,8},{10,11... | collective-permute-start | bytes 1179656 | tf_op jit(solution)/shard_map/ppermute | solution.py:384
  9.1 0.7 collective-permute-done
  9.8 1.1 fusion.21
  10.9 1.4 collective-permute-start.1
  12.2 1.4 collective-permute-start.3
  13.6 1.6 %collective-permute-start.2 = (bf16[64,768]{1,0:T(8,128)(2,1)S(1)}, bf16[64,768]{1,0:T(8,128)(2,1)S(1)}, u32[]{:S(2)}, u32[]{:S(2)}) collective-permute-start(bf16[64,768]{1,0:T(8,128)(2,1)S(1)} %get-tuple-element.53), channel_id=1, source_target_pairs={{0,4},{2,6},{4,0},{6,2},{1,5},{3,7},{5,1},{7,3},{8,12},{10,14},{12... | collective-permute-start | bytes 294920 | tf_op jit(solution)/shard_map/ppermute | solution.py:29
  15.2 0.9 collective-permute-done.1
  16.2 2.6 %collective-permute-done.2 = bf16[64,768]{1,0:T(8,128)(2,1)S(1)} collective-permute-done((bf16[64,768]{1,0:T(8,128)(2,1)S(1)}, bf16[64,768]{1,0:T(8,128)(2,1)S(1)}, u32[]{:S(2)}, u32[]{:S(2)}) %collective-permute-start.2) | collective-permute-done | bytes 98336 | tf_op jit(solution)/shard_map/ppermute | solution.py:29
  18.8 1.0 fusion.14
  19.8 1.0 convolution_convert_fusion
  20.8 5.2 %all-to-all-start = ((bf16[8,32,768]{2,1,0:T(8,128)(2,1)}), bf16[8,32,768]{2,1,0:T(8,128)(2,1)S(1)}, u32[]{:S(2)}, u32[]{:S(2)}) async-start(bf16[8,32,768]{2,1,0:T(8,128)(2,1)} %bitcast.6), calls=%async_computation | async-start | bytes 786432 | tf_op jit(solution)/shard_map/all_to_all | solution.py:405
  26.1 8.1 %all-to-all-done = bf16[8,32,768]{2,1,0:T(8,128)(2,1)S(1)} async-done(((bf16[8,32,768]{2,1,0:T(8,128)(2,1)}), bf16[8,32,768]{2,1,0:T(8,128)(2,1)S(1)}, u32[]{:S(2)}, u32[]{:S(2)}) %all-to-all-start) | async-done | bytes 393248 | tf_op jit(solution)/shard_map/all_to_all | solution.py:405
  34.6 3.9 %collective-permute-start.4 = (bf16[16,6144]{1,0:T(8,128)(2,1)S(1)}, bf16[16,6144]{1,0:T(8,128)(2,1)S(1)}, u32[]{:S(2)}, u32[]{:S(2)}) collective-permute-start(bf16[16,6144]{1,0:T(8,128)(2,1)S(1)} %bitcast.53), channel_id=1, source_target_pairs={{0,8},{1,25},{8,0},{9,17},{16,24},{17,9},{24,16},{25,1},{2,10},{3,... | collective-permute-start | bytes 589832 | tf_op jit(solution)/shard_map/ppermute | solution.py:47
  38.5 2.8 %collective-permute-start.6 = (bf16[16,6144]{1,0:T(8,128)(2,1)S(1)}, bf16[16,6144]{1,0:T(8,128)(2,1)S(1)}, u32[]{:S(2)}, u32[]{:S(2)}) collective-permute-start(bf16[16,6144]{1,0:T(8,128)(2,1)S(1)} %bitcast.55), channel_id=1, source_target_pairs={{0,32},{1,97},{32,0},{33,65},{64,96},{65,33},{96,64},{97,1},{2,34}... | collective-permute-start | bytes 589832 | tf_op jit(solution)/shard_map/ppermute | solution.py:47
  41.4 3.0 %collective-permute-done.6 = bf16[16,6144]{1,0:T(8,128)(2,1)S(1)} collective-permute-done((bf16[16,6144]{1,0:T(8,128)(2,1)S(1)}, bf16[16,6144]{1,0:T(8,128)(2,1)S(1)}, u32[]{:S(2)}, u32[]{:S(2)}) %collective-permute-start.6) | collective-permute-done | bytes 196640 | tf_op jit(solution)/shard_map/ppermute | solution.py:47
  44.7 0.4 collective-permute-start.10
  45.1 2.4 %collective-permute-start.8 = (bf16[32,6144]{1,0:T(8,128)(2,1)S(1)}, bf16[32,6144]{1,0:T(8,128)(2,1)S(1)}, u32[]{:S(2)}, u32[]{:S(2)}) collective-permute-start(bf16[32,6144]{1,0:T(8,128)(2,1)S(1)} %constant_dynamic-update-slice_fusion.refs_0_), channel_id=1, source_target_pairs={{0,32},{1,97},{32,64},{33,1},{64,96},{65,33},{96,0},{97,65},{2,34}... | collective-permute-start | bytes 1179656 | tf_op jit(solution)/shard_map/ppermute | solution.py:38
  47.5 4.0 %collective-permute-done.7.refs_3_ = bf16[32,6144]{1,0:T(8,128)(2,1)S(1)} collective-permute-done((bf16[32,6144]{1,0:T(8,128)(2,1)S(1)}, bf16[32,6144]{1,0:T(8,128)(2,1)S(1)}, u32[]{:S(2)}, u32[]{:S(2)}) %collective-permute-start.7) | collective-permute-done | bytes 393248 | tf_op jit(solution)/shard_map/ppermute | solution.py:47
  51.6 3.4 %collective-permute-start.15 = (bf16[32,6144]{1,0:T(8,128)(2,1)S(1)}, bf16[32,6144]{1,0:T(8,128)(2,1)S(1)}, u32[]{:S(2)}, u32[]{:S(2)}) collective-permute-start(bf16[32,6144]{1,0:T(8,128)(2,1)S(1)} %collective-permute-done.5.refs_1_), channel_id=1, source_target_pairs={{0,32},{1,97},{32,64},{33,1},{64,96},{65,33},{96,0},{97,65},{2,34}... | collective-permute-start | bytes 1179656 | tf_op jit(solution)/shard_map/ppermute | solution.py:38
  54.9 0.8 collective-permute-done.10.refs_2_
  55.8 3.1 %collective-permute-start.9 = (bf16[32,6144]{1,0:T(8,128)(2,1)S(1)}, bf16[32,6144]{1,0:T(8,128)(2,1)S(1)}, u32[]{:S(2)}, u32[]{:S(2)}) collective-permute-start(bf16[32,6144]{1,0:T(8,128)(2,1)S(1)} %collective-permute-done.8.refs_0_), channel_id=1, source_target_pairs={{0,32},{1,97},{32,64},{33,1},{64,96},{65,33},{96,0},{97,65},{2,34}... | collective-permute-start | bytes 1179656 | tf_op jit(solution)/shard_map/ppermute | solution.py:38
  59.0 1.0 collective-permute-done.17.refs_3_
  60.0 1.3 collective-permute-start.18
  61.3 2.4 %collective-permute-start.16 = (bf16[32,6144]{1,0:T(8,128)(2,1)S(1)}, bf16[32,6144]{1,0:T(8,128)(2,1)S(1)}, u32[]{:S(2)}, u32[]{:S(2)}) collective-permute-start(bf16[32,6144]{1,0:T(8,128)(2,1)S(1)} %collective-permute-done.15.refs_1_), channel_id=1, source_target_pairs={{0,32},{1,97},{32,64},{33,1},{64,96},{65,33},{96,0},{97,65},{2,34}... | collective-permute-start | bytes 1179656 | tf_op jit(solution)/shard_map/ppermute | solution.py:38
  63.8 8.2 %expert_rows_first.1 = (bf16[64,6144]{1,0:T(8,128)(2,1)S(1)}, bf16[64,6144]{1,0:T(8,128)(2,1)S(1)}, bf16[6144,512]{1,0:T(8,128)(2,1)S(1)}, bf16[6144,512]{1,0:T(8,128)(2,1)S(1)}, bf16[512,6144]{1,0:T(8,128)(2,1)S(1)}) custom-call(bf16[32,6144]{1,0:T(8,128)(2,1)S(1)} %constant_dynamic-update-slice_fusion.refs_0_, ...), custom_call_target="tpu_custom_call" | custom-call | flops 1000000 | bytes 100000 | tf_op jit(solution)/shard_map/expert_rows_first/pallas_call | solution.py:162
  72.0 0.8 lay_rows.1
  72.9 0.6 collective-permute-start.13
  73.5 4.8 %expert_rows.4 = (bf16[64,6144]{1,0:T(8,128)(2,1)S(1)}, bf16[64,6144]{1,0:T(8,128)(2,1)S(1)}) custom-call(bf16[32,6144]{1,0:T(8,128)(2,1)S(1)} %collective-permute-done.9.refs_4_.refs_0_, bf16[32,6144]{1,0:T(8,128)(2,1)S(1)} %collective-permute-done.16.refs_1_, bf16[32,6144]{1,0:T(8,128)(2,1)S(1)} %collective-permute-done.11.refs_5_.refs_2_, ...), custom_call_target="tpu_custom_call" | custom-call | flops 1000000 | bytes 100000 | tf_op jit(solution)/shard_map/expert_rows/pallas_call | solution.py:162
  78.3 0.7 collective-permute-start.19
  79.1 0.2 select_reduce_fusion.1
  79.5 1.3 collective-permute-start.25
  80.7 4.8 %expert_rows.5 = (bf16[64,6144]{1,0:T(8,128)(2,1)S(1)}, bf16[64,6144]{1,0:T(8,128)(2,1)S(1)}) custom-call(bf16[32,6144]{1,0:T(8,128)(2,1)S(1)} %collective-permute-done.8.refs_0_, bf16[32,6144]{1,0:T(8,128)(2,1)S(1)} %collective-permute-done.15.refs_1_, bf16[32,6144]{1,0:T(8,128)(2,1)S(1)} %collective-permute-done.10.refs_2_, ...), custom_call_target="tpu_custom_call" | custom-call | flops 1000000 | bytes 100000 | tf_op jit(solution)/shard_map/expert_rows/pallas_call | solution.py:162
  85.6 4.2 %expert_rows.3 = (bf16[64,6144]{1,0:T(8,128)(2,1)S(1)}, bf16[64,6144]{1,0:T(8,128)(2,1)S(1)}) custom-call(bf16[64,6144]{1,0:T(8,128)(2,1)S(1)} %collective-permute-done.12.refs_0_, bf16[64,6144]{1,0:T(8,128)(2,1)S(1)} %collective-permute-done.13.refs_1_, bf16[6144,512]{1,0:T(8,128)(2,1)S(1)} %get-tuple-element.27.refs_2_.refs_4_, ...), custom_call_target="tpu_custom_call" | custom-call | flops 1000000 | bytes 100000 | tf_op jit(solution)/shard_map/expert_rows/pallas_call | solution.py:162
  89.8 2.7 %collective-permute-start.14 = (bf16[64,6144]{1,0:T(8,128)(2,1)S(1)}, bf16[64,6144]{1,0:T(8,128)(2,1)S(1)}, u32[]{:S(2)}, u32[]{:S(2)}) collective-permute-start(bf16[64,6144]{1,0:T(8,128)(2,1)S(1)} %get-tuple-element.30), channel_id=1, source_target_pairs={{0,32},{1,97},{32,64},{33,1},{64,96},{65,33},{96,0},{97,65},{2,34}... | collective-permute-start | bytes 2359304 | tf_op jit(solution)/shard_map/ppermute | solution.py:38
  92.5 1.1 collective-permute-start.24
  94.0 0.5 collective-permute-start.26
  94.5 11.9 %collective-permute-done.14 = bf16[64,6144]{1,0:T(8,128)(2,1)S(1)} collective-permute-done((bf16[64,6144]{1,0:T(8,128)(2,1)S(1)}, bf16[64,6144]{1,0:T(8,128)(2,1)S(1)}, u32[]{:S(2)}, u32[]{:S(2)}) %collective-permute-start.14) | collective-permute-done | bytes 786464 | tf_op jit(solution)/shard_map/ppermute | solution.py:38
  106.4 3.6 %collective-permute-done.20 = bf16[64,6144]{1,0:T(8,128)(2,1)S(1)} collective-permute-done((bf16[64,6144]{1,0:T(8,128)(2,1)S(1)}, bf16[64,6144]{1,0:T(8,128)(2,1)S(1)}, u32[]{:S(2)}, u32[]{:S(2)}) %collective-permute-start.20) | collective-permute-done | bytes 786464 | tf_op jit(solution)/shard_map/ppermute | solution.py:38
  110.0 0.3 fusion.43
  110.4 2.2 %collective-permute-start.21 = (bf16[16,6144]{1,0:T(8,128)(2,1)S(1)}, bf16[16,6144]{1,0:T(8,128)(2,1)S(1)}, u32[]{:S(2)}, u32[]{:S(2)}) collective-permute-start(bf16[16,6144]{1,0:T(8,128)(2,1)S(1)} %get-tuple-element.45), channel_id=1, source_target_pairs={{0,8},{1,25},{8,0},{9,17},{16,24},{17,9},{24,16},{25,1},{2,10},{3,... | collective-permute-start | bytes 589832 | tf_op jit(solution)/shard_map/ppermute | solution.py:47
  112.6 2.2 %collective-permute-start.23 = (bf16[16,6144]{1,0:T(8,128)(2,1)S(1)}, bf16[16,6144]{1,0:T(8,128)(2,1)S(1)}, u32[]{:S(2)}, u32[]{:S(2)}) collective-permute-start(bf16[16,6144]{1,0:T(8,128)(2,1)S(1)} %get-tuple-element.46), channel_id=1, source_target_pairs={{0,16},{8,24},{16,0},{24,8},{1,17},{9,25},{17,1},{25,9},{2,18},{10... | collective-permute-start | bytes 589832 | tf_op jit(solution)/shard_map/ppermute | solution.py:29
  114.8 0.3 fusion.44
  115.2 0.7 collective-permute-start.27
  115.8 3.5 %collective-permute-done.21 = bf16[16,6144]{1,0:T(8,128)(2,1)S(1)} collective-permute-done((bf16[16,6144]{1,0:T(8,128)(2,1)S(1)}, bf16[16,6144]{1,0:T(8,128)(2,1)S(1)}, u32[]{:S(2)}, u32[]{:S(2)}) %collective-permute-start.21) | collective-permute-done | bytes 196640 | tf_op jit(solution)/shard_map/ppermute | solution.py:47
  119.3 4.8 %collective-permute-done.22 = bf16[16,6144]{1,0:T(8,128)(2,1)S(1)} collective-permute-done((bf16[16,6144]{1,0:T(8,128)(2,1)S(1)}, bf16[16,6144]{1,0:T(8,128)(2,1)S(1)}, u32[]{:S(2)}, u32[]{:S(2)}) %collective-permute-start.22) | collective-permute-done | bytes 196640 | tf_op jit(solution)/shard_map/ppermute | solution.py:47
  124.6 21.9 %all_to_all.10 = bf16[8,32,768]{2,1,0:T(8,128)(2,1)S(1)} all-to-all(bf16[8,32,768]{2,1,0:T(8,128)(2,1)S(1)} %fusion.7), channel_id=1, replica_groups=mesh['y'=4,'z'=4,'x'=4,'c'=2] {'x','c'}, dimensions={0} | all-to-all | bytes 786432 | tf_op jit(solution)/shard_map/all_to_all | solution.py:458
  146.5 0.9 fusion
  (73 shorter events, 3.0 us)
Async XLA Ops:
  0.0 79.1 %copy-start = (bf16[6144,8]{0,1:T(8,128)(2,1)S(1)}, bf16[6144,8]{0,1:T(8,128)(2,1)}, u32[]{:S(2)}) copy-start(bf16[6144,8]{0,1:T(8,128)(2,1)} %param.23) | copy-start | bytes 294916
  0.0 8.2 %copy-start.3 = (s32[64,2]{0,1:T(2,128)S(1)}, s32[64,2]{0,1:T(2,128)}, u32[]{:S(2)}) copy-start(s32[64,2]{0,1:T(2,128)} %param.24) | copy-start | bytes 1540
  6.7 3.1 %collective-permute-start = (bf16[4,64,768]{2,1,0:T(8,128)(2,1)}, bf16[4,64,768]{2,1,0:T(8,128)(2,1)S(1)}, u32[]{:S(2)}, u32[]{:S(2)}) collective-permute-start(bf16[4,64,768]{2,1,0:T(8,128)(2,1)} %get-tuple-element.22), channel_id=1, source_target_pairs={{0,1},{1,0},{2,3},{3,2},{4,5},{5,4},{6,7},{7,6},{8,9},{9,8},{10,11... | collective-permute-start | bytes 1179656 | tf_op jit(solution)/shard_map/ppermute | solution.py:384
  8.9 17.1 %copy-start.2 = (bf16[6144]{0:T(1024)(128)(2,1)S(1)}, bf16[6144]{0:T(1024)(128)(2,1)}, u32[]{:S(2)}) copy-start(bf16[6144]{0:T(1024)(128)(2,1)} %param.22) | copy-start | bytes 36868
  10.9 5.3 %collective-permute-start.1 = (bf16[64,768]{1,0:T(8,128)(2,1)S(1)}, bf16[64,768]{1,0:T(8,128)(2,1)S(1)}, u32[]{:S(2)}, u32[]{:S(2)}) collective-permute-start(bf16[64,768]{1,0:T(8,128)(2,1)S(1)} %get-tuple-element.51), channel_id=1, source_target_pairs={{0,2},{2,4},{4,6},{6,0},{1,3},{3,5},{5,7},{7,1},{8,10},{10,12},{12... | collective-permute-start | bytes 294920 | tf_op jit(solution)/shard_map/ppermute | solution.py:29
  12.2 3.9 %collective-permute-start.3 = (bf16[64,768]{1,0:T(8,128)(2,1)S(1)}, bf16[64,768]{1,0:T(8,128)(2,1)S(1)}, u32[]{:S(2)}, u32[]{:S(2)}) collective-permute-start(bf16[64,768]{1,0:T(8,128)(2,1)S(1)} %get-tuple-element.52), channel_id=1, source_target_pairs={{0,6},{2,0},{4,2},{6,4},{1,7},{3,1},{5,3},{7,5},{8,14},{10,8},{12,... | collective-permute-start | bytes 294920 | tf_op jit(solution)/shard_map/ppermute | solution.py:29
  13.6 5.2 %collective-permute-start.2 = (bf16[64,768]{1,0:T(8,128)(2,1)S(1)}, bf16[64,768]{1,0:T(8,128)(2,1)S(1)}, u32[]{:S(2)}, u32[]{:S(2)}) collective-permute-start(bf16[64,768]{1,0:T(8,128)(2,1)S(1)} %get-tuple-element.53), channel_id=1, source_target_pairs={{0,4},{2,6},{4,0},{6,2},{1,5},{3,7},{5,1},{7,3},{8,12},{10,14},{12... | collective-permute-start | bytes 294920 | tf_op jit(solution)/shard_map/ppermute | solution.py:29
  20.8 13.3 %all-to-all-start = ((bf16[8,32,768]{2,1,0:T(8,128)(2,1)}), bf16[8,32,768]{2,1,0:T(8,128)(2,1)S(1)}, u32[]{:S(2)}, u32[]{:S(2)}) async-start(bf16[8,32,768]{2,1,0:T(8,128)(2,1)} %bitcast.6), calls=%async_computation | async-start | bytes 786432 | tf_op jit(solution)/shard_map/all_to_all | solution.py:405
  34.6 10.0 %collective-permute-start.4 = (bf16[16,6144]{1,0:T(8,128)(2,1)S(1)}, bf16[16,6144]{1,0:T(8,128)(2,1)S(1)}, u32[]{:S(2)}, u32[]{:S(2)}) collective-permute-start(bf16[16,6144]{1,0:T(8,128)(2,1)S(1)} %bitcast.53), channel_id=1, source_target_pairs={{0,8},{1,25},{8,0},{9,17},{16,24},{17,9},{24,16},{25,1},{2,10},{3,... | collective-permute-start | bytes 589832 | tf_op jit(solution)/shard_map/ppermute | solution.py:47
  38.5 5.9 %collective-permute-start.6 = (bf16[16,6144]{1,0:T(8,128)(2,1)S(1)}, bf16[16,6144]{1,0:T(8,128)(2,1)S(1)}, u32[]{:S(2)}, u32[]{:S(2)}) collective-permute-start(bf16[16,6144]{1,0:T(8,128)(2,1)S(1)} %bitcast.55), channel_id=1, source_target_pairs={{0,32},{1,97},{32,0},{33,65},{64,96},{65,33},{96,64},{97,1},{2,34}... | collective-permute-start | bytes 589832 | tf_op jit(solution)/shard_map/ppermute | solution.py:47
  44.4 7.0 %collective-permute-start.7 = (bf16[32,6144]{1,0:T(8,128)(2,1)S(1)}, bf16[32,6144]{1,0:T(8,128)(2,1)S(1)}, u32[]{:S(2)}, u32[]{:S(2)}) collective-permute-start(bf16[32,6144]{1,0:T(8,128)(2,1)S(1)} %constant_dynamic-update-slice_fusion.2.refs_2_), channel_id=1, source_target_pairs={{0,96},{1,33},{32,64},{33,1},{64,32},{65,97},{96,0},{97,65},{2,98}... | collective-permute-start | bytes 1179656 | tf_op jit(solution)/shard_map/ppermute | solution.py:47
  44.6 7.0 %collective-permute-start.5 = (bf16[32,6144]{1,0:T(8,128)(2,1)S(1)}, bf16[32,6144]{1,0:T(8,128)(2,1)S(1)}, u32[]{:S(2)}, u32[]{:S(2)}) collective-permute-start(bf16[32,6144]{1,0:T(8,128)(2,1)S(1)} %constant_dynamic-update-slice_fusion.refs_0_), channel_id=1, source_target_pairs={{0,24},{1,9},{8,16},{9,1},{16,8},{17,25},{24,0},{25,17},{2,26},{3,... | collective-permute-start | bytes 1179656 | tf_op jit(solution)/shard_map/ppermute | solution.py:47
  44.7 11.1 %collective-permute-start.10 = (bf16[32,6144]{1,0:T(8,128)(2,1)S(1)}, bf16[32,6144]{1,0:T(8,128)(2,1)S(1)}, u32[]{:S(2)}, u32[]{:S(2)}) collective-permute-start(bf16[32,6144]{1,0:T(8,128)(2,1)S(1)} %constant_dynamic-update-slice_fusion.2.refs_2_), channel_id=1, source_target_pairs={{0,8},{1,25},{8,16},{9,1},{16,24},{17,9},{24,0},{25,17},{2,10},{3,... | collective-permute-start | bytes 1179656 | tf_op jit(solution)/shard_map/ppermute | solution.py:38
  45.1 10.8 %collective-permute-start.8 = (bf16[32,6144]{1,0:T(8,128)(2,1)S(1)}, bf16[32,6144]{1,0:T(8,128)(2,1)S(1)}, u32[]{:S(2)}, u32[]{:S(2)}) collective-permute-start(bf16[32,6144]{1,0:T(8,128)(2,1)S(1)} %constant_dynamic-update-slice_fusion.refs_0_), channel_id=1, source_target_pairs={{0,32},{1,97},{32,64},{33,1},{64,96},{65,33},{96,0},{97,65},{2,34}... | collective-permute-start | bytes 1179656 | tf_op jit(solution)/shard_map/ppermute | solution.py:38
  51.4 8.6 %collective-permute-start.17 = (bf16[32,6144]{1,0:T(8,128)(2,1)S(1)}, bf16[32,6144]{1,0:T(8,128)(2,1)S(1)}, u32[]{:S(2)}, u32[]{:S(2)}) collective-permute-start(bf16[32,6144]{1,0:T(8,128)(2,1)S(1)} %collective-permute-done.7.refs_3_), channel_id=1, source_target_pairs={{0,8},{1,25},{8,16},{9,1},{16,24},{17,9},{24,0},{25,17},{2,10},{3,... | collective-permute-start | bytes 1179656 | tf_op jit(solution)/shard_map/ppermute | solution.py:38
  51.6 9.8 %collective-permute-start.15 = (bf16[32,6144]{1,0:T(8,128)(2,1)S(1)}, bf16[32,6144]{1,0:T(8,128)(2,1)S(1)}, u32[]{:S(2)}, u32[]{:S(2)}) collective-permute-start(bf16[32,6144]{1,0:T(8,128)(2,1)S(1)} %collective-permute-done.5.refs_1_), channel_id=1, source_target_pairs={{0,32},{1,97},{32,64},{33,1},{64,96},{65,33},{96,0},{97,65},{2,34}... | collective-permute-start | bytes 1179656 | tf_op jit(solution)/shard_map/ppermute | solution.py:38
  55.8 16.2 %collective-permute-start.11 = (bf16[32,6144]{1,0:T(8,128)(2,1)S(1)}, bf16[32,6144]{1,0:T(8,128)(2,1)S(1)}, u32[]{:S(2)}, u32[]{:S(2)}) collective-permute-start(bf16[32,6144]{1,0:T(8,128)(2,1)S(1)} %collective-permute-done.10.refs_2_), channel_id=1, source_target_pairs={{0,8},{1,25},{8,16},{9,1},{16,24},{17,9},{24,0},{25,17},{2,10},{3,... | collective-permute-start | bytes 1179656 | tf_op jit(solution)/shard_map/ppermute | solution.py:38
  55.8 16.2 %collective-permute-start.9 = (bf16[32,6144]{1,0:T(8,128)(2,1)S(1)}, bf16[32,6144]{1,0:T(8,128)(2,1)S(1)}, u32[]{:S(2)}, u32[]{:S(2)}) collective-permute-start(bf16[32,6144]{1,0:T(8,128)(2,1)S(1)} %collective-permute-done.8.refs_0_), channel_id=1, source_target_pairs={{0,32},{1,97},{32,64},{33,1},{64,96},{65,33},{96,0},{97,65},{2,34}... | collective-permute-start | bytes 1179656 | tf_op jit(solution)/shard_map/ppermute | solution.py:38
  60.0 13.5 %collective-permute-start.18 = (bf16[32,6144]{1,0:T(8,128)(2,1)S(1)}, bf16[32,6144]{1,0:T(8,128)(2,1)S(1)}, u32[]{:S(2)}, u32[]{:S(2)}) collective-permute-start(bf16[32,6144]{1,0:T(8,128)(2,1)S(1)} %collective-permute-done.17.refs_3_), channel_id=1, source_target_pairs={{0,8},{1,25},{8,16},{9,1},{16,24},{17,9},{24,0},{25,17},{2,10},{3,... | collective-permute-start | bytes 1179656 | tf_op jit(solution)/shard_map/ppermute | solution.py:38
  61.3 12.2 %collective-permute-start.16 = (bf16[32,6144]{1,0:T(8,128)(2,1)S(1)}, bf16[32,6144]{1,0:T(8,128)(2,1)S(1)}, u32[]{:S(2)}, u32[]{:S(2)}) collective-permute-start(bf16[32,6144]{1,0:T(8,128)(2,1)S(1)} %collective-permute-done.15.refs_1_), channel_id=1, source_target_pairs={{0,32},{1,97},{32,64},{33,1},{64,96},{65,33},{96,0},{97,65},{2,34}... | collective-permute-start | bytes 1179656 | tf_op jit(solution)/shard_map/ppermute | solution.py:38
  72.8 12.8 %collective-permute-start.12 = (bf16[64,6144]{1,0:T(8,128)(2,1)S(1)}, bf16[64,6144]{1,0:T(8,128)(2,1)S(1)}, u32[]{:S(2)}, u32[]{:S(2)}) collective-permute-start(bf16[64,6144]{1,0:T(8,128)(2,1)S(1)} %get-tuple-element.25), channel_id=1, source_target_pairs={{0,96},{1,33},{32,0},{33,65},{64,32},{65,97},{96,64},{97,1},{2,98}... | collective-permute-start | bytes 2359304 | tf_op jit(solution)/shard_map/ppermute | solution.py:38
  72.9 12.7 %collective-permute-start.13 = (bf16[64,6144]{1,0:T(8,128)(2,1)S(1)}, bf16[64,6144]{1,0:T(8,128)(2,1)S(1)}, u32[]{:S(2)}, u32[]{:S(2)}) collective-permute-start(bf16[64,6144]{1,0:T(8,128)(2,1)S(1)} %get-tuple-element.26), channel_id=1, source_target_pairs={{0,24},{1,9},{8,0},{9,17},{16,8},{17,25},{24,16},{25,1},{2,26},{3,... | collective-permute-start | bytes 2359304 | tf_op jit(solution)/shard_map/ppermute | solution.py:38
  78.3 15.2 %collective-permute-start.19 = (bf16[64,6144]{1,0:T(8,128)(2,1)S(1)}, bf16[64,6144]{1,0:T(8,128)(2,1)S(1)}, u32[]{:S(2)}, u32[]{:S(2)}) collective-permute-start(bf16[64,6144]{1,0:T(8,128)(2,1)S(1)} %get-tuple-element.31.refs_7_), channel_id=1, source_target_pairs={{0,96},{1,33},{32,0},{33,65},{64,32},{65,97},{96,64},{97,1},{2,98}... | collective-permute-start | bytes 2359304 | tf_op jit(solution)/shard_map/ppermute | solution.py:38
  79.5 14.4 %collective-permute-start.25 = (bf16[64,6144]{1,0:T(8,128)(2,1)S(1)}, bf16[64,6144]{1,0:T(8,128)(2,1)S(1)}, u32[]{:S(2)}, u32[]{:S(2)}) collective-permute-start(bf16[64,6144]{1,0:T(8,128)(2,1)S(1)} %get-tuple-element.32.refs_8_), channel_id=1, source_target_pairs={{0,24},{1,9},{8,0},{9,17},{16,8},{17,25},{24,16},{25,1},{2,26},{3,... | collective-permute-start | bytes 2359304 | tf_op jit(solution)/shard_map/ppermute | solution.py:38
  89.8 16.6 %collective-permute-start.14 = (bf16[64,6144]{1,0:T(8,128)(2,1)S(1)}, bf16[64,6144]{1,0:T(8,128)(2,1)S(1)}, u32[]{:S(2)}, u32[]{:S(2)}) collective-permute-start(bf16[64,6144]{1,0:T(8,128)(2,1)S(1)} %get-tuple-element.30), channel_id=1, source_target_pairs={{0,32},{1,97},{32,64},{33,1},{64,96},{65,33},{96,0},{97,65},{2,34}... | collective-permute-start | bytes 2359304 | tf_op jit(solution)/shard_map/ppermute | solution.py:38
  92.5 22.3 %collective-permute-start.24 = (bf16[64,6144]{1,0:T(8,128)(2,1)S(1)}, bf16[64,6144]{1,0:T(8,128)(2,1)S(1)}, u32[]{:S(2)}, u32[]{:S(2)}) collective-permute-start(bf16[64,6144]{1,0:T(8,128)(2,1)S(1)} %get-tuple-element.35), channel_id=1, source_target_pairs={{0,8},{1,25},{8,16},{9,1},{16,24},{17,9},{24,0},{25,17},{2,10},{3,... | collective-permute-start | bytes 2359304 | tf_op jit(solution)/shard_map/ppermute | solution.py:38
  93.7 16.3 %collective-permute-start.20 = (bf16[64,6144]{1,0:T(8,128)(2,1)S(1)}, bf16[64,6144]{1,0:T(8,128)(2,1)S(1)}, u32[]{:S(2)}, u32[]{:S(2)}) collective-permute-start(bf16[64,6144]{1,0:T(8,128)(2,1)S(1)} %add_convert_fusion.1), channel_id=1, source_target_pairs={{0,96},{1,33},{32,0},{33,65},{64,32},{65,97},{96,64},{97,1},{2,98}... | collective-permute-start | bytes 2359304 | tf_op jit(solution)/shard_map/ppermute | solution.py:38
  94.0 20.8 %collective-permute-start.26 = (bf16[64,6144]{1,0:T(8,128)(2,1)S(1)}, bf16[64,6144]{1,0:T(8,128)(2,1)S(1)}, u32[]{:S(2)}, u32[]{:S(2)}) collective-permute-start(bf16[64,6144]{1,0:T(8,128)(2,1)S(1)} %add_convert_fusion), channel_id=1, source_target_pairs={{0,24},{1,9},{8,0},{9,17},{16,8},{17,25},{24,16},{25,1},{2,26},{3,... | collective-permute-start | bytes 2359304 | tf_op jit(solution)/shard_map/ppermute | solution.py:38
  110.4 9.0 %collective-permute-start.21 = (bf16[16,6144]{1,0:T(8,128)(2,1)S(1)}, bf16[16,6144]{1,0:T(8,128)(2,1)S(1)}, u32[]{:S(2)}, u32[]{:S(2)}) collective-permute-start(bf16[16,6144]{1,0:T(8,128)(2,1)S(1)} %get-tuple-element.45), channel_id=1, source_target_pairs={{0,8},{1,25},{8,0},{9,17},{16,24},{17,9},{24,16},{25,1},{2,10},{3,... | collective-permute-start | bytes 589832 | tf_op jit(solution)/shard_map/ppermute | solution.py:47
  112.6 6.8 %collective-permute-start.23 = (bf16[16,6144]{1,0:T(8,128)(2,1)S(1)}, bf16[16,6144]{1,0:T(8,128)(2,1)S(1)}, u32[]{:S(2)}, u32[]{:S(2)}) collective-permute-start(bf16[16,6144]{1,0:T(8,128)(2,1)S(1)} %get-tuple-element.46), channel_id=1, source_target_pairs={{0,16},{8,24},{16,0},{24,8},{1,17},{9,25},{17,1},{25,9},{2,18},{10... | collective-permute-start | bytes 589832 | tf_op jit(solution)/shard_map/ppermute | solution.py:29
  114.8 9.3 %collective-permute-start.22 = (bf16[16,6144]{1,0:T(8,128)(2,1)S(1)}, bf16[16,6144]{1,0:T(8,128)(2,1)S(1)}, u32[]{:S(2)}, u32[]{:S(2)}) collective-permute-start(bf16[16,6144]{1,0:T(8,128)(2,1)S(1)} %get-tuple-element.47), channel_id=1, source_target_pairs={{0,24},{1,9},{8,16},{9,1},{16,8},{17,25},{24,0},{25,17},{2,26},{3,... | collective-permute-start | bytes 589832 | tf_op jit(solution)/shard_map/ppermute | solution.py:47
  115.2 9.1 %collective-permute-start.27 = (bf16[16,6144]{1,0:T(8,128)(2,1)S(1)}, bf16[16,6144]{1,0:T(8,128)(2,1)S(1)}, u32[]{:S(2)}, u32[]{:S(2)}) collective-permute-start(bf16[16,6144]{1,0:T(8,128)(2,1)S(1)} %get-tuple-element.48), channel_id=1, source_target_pairs={{0,32},{1,97},{32,0},{33,65},{64,96},{65,33},{96,64},{97,1},{2,34}... | collective-permute-start | bytes 589832 | tf_op jit(solution)/shard_map/ppermute | solution.py:47
  115.8 8.4 %collective-permute-start.29 = (bf16[16,6144]{1,0:T(8,128)(2,1)S(1)}, bf16[16,6144]{1,0:T(8,128)(2,1)S(1)}, u32[]{:S(2)}, u32[]{:S(2)}) collective-permute-start(bf16[16,6144]{1,0:T(8,128)(2,1)S(1)} %get-tuple-element.49), channel_id=1, source_target_pairs={{0,64},{32,96},{64,0},{96,32},{1,65},{33,97},{65,1},{97,33},{2,66}... | collective-permute-start | bytes 589832 | tf_op jit(solution)/shard_map/ppermute | solution.py:29
  119.3 4.9 %collective-permute-start.28 = (bf16[16,6144]{1,0:T(8,128)(2,1)S(1)}, bf16[16,6144]{1,0:T(8,128)(2,1)S(1)}, u32[]{:S(2)}, u32[]{:S(2)}) collective-permute-start(bf16[16,6144]{1,0:T(8,128)(2,1)S(1)} %get-tuple-element.50), channel_id=1, source_target_pairs={{0,96},{1,33},{32,64},{33,1},{64,32},{65,97},{96,0},{97,65},{2,98}... | collective-permute-start | bytes 589832 | tf_op jit(solution)/shard_map/ppermute | solution.py:47
  124.4 23.0 %copy-start.1 = (bf16[6144,8]{0,1:T(8,128)(2,1)S(1)}, bf16[6144,8]{0,1:T(8,128)(2,1)}, u32[]{:S(2)}) copy-start(bf16[6144,8]{0,1:T(8,128)(2,1)} %param.23) | copy-start | bytes 294916

commit v7 on v6

--- a/solution.py
+++ b/solution.py
@@ -66,12 +66,19 @@
     arrivals = []
     place = 0
     for index, (source, count) in enumerate(zip(sources, taken)):
-        arrivals.append(
-            pltpu.make_async_copy(source, rows.at[pl.ds(place, count)], in_sems.at[index])
-        )
+        for k in range(DEEP):
+            part = pl.ds(k * deep, deep)
+            arrivals.append(
+                pltpu.make_async_copy(
+                    source.at[:, part],
+                    rows.at[pl.ds(place, count), part],
+                    in_sems.at[index * DEEP + k],
+                )
+            )
         place += count
-    for copy in arrivals:
-        copy.start()
+    for k in range(DEEP):
+        for copy in arrivals[k::DEEP]:
+            copy.start()
     groups = [()] * (DEEP + WIDE)
     if not kept:
         groups = []
@@ -99,10 +106,10 @@
                 copy.start()
         weights = near
     w_gate, w_up, w_down = weights
-    for copy in arrivals:
-        copy.wait()
 
     for k in range(DEEP):
+        for copy in arrivals[k::DEEP]:
+            copy.wait()
         for copy in groups[k]:
             copy.wait()
         part = pl.ds(k * deep, deep)
@@ -150,7 +157,7 @@
         pltpu.VMEM((total, hidden), jnp.float32),
         pltpu.VMEM((total, hidden), jnp.float32),
         pltpu.VMEM((total, width), jnp.bfloat16),
-        pltpu.SemaphoreType.DMA((len(taken),)),
+        pltpu.SemaphoreType.DMA((len(taken) * DEEP,)),
         pltpu.SemaphoreType.DMA((len(given) * WIDE,)),
     ]
     if kept:

time: 148 us -> 146 us (0.986)
  blocking collectives: 21.9 us -> 19.6 us
  Pallas kernels: 29.5 us -> 31.2 us
    all_to_all x1, blocking collectives: 21.9 us -> 19.6 us  [body(): back = lax.all_to_all(weighted, EXPERT_AXES, 0, 0, tiled=True)]
    ppermute x8, waiting for transfers between devices: 15.4 us -> 13.7 us  [swap(): return lax.ppermute(value, (axis, 'c'), perm)]
    ppermute x8, starting transfers between devices: 9.81 us -> 11.5 us  [swap(): return lax.ppermute(value, (axis, 'c'), perm)]
    ppermute x5, starting transfers between devices: 6.6 us -> 4.92 us  [shift(): lax.ppermute(value, axis, [(i, (i + step) % SIDE) for i in range(SIDE)])]
    pallas_call x4, Pallas kernels: 22 us -> 23.7 us  [expert_call(): pl.pallas_call(functools.partial(expert_kernel, taken, given, kept, len(a...]
  transfers between devices with their start and end apart: 31 -> 31, of which waited for: 13 -> 15; matrix products, arithmetic and copies ran while one was open for 2% -> 2% of each run, Pallas kernels for 15% -> 17%
where the time goes in v7:
time: 146 us
  waiting for transfers between devices  44.4 us (30%)
  starting transfers between devices  43.3 us (30%)
  Pallas kernels  31.2 us (21%)
  blocking collectives  19.6 us (13%)
  other arithmetic  4.14 us (3%)
  matrix products  2.24 us (2%)
    pallas_call x4, Pallas kernels, expert_call(): pl.pallas_call(functools.partial(expert_kernel, taken, given, kept, len(a...  23.7 us
    ppermute x16, starting transfers between devices, ring(): return lax.ppermute(value, (axis, 'c'), perm)  20.1 us
    all_to_all x1, blocking collectives, body(): back = lax.all_to_all(weighted, EXPERT_AXES, 0, 0, tiled=True)  19.6 us
    ppermute x16, waiting for transfers between devices, ring(): return lax.ppermute(value, (axis, 'c'), perm)  17.4 us
    ppermute x8, waiting for transfers between devices, swap(): return lax.ppermute(value, (axis, 'c'), perm)  13.7 us
    ppermute x8, starting transfers between devices, swap(): return lax.ppermute(value, (axis, 'c'), perm)  11.5 us
    all_to_all x1, waiting for transfers between devices, body(): lax.all_to_all(sent, EXPERT_AXES, 0, 0, tiled=True).astype(jnp.float32)  8.06 us
    pallas_call x1, Pallas kernels, attend(): pl.pallas_call(attend_kernel, out_shape=(shape, shape), in_specs=[anywher...  6.72 us
  transfers between devices with their start and end apart: 31, of which 15 were waited for; matrix products, arithmetic and copies ran while one was open for 2% of the time, Pallas kernels for 17%

profile of v7, /device:TPU:1, one launch (start us, length us, event | category | flops | bytes accessed | tf_op | source)
XLA Modules:
  0.0 146.0 jit_solution(15882373626528436796)
XLA Ops:
  0.0 6.7 %attend_rows.1 = (bf16[4,64,768]{2,1,0:T(8,128)(2,1)}, bf16[4,64,768]{2,1,0:T(8,128)(2,1)}) custom-call(s32[64]{0:T(128)} %lengths.1, bf16[64,384]{1,0:T(8,128)(2,1)} %queries.1, bf16[64,128]{1,0:T(8,128)(2,1)} %new_keys.1, bf16[64,128]{1,0:T(8,128)(2,1)} %new_values.1, bf16[64,256,128]{2,1,0:T(8,128)(2,1)} %cache_k.1, bf16[64,256,128]{2,1,0:T(8,128)(2,1)} %cache_v.1, ...), custom_call_target="tpu_custom_call" | custom-call | flops 301989888 | bytes 8388608 | tf_op jit(solution)/shard_map/attend_rows/pallas_call | solution.py:329
  6.7 1.5 %collective-permute-start = (bf16[4,64,768]{2,1,0:T(8,128)(2,1)}, bf16[4,64,768]{2,1,0:T(8,128)(2,1)S(1)}, u32[]{:S(2)}, u32[]{:S(2)}) collective-permute-start(bf16[4,64,768]{2,1,0:T(8,128)(2,1)} %get-tuple-element.22), channel_id=1, source_target_pairs={{0,1},{1,0},{2,3},{3,2},{4,5},{5,4},{6,7},{7,6},{8,9},{9,8},{10,11... | collective-permute-start | bytes 1179656 | tf_op jit(solution)/shard_map/ppermute | solution.py:391
  9.1 0.7 collective-permute-done
  9.8 1.1 fusion.21
  10.9 1.4 collective-permute-start.1
  12.2 1.4 collective-permute-start.3
  13.6 1.6 %collective-permute-start.2 = (bf16[64,768]{1,0:T(8,128)(2,1)S(1)}, bf16[64,768]{1,0:T(8,128)(2,1)S(1)}, u32[]{:S(2)}, u32[]{:S(2)}) collective-permute-start(bf16[64,768]{1,0:T(8,128)(2,1)S(1)} %get-tuple-element.53), channel_id=1, source_target_pairs={{0,4},{2,6},{4,0},{6,2},{1,5},{3,7},{5,1},{7,3},{8,12},{10,14},{12... | collective-permute-start | bytes 294920 | tf_op jit(solution)/shard_map/ppermute | solution.py:29
  15.2 0.9 collective-permute-done.1
  16.2 2.6 %collective-permute-done.2 = bf16[64,768]{1,0:T(8,128)(2,1)S(1)} collective-permute-done((bf16[64,768]{1,0:T(8,128)(2,1)S(1)}, bf16[64,768]{1,0:T(8,128)(2,1)S(1)}, u32[]{:S(2)}, u32[]{:S(2)}) %collective-permute-start.2) | collective-permute-done | bytes 98336 | tf_op jit(solution)/shard_map/ppermute | solution.py:29
  18.8 1.0 fusion.14
  19.8 1.0 convolution_convert_fusion
  20.8 5.2 %all-to-all-start = ((bf16[8,32,768]{2,1,0:T(8,128)(2,1)}), bf16[8,32,768]{2,1,0:T(8,128)(2,1)S(1)}, u32[]{:S(2)}, u32[]{:S(2)}) async-start(bf16[8,32,768]{2,1,0:T(8,128)(2,1)} %bitcast.6), calls=%async_computation | async-start | bytes 786432 | tf_op jit(solution)/shard_map/all_to_all | solution.py:412
  26.1 8.1 %all-to-all-done = bf16[8,32,768]{2,1,0:T(8,128)(2,1)S(1)} async-done(((bf16[8,32,768]{2,1,0:T(8,128)(2,1)}), bf16[8,32,768]{2,1,0:T(8,128)(2,1)S(1)}, u32[]{:S(2)}, u32[]{:S(2)}) %all-to-all-start) | async-done | bytes 393248 | tf_op jit(solution)/shard_map/all_to_all | solution.py:412
  34.6 3.9 %collective-permute-start.4 = (bf16[16,6144]{1,0:T(8,128)(2,1)S(1)}, bf16[16,6144]{1,0:T(8,128)(2,1)S(1)}, u32[]{:S(2)}, u32[]{:S(2)}) collective-permute-start(bf16[16,6144]{1,0:T(8,128)(2,1)S(1)} %bitcast.53), channel_id=1, source_target_pairs={{0,8},{1,25},{8,0},{9,17},{16,24},{17,9},{24,16},{25,1},{2,10},{3,... | collective-permute-start | bytes 589832 | tf_op jit(solution)/shard_map/ppermute | solution.py:47
  38.5 2.8 %collective-permute-start.6 = (bf16[16,6144]{1,0:T(8,128)(2,1)S(1)}, bf16[16,6144]{1,0:T(8,128)(2,1)S(1)}, u32[]{:S(2)}, u32[]{:S(2)}) collective-permute-start(bf16[16,6144]{1,0:T(8,128)(2,1)S(1)} %bitcast.55), channel_id=1, source_target_pairs={{0,32},{1,97},{32,0},{33,65},{64,96},{65,33},{96,64},{97,1},{2,34}... | collective-permute-start | bytes 589832 | tf_op jit(solution)/shard_map/ppermute | solution.py:47
  41.4 3.0 %collective-permute-done.6 = bf16[16,6144]{1,0:T(8,128)(2,1)S(1)} collective-permute-done((bf16[16,6144]{1,0:T(8,128)(2,1)S(1)}, bf16[16,6144]{1,0:T(8,128)(2,1)S(1)}, u32[]{:S(2)}, u32[]{:S(2)}) %collective-permute-start.6) | collective-permute-done | bytes 196640 | tf_op jit(solution)/shard_map/ppermute | solution.py:47
  44.7 0.4 collective-permute-start.10
  45.1 2.4 %collective-permute-start.8 = (bf16[32,6144]{1,0:T(8,128)(2,1)S(1)}, bf16[32,6144]{1,0:T(8,128)(2,1)S(1)}, u32[]{:S(2)}, u32[]{:S(2)}) collective-permute-start(bf16[32,6144]{1,0:T(8,128)(2,1)S(1)} %constant_dynamic-update-slice_fusion.refs_0_), channel_id=1, source_target_pairs={{0,32},{1,97},{32,64},{33,1},{64,96},{65,33},{96,0},{97,65},{2,34}... | collective-permute-start | bytes 1179656 | tf_op jit(solution)/shard_map/ppermute | solution.py:38
  47.5 4.0 %collective-permute-done.7.refs_3_ = bf16[32,6144]{1,0:T(8,128)(2,1)S(1)} collective-permute-done((bf16[32,6144]{1,0:T(8,128)(2,1)S(1)}, bf16[32,6144]{1,0:T(8,128)(2,1)S(1)}, u32[]{:S(2)}, u32[]{:S(2)}) %collective-permute-start.7) | collective-permute-done | bytes 393248 | tf_op jit(solution)/shard_map/ppermute | solution.py:47
  51.6 3.4 %collective-permute-start.15 = (bf16[32,6144]{1,0:T(8,128)(2,1)S(1)}, bf16[32,6144]{1,0:T(8,128)(2,1)S(1)}, u32[]{:S(2)}, u32[]{:S(2)}) collective-permute-start(bf16[32,6144]{1,0:T(8,128)(2,1)S(1)} %collective-permute-done.5.refs_1_), channel_id=1, source_target_pairs={{0,32},{1,97},{32,64},{33,1},{64,96},{65,33},{96,0},{97,65},{2,34}... | collective-permute-start | bytes 1179656 | tf_op jit(solution)/shard_map/ppermute | solution.py:38
  54.9 0.8 collective-permute-done.10.refs_2_
  55.8 3.1 %collective-permute-start.9 = (bf16[32,6144]{1,0:T(8,128)(2,1)S(1)}, bf16[32,6144]{1,0:T(8,128)(2,1)S(1)}, u32[]{:S(2)}, u32[]{:S(2)}) collective-permute-start(bf16[32,6144]{1,0:T(8,128)(2,1)S(1)} %collective-permute-done.8.refs_0_), channel_id=1, source_target_pairs={{0,32},{1,97},{32,64},{33,1},{64,96},{65,33},{96,0},{97,65},{2,34}... | collective-permute-start | bytes 1179656 | tf_op jit(solution)/shard_map/ppermute | solution.py:38
  59.0 1.0 collective-permute-done.17.refs_3_
  60.0 1.3 collective-permute-start.18
  61.3 2.4 %collective-permute-start.16 = (bf16[32,6144]{1,0:T(8,128)(2,1)S(1)}, bf16[32,6144]{1,0:T(8,128)(2,1)S(1)}, u32[]{:S(2)}, u32[]{:S(2)}) collective-permute-start(bf16[32,6144]{1,0:T(8,128)(2,1)S(1)} %collective-permute-done.15.refs_1_), channel_id=1, source_target_pairs={{0,32},{1,97},{32,64},{33,1},{64,96},{65,33},{96,0},{97,65},{2,34}... | collective-permute-start | bytes 1179656 | tf_op jit(solution)/shard_map/ppermute | solution.py:38
  63.8 8.2 %expert_rows_first.1 = (bf16[64,6144]{1,0:T(8,128)(2,1)S(1)}, bf16[64,6144]{1,0:T(8,128)(2,1)S(1)}, bf16[6144,512]{1,0:T(8,128)(2,1)S(1)}, bf16[6144,512]{1,0:T(8,128)(2,1)S(1)}, bf16[512,6144]{1,0:T(8,128)(2,1)S(1)}) custom-call(bf16[32,6144]{1,0:T(8,128)(2,1)S(1)} %constant_dynamic-update-slice_fusion.refs_0_, ...), custom_call_target="tpu_custom_call" | custom-call | flops 1000000 | bytes 100000 | tf_op jit(solution)/shard_map/expert_rows_first/pallas_call | solution.py:169
  72.0 0.8 lay_rows.1
  72.9 0.6 collective-permute-start.13
  73.5 5.3 %expert_rows.4 = (bf16[64,6144]{1,0:T(8,128)(2,1)S(1)}, bf16[64,6144]{1,0:T(8,128)(2,1)S(1)}) custom-call(bf16[32,6144]{1,0:T(8,128)(2,1)S(1)} %collective-permute-done.9.refs_4_.refs_0_, bf16[32,6144]{1,0:T(8,128)(2,1)S(1)} %collective-permute-done.16.refs_1_, bf16[32,6144]{1,0:T(8,128)(2,1)S(1)} %collective-permute-done.11.refs_5_.refs_2_, ...), custom_call_target="tpu_custom_call" | custom-call | flops 1000000 | bytes 100000 | tf_op jit(solution)/shard_map/expert_rows/pallas_call | solution.py:169
  78.8 0.7 collective-permute-start.19
  80.0 1.3 collective-permute-start.25
  81.3 5.3 %expert_rows.5 = (bf16[64,6144]{1,0:T(8,128)(2,1)S(1)}, bf16[64,6144]{1,0:T(8,128)(2,1)S(1)}) custom-call(bf16[32,6144]{1,0:T(8,128)(2,1)S(1)} %collective-permute-done.8.refs_0_, bf16[32,6144]{1,0:T(8,128)(2,1)S(1)} %collective-permute-done.15.refs_1_, bf16[32,6144]{1,0:T(8,128)(2,1)S(1)} %collective-permute-done.10.refs_2_, ...), custom_call_target="tpu_custom_call" | custom-call | flops 1000000 | bytes 100000 | tf_op jit(solution)/shard_map/expert_rows/pallas_call | solution.py:169
  86.6 4.9 %expert_rows.3 = (bf16[64,6144]{1,0:T(8,128)(2,1)S(1)}, bf16[64,6144]{1,0:T(8,128)(2,1)S(1)}) custom-call(bf16[64,6144]{1,0:T(8,128)(2,1)S(1)} %collective-permute-done.12.refs_0_, bf16[64,6144]{1,0:T(8,128)(2,1)S(1)} %collective-permute-done.13.refs_1_, bf16[6144,512]{1,0:T(8,128)(2,1)S(1)} %get-tuple-element.27.refs_2_.refs_4_, ...), custom_call_target="tpu_custom_call" | custom-call | flops 1000000 | bytes 100000 | tf_op jit(solution)/shard_map/expert_rows/pallas_call | solution.py:169
  91.5 2.7 %collective-permute-start.14 = (bf16[64,6144]{1,0:T(8,128)(2,1)S(1)}, bf16[64,6144]{1,0:T(8,128)(2,1)S(1)}, u32[]{:S(2)}, u32[]{:S(2)}) collective-permute-start(bf16[64,6144]{1,0:T(8,128)(2,1)S(1)} %get-tuple-element.30), channel_id=1, source_target_pairs={{0,32},{1,97},{32,64},{33,1},{64,96},{65,33},{96,0},{97,65},{2,34}... | collective-permute-start | bytes 2359304 | tf_op jit(solution)/shard_map/ppermute | solution.py:38
  94.1 1.0 collective-permute-start.24
  95.7 0.5 collective-permute-start.26
  96.2 11.1 %collective-permute-done.14 = bf16[64,6144]{1,0:T(8,128)(2,1)S(1)} collective-permute-done((bf16[64,6144]{1,0:T(8,128)(2,1)S(1)}, bf16[64,6144]{1,0:T(8,128)(2,1)S(1)}, u32[]{:S(2)}, u32[]{:S(2)}) %collective-permute-start.14) | collective-permute-done | bytes 786464 | tf_op jit(solution)/shard_map/ppermute | solution.py:38
  107.3 4.4 %collective-permute-done.20 = bf16[64,6144]{1,0:T(8,128)(2,1)S(1)} collective-permute-done((bf16[64,6144]{1,0:T(8,128)(2,1)S(1)}, bf16[64,6144]{1,0:T(8,128)(2,1)S(1)}, u32[]{:S(2)}, u32[]{:S(2)}) %collective-permute-start.20) | collective-permute-done | bytes 786464 | tf_op jit(solution)/shard_map/ppermute | solution.py:38
  112.0 1.2 collective-permute-start.21
  113.2 0.6 collective-permute-start.23
  113.8 1.6 %collective-permute-start.22 = (bf16[16,6144]{1,0:T(8,128)(2,1)S(1)}, bf16[16,6144]{1,0:T(8,128)(2,1)S(1)}, u32[]{:S(2)}, u32[]{:S(2)}) collective-permute-start(bf16[16,6144]{1,0:T(8,128)(2,1)S(1)} %get-tuple-element.47), channel_id=1, source_target_pairs={{0,24},{1,9},{8,16},{9,1},{16,8},{17,25},{24,0},{25,17},{2,26},{3,... | collective-permute-start | bytes 589832 | tf_op jit(solution)/shard_map/ppermute | solution.py:47
  115.7 1.8 %collective-permute-start.27 = (bf16[16,6144]{1,0:T(8,128)(2,1)S(1)}, bf16[16,6144]{1,0:T(8,128)(2,1)S(1)}, u32[]{:S(2)}, u32[]{:S(2)}) collective-permute-start(bf16[16,6144]{1,0:T(8,128)(2,1)S(1)} %get-tuple-element.48), channel_id=1, source_target_pairs={{0,32},{1,97},{32,0},{33,65},{64,96},{65,33},{96,64},{97,1},{2,34}... | collective-permute-start | bytes 589832 | tf_op jit(solution)/shard_map/ppermute | solution.py:47
  117.5 2.9 %collective-permute-done.21 = bf16[16,6144]{1,0:T(8,128)(2,1)S(1)} collective-permute-done((bf16[16,6144]{1,0:T(8,128)(2,1)S(1)}, bf16[16,6144]{1,0:T(8,128)(2,1)S(1)}, u32[]{:S(2)}, u32[]{:S(2)}) %collective-permute-start.21) | collective-permute-done | bytes 196640 | tf_op jit(solution)/shard_map/ppermute | solution.py:47
  120.4 2.3 %collective-permute-done.22 = bf16[16,6144]{1,0:T(8,128)(2,1)S(1)} collective-permute-done((bf16[16,6144]{1,0:T(8,128)(2,1)S(1)}, bf16[16,6144]{1,0:T(8,128)(2,1)S(1)}, u32[]{:S(2)}, u32[]{:S(2)}) %collective-permute-start.22) | collective-permute-done | bytes 196640 | tf_op jit(solution)/shard_map/ppermute | solution.py:47
  122.8 1.1 collective-permute-done.29
  123.9 1.4 collective-permute-done.28
  125.6 19.6 %all_to_all.10 = bf16[8,32,768]{2,1,0:T(8,128)(2,1)S(1)} all-to-all(bf16[8,32,768]{2,1,0:T(8,128)(2,1)S(1)} %fusion.7), channel_id=1, replica_groups=mesh['y'=4,'z'=4,'x'=4,'c'=2] {'x','c'}, dimensions={0} | all-to-all | bytes 786432 | tf_op jit(solution)/shard_map/all_to_all | solution.py:465
  145.1 0.9 fusion
  (73 shorter events, 3.8 us)
Async XLA Ops:
  0.0 79.6 %copy-start = (bf16[6144,8]{0,1:T(8,128)(2,1)S(1)}, bf16[6144,8]{0,1:T(8,128)(2,1)}, u32[]{:S(2)}) copy-start(bf16[6144,8]{0,1:T(8,128)(2,1)} %param.23) | copy-start | bytes 294916
  0.0 8.2 %copy-start.3 = (s32[64,2]{0,1:T(2,128)S(1)}, s32[64,2]{0,1:T(2,128)}, u32[]{:S(2)}) copy-start(s32[64,2]{0,1:T(2,128)} %param.24) | copy-start | bytes 1540
  6.7 3.1 %collective-permute-start = (bf16[4,64,768]{2,1,0:T(8,128)(2,1)}, bf16[4,64,768]{2,1,0:T(8,128)(2,1)S(1)}, u32[]{:S(2)}, u32[]{:S(2)}) collective-permute-start(bf16[4,64,768]{2,1,0:T(8,128)(2,1)} %get-tuple-element.22), channel_id=1, source_target_pairs={{0,1},{1,0},{2,3},{3,2},{4,5},{5,4},{6,7},{7,6},{8,9},{9,8},{10,11... | collective-permute-start | bytes 1179656 | tf_op jit(solution)/shard_map/ppermute | solution.py:391
  8.9 17.1 %copy-start.2 = (bf16[6144]{0:T(1024)(128)(2,1)S(1)}, bf16[6144]{0:T(1024)(128)(2,1)}, u32[]{:S(2)}) copy-start(bf16[6144]{0:T(1024)(128)(2,1)} %param.22) | copy-start | bytes 36868
  10.9 5.3 %collective-permute-start.1 = (bf16[64,768]{1,0:T(8,128)(2,1)S(1)}, bf16[64,768]{1,0:T(8,128)(2,1)S(1)}, u32[]{:S(2)}, u32[]{:S(2)}) collective-permute-start(bf16[64,768]{1,0:T(8,128)(2,1)S(1)} %get-tuple-element.51), channel_id=1, source_target_pairs={{0,2},{2,4},{4,6},{6,0},{1,3},{3,5},{5,7},{7,1},{8,10},{10,12},{12... | collective-permute-start | bytes 294920 | tf_op jit(solution)/shard_map/ppermute | solution.py:29
  12.2 3.9 %collective-permute-start.3 = (bf16[64,768]{1,0:T(8,128)(2,1)S(1)}, bf16[64,768]{1,0:T(8,128)(2,1)S(1)}, u32[]{:S(2)}, u32[]{:S(2)}) collective-permute-start(bf16[64,768]{1,0:T(8,128)(2,1)S(1)} %get-tuple-element.52), channel_id=1, source_target_pairs={{0,6},{2,0},{4,2},{6,4},{1,7},{3,1},{5,3},{7,5},{8,14},{10,8},{12,... | collective-permute-start | bytes 294920 | tf_op jit(solution)/shard_map/ppermute | solution.py:29
  13.6 5.2 %collective-permute-start.2 = (bf16[64,768]{1,0:T(8,128)(2,1)S(1)}, bf16[64,768]{1,0:T(8,128)(2,1)S(1)}, u32[]{:S(2)}, u32[]{:S(2)}) collective-permute-start(bf16[64,768]{1,0:T(8,128)(2,1)S(1)} %get-tuple-element.53), channel_id=1, source_target_pairs={{0,4},{2,6},{4,0},{6,2},{1,5},{3,7},{5,1},{7,3},{8,12},{10,14},{12... | collective-permute-start | bytes 294920 | tf_op jit(solution)/shard_map/ppermute | solution.py:29
  20.8 13.3 %all-to-all-start = ((bf16[8,32,768]{2,1,0:T(8,128)(2,1)}), bf16[8,32,768]{2,1,0:T(8,128)(2,1)S(1)}, u32[]{:S(2)}, u32[]{:S(2)}) async-start(bf16[8,32,768]{2,1,0:T(8,128)(2,1)} %bitcast.6), calls=%async_computation | async-start | bytes 786432 | tf_op jit(solution)/shard_map/all_to_all | solution.py:412
  34.6 10.0 %collective-permute-start.4 = (bf16[16,6144]{1,0:T(8,128)(2,1)S(1)}, bf16[16,6144]{1,0:T(8,128)(2,1)S(1)}, u32[]{:S(2)}, u32[]{:S(2)}) collective-permute-start(bf16[16,6144]{1,0:T(8,128)(2,1)S(1)} %bitcast.53), channel_id=1, source_target_pairs={{0,8},{1,25},{8,0},{9,17},{16,24},{17,9},{24,16},{25,1},{2,10},{3,... | collective-permute-start | bytes 589832 | tf_op jit(solution)/shard_map/ppermute | solution.py:47
  38.5 5.9 %collective-permute-start.6 = (bf16[16,6144]{1,0:T(8,128)(2,1)S(1)}, bf16[16,6144]{1,0:T(8,128)(2,1)S(1)}, u32[]{:S(2)}, u32[]{:S(2)}) collective-permute-start(bf16[16,6144]{1,0:T(8,128)(2,1)S(1)} %bitcast.55), channel_id=1, source_target_pairs={{0,32},{1,97},{32,0},{33,65},{64,96},{65,33},{96,64},{97,1},{2,34}... | collective-permute-start | bytes 589832 | tf_op jit(solution)/shard_map/ppermute | solution.py:47
  44.4 7.0 %collective-permute-start.7 = (bf16[32,6144]{1,0:T(8,128)(2,1)S(1)}, bf16[32,6144]{1,0:T(8,128)(2,1)S(1)}, u32[]{:S(2)}, u32[]{:S(2)}) collective-permute-start(bf16[32,6144]{1,0:T(8,128)(2,1)S(1)} %constant_dynamic-update-slice_fusion.2.refs_2_), channel_id=1, source_target_pairs={{0,96},{1,33},{32,64},{33,1},{64,32},{65,97},{96,0},{97,65},{2,98}... | collective-permute-start | bytes 1179656 | tf_op jit(solution)/shard_map/ppermute | solution.py:47
  44.6 7.0 %collective-permute-start.5 = (bf16[32,6144]{1,0:T(8,128)(2,1)S(1)}, bf16[32,6144]{1,0:T(8,128)(2,1)S(1)}, u32[]{:S(2)}, u32[]{:S(2)}) collective-permute-start(bf16[32,6144]{1,0:T(8,128)(2,1)S(1)} %constant_dynamic-update-slice_fusion.refs_0_), channel_id=1, source_target_pairs={{0,24},{1,9},{8,16},{9,1},{16,8},{17,25},{24,0},{25,17},{2,26},{3,... | collective-permute-start | bytes 1179656 | tf_op jit(solution)/shard_map/ppermute | solution.py:47
  44.7 11.1 %collective-permute-start.10 = (bf16[32,6144]{1,0:T(8,128)(2,1)S(1)}, bf16[32,6144]{1,0:T(8,128)(2,1)S(1)}, u32[]{:S(2)}, u32[]{:S(2)}) collective-permute-start(bf16[32,6144]{1,0:T(8,128)(2,1)S(1)} %constant_dynamic-update-slice_fusion.2.refs_2_), channel_id=1, source_target_pairs={{0,8},{1,25},{8,16},{9,1},{16,24},{17,9},{24,0},{25,17},{2,10},{3,... | collective-permute-start | bytes 1179656 | tf_op jit(solution)/shard_map/ppermute | solution.py:38
  45.1 10.8 %collective-permute-start.8 = (bf16[32,6144]{1,0:T(8,128)(2,1)S(1)}, bf16[32,6144]{1,0:T(8,128)(2,1)S(1)}, u32[]{:S(2)}, u32[]{:S(2)}) collective-permute-start(bf16[32,6144]{1,0:T(8,128)(2,1)S(1)} %constant_dynamic-update-slice_fusion.refs_0_), channel_id=1, source_target_pairs={{0,32},{1,97},{32,64},{33,1},{64,96},{65,33},{96,0},{97,65},{2,34}... | collective-permute-start | bytes 1179656 | tf_op jit(solution)/shard_map/ppermute | solution.py:38
  51.4 8.6 %collective-permute-start.17 = (bf16[32,6144]{1,0:T(8,128)(2,1)S(1)}, bf16[32,6144]{1,0:T(8,128)(2,1)S(1)}, u32[]{:S(2)}, u32[]{:S(2)}) collective-permute-start(bf16[32,6144]{1,0:T(8,128)(2,1)S(1)} %collective-permute-done.7.refs_3_), channel_id=1, source_target_pairs={{0,8},{1,25},{8,16},{9,1},{16,24},{17,9},{24,0},{25,17},{2,10},{3,... | collective-permute-start | bytes 1179656 | tf_op jit(solution)/shard_map/ppermute | solution.py:38
  51.6 9.8 %collective-permute-start.15 = (bf16[32,6144]{1,0:T(8,128)(2,1)S(1)}, bf16[32,6144]{1,0:T(8,128)(2,1)S(1)}, u32[]{:S(2)}, u32[]{:S(2)}) collective-permute-start(bf16[32,6144]{1,0:T(8,128)(2,1)S(1)} %collective-permute-done.5.refs_1_), channel_id=1, source_target_pairs={{0,32},{1,97},{32,64},{33,1},{64,96},{65,33},{96,0},{97,65},{2,34}... | collective-permute-start | bytes 1179656 | tf_op jit(solution)/shard_map/ppermute | solution.py:38
  55.8 16.2 %collective-permute-start.11 = (bf16[32,6144]{1,0:T(8,128)(2,1)S(1)}, bf16[32,6144]{1,0:T(8,128)(2,1)S(1)}, u32[]{:S(2)}, u32[]{:S(2)}) collective-permute-start(bf16[32,6144]{1,0:T(8,128)(2,1)S(1)} %collective-permute-done.10.refs_2_), channel_id=1, source_target_pairs={{0,8},{1,25},{8,16},{9,1},{16,24},{17,9},{24,0},{25,17},{2,10},{3,... | collective-permute-start | bytes 1179656 | tf_op jit(solution)/shard_map/ppermute | solution.py:38
  55.8 16.2 %collective-permute-start.9 = (bf16[32,6144]{1,0:T(8,128)(2,1)S(1)}, bf16[32,6144]{1,0:T(8,128)(2,1)S(1)}, u32[]{:S(2)}, u32[]{:S(2)}) collective-permute-start(bf16[32,6144]{1,0:T(8,128)(2,1)S(1)} %collective-permute-done.8.refs_0_), channel_id=1, source_target_pairs={{0,32},{1,97},{32,64},{33,1},{64,96},{65,33},{96,0},{97,65},{2,34}... | collective-permute-start | bytes 1179656 | tf_op jit(solution)/shard_map/ppermute | solution.py:38
  60.0 13.5 %collective-permute-start.18 = (bf16[32,6144]{1,0:T(8,128)(2,1)S(1)}, bf16[32,6144]{1,0:T(8,128)(2,1)S(1)}, u32[]{:S(2)}, u32[]{:S(2)}) collective-permute-start(bf16[32,6144]{1,0:T(8,128)(2,1)S(1)} %collective-permute-done.17.refs_3_), channel_id=1, source_target_pairs={{0,8},{1,25},{8,16},{9,1},{16,24},{17,9},{24,0},{25,17},{2,10},{3,... | collective-permute-start | bytes 1179656 | tf_op jit(solution)/shard_map/ppermute | solution.py:38
  61.3 12.2 %collective-permute-start.16 = (bf16[32,6144]{1,0:T(8,128)(2,1)S(1)}, bf16[32,6144]{1,0:T(8,128)(2,1)S(1)}, u32[]{:S(2)}, u32[]{:S(2)}) collective-permute-start(bf16[32,6144]{1,0:T(8,128)(2,1)S(1)} %collective-permute-done.15.refs_1_), channel_id=1, source_target_pairs={{0,32},{1,97},{32,64},{33,1},{64,96},{65,33},{96,0},{97,65},{2,34}... | collective-permute-start | bytes 1179656 | tf_op jit(solution)/shard_map/ppermute | solution.py:38
  72.8 13.7 %collective-permute-start.12 = (bf16[64,6144]{1,0:T(8,128)(2,1)S(1)}, bf16[64,6144]{1,0:T(8,128)(2,1)S(1)}, u32[]{:S(2)}, u32[]{:S(2)}) collective-permute-start(bf16[64,6144]{1,0:T(8,128)(2,1)S(1)} %get-tuple-element.25), channel_id=1, source_target_pairs={{0,96},{1,33},{32,0},{33,65},{64,32},{65,97},{96,64},{97,1},{2,98}... | collective-permute-start | bytes 2359304 | tf_op jit(solution)/shard_map/ppermute | solution.py:38
  72.9 13.7 %collective-permute-start.13 = (bf16[64,6144]{1,0:T(8,128)(2,1)S(1)}, bf16[64,6144]{1,0:T(8,128)(2,1)S(1)}, u32[]{:S(2)}, u32[]{:S(2)}) collective-permute-start(bf16[64,6144]{1,0:T(8,128)(2,1)S(1)} %get-tuple-element.26), channel_id=1, source_target_pairs={{0,24},{1,9},{8,0},{9,17},{16,8},{17,25},{24,16},{25,1},{2,26},{3,... | collective-permute-start | bytes 2359304 | tf_op jit(solution)/shard_map/ppermute | solution.py:38
  78.8 16.4 %collective-permute-start.19 = (bf16[64,6144]{1,0:T(8,128)(2,1)S(1)}, bf16[64,6144]{1,0:T(8,128)(2,1)S(1)}, u32[]{:S(2)}, u32[]{:S(2)}) collective-permute-start(bf16[64,6144]{1,0:T(8,128)(2,1)S(1)} %get-tuple-element.31.refs_7_), channel_id=1, source_target_pairs={{0,96},{1,33},{32,0},{33,65},{64,32},{65,97},{96,64},{97,1},{2,98}... | collective-permute-start | bytes 2359304 | tf_op jit(solution)/shard_map/ppermute | solution.py:38
  80.0 15.5 %collective-permute-start.25 = (bf16[64,6144]{1,0:T(8,128)(2,1)S(1)}, bf16[64,6144]{1,0:T(8,128)(2,1)S(1)}, u32[]{:S(2)}, u32[]{:S(2)}) collective-permute-start(bf16[64,6144]{1,0:T(8,128)(2,1)S(1)} %get-tuple-element.32.refs_8_), channel_id=1, source_target_pairs={{0,24},{1,9},{8,0},{9,17},{16,8},{17,25},{24,16},{25,1},{2,26},{3,... | collective-permute-start | bytes 2359304 | tf_op jit(solution)/shard_map/ppermute | solution.py:38
  91.5 15.8 %collective-permute-start.14 = (bf16[64,6144]{1,0:T(8,128)(2,1)S(1)}, bf16[64,6144]{1,0:T(8,128)(2,1)S(1)}, u32[]{:S(2)}, u32[]{:S(2)}) collective-permute-start(bf16[64,6144]{1,0:T(8,128)(2,1)S(1)} %get-tuple-element.30), channel_id=1, source_target_pairs={{0,32},{1,97},{32,64},{33,1},{64,96},{65,33},{96,0},{97,65},{2,34}... | collective-permute-start | bytes 2359304 | tf_op jit(solution)/shard_map/ppermute | solution.py:38
  94.1 21.2 %collective-permute-start.24 = (bf16[64,6144]{1,0:T(8,128)(2,1)S(1)}, bf16[64,6144]{1,0:T(8,128)(2,1)S(1)}, u32[]{:S(2)}, u32[]{:S(2)}) collective-permute-start(bf16[64,6144]{1,0:T(8,128)(2,1)S(1)} %get-tuple-element.35), channel_id=1, source_target_pairs={{0,8},{1,25},{8,16},{9,1},{16,24},{17,9},{24,0},{25,17},{2,10},{3,... | collective-permute-start | bytes 2359304 | tf_op jit(solution)/shard_map/ppermute | solution.py:38
  95.4 16.3 %collective-permute-start.20 = (bf16[64,6144]{1,0:T(8,128)(2,1)S(1)}, bf16[64,6144]{1,0:T(8,128)(2,1)S(1)}, u32[]{:S(2)}, u32[]{:S(2)}) collective-permute-start(bf16[64,6144]{1,0:T(8,128)(2,1)S(1)} %add_convert_fusion.1), channel_id=1, source_target_pairs={{0,96},{1,33},{32,0},{33,65},{64,32},{65,97},{96,64},{97,1},{2,98}... | collective-permute-start | bytes 2359304 | tf_op jit(solution)/shard_map/ppermute | solution.py:38
  95.7 19.7 %collective-permute-start.26 = (bf16[64,6144]{1,0:T(8,128)(2,1)S(1)}, bf16[64,6144]{1,0:T(8,128)(2,1)S(1)}, u32[]{:S(2)}, u32[]{:S(2)}) collective-permute-start(bf16[64,6144]{1,0:T(8,128)(2,1)S(1)} %add_convert_fusion), channel_id=1, source_target_pairs={{0,24},{1,9},{8,0},{9,17},{16,8},{17,25},{24,16},{25,1},{2,26},{3,... | collective-permute-start | bytes 2359304 | tf_op jit(solution)/shard_map/ppermute | solution.py:38
  112.0 8.4 %collective-permute-start.21 = (bf16[16,6144]{1,0:T(8,128)(2,1)S(1)}, bf16[16,6144]{1,0:T(8,128)(2,1)S(1)}, u32[]{:S(2)}, u32[]{:S(2)}) collective-permute-start(bf16[16,6144]{1,0:T(8,128)(2,1)S(1)} %get-tuple-element.45), channel_id=1, source_target_pairs={{0,8},{1,25},{8,0},{9,17},{16,24},{17,9},{24,16},{25,1},{2,10},{3,... | collective-permute-start | bytes 589832 | tf_op jit(solution)/shard_map/ppermute | solution.py:47
  113.2 7.2 %collective-permute-start.23 = (bf16[16,6144]{1,0:T(8,128)(2,1)S(1)}, bf16[16,6144]{1,0:T(8,128)(2,1)S(1)}, u32[]{:S(2)}, u32[]{:S(2)}) collective-permute-start(bf16[16,6144]{1,0:T(8,128)(2,1)S(1)} %get-tuple-element.46), channel_id=1, source_target_pairs={{0,16},{8,24},{16,0},{24,8},{1,17},{9,25},{17,1},{25,9},{2,18},{10... | collective-permute-start | bytes 589832 | tf_op jit(solution)/shard_map/ppermute | solution.py:29
  113.8 8.9 %collective-permute-start.22 = (bf16[16,6144]{1,0:T(8,128)(2,1)S(1)}, bf16[16,6144]{1,0:T(8,128)(2,1)S(1)}, u32[]{:S(2)}, u32[]{:S(2)}) collective-permute-start(bf16[16,6144]{1,0:T(8,128)(2,1)S(1)} %get-tuple-element.47), channel_id=1, source_target_pairs={{0,24},{1,9},{8,16},{9,1},{16,8},{17,25},{24,0},{25,17},{2,26},{3,... | collective-permute-start | bytes 589832 | tf_op jit(solution)/shard_map/ppermute | solution.py:47
  115.7 7.1 %collective-permute-start.27 = (bf16[16,6144]{1,0:T(8,128)(2,1)S(1)}, bf16[16,6144]{1,0:T(8,128)(2,1)S(1)}, u32[]{:S(2)}, u32[]{:S(2)}) collective-permute-start(bf16[16,6144]{1,0:T(8,128)(2,1)S(1)} %get-tuple-element.48), channel_id=1, source_target_pairs={{0,32},{1,97},{32,0},{33,65},{64,96},{65,33},{96,64},{97,1},{2,34}... | collective-permute-start | bytes 589832 | tf_op jit(solution)/shard_map/ppermute | solution.py:47
  117.5 6.3 %collective-permute-start.29 = (bf16[16,6144]{1,0:T(8,128)(2,1)S(1)}, bf16[16,6144]{1,0:T(8,128)(2,1)S(1)}, u32[]{:S(2)}, u32[]{:S(2)}) collective-permute-start(bf16[16,6144]{1,0:T(8,128)(2,1)S(1)} %get-tuple-element.49), channel_id=1, source_target_pairs={{0,64},{32,96},{64,0},{96,32},{1,65},{33,97},{65,1},{97,33},{2,66}... | collective-permute-start | bytes 589832 | tf_op jit(solution)/shard_map/ppermute | solution.py:29
  120.4 4.8 %collective-permute-start.28 = (bf16[16,6144]{1,0:T(8,128)(2,1)S(1)}, bf16[16,6144]{1,0:T(8,128)(2,1)S(1)}, u32[]{:S(2)}, u32[]{:S(2)}) collective-permute-start(bf16[16,6144]{1,0:T(8,128)(2,1)S(1)} %get-tuple-element.50), channel_id=1, source_target_pairs={{0,96},{1,33},{32,64},{33,1},{64,32},{65,97},{96,0},{97,65},{2,98}... | collective-permute-start | bytes 589832 | tf_op jit(solution)/shard_map/ppermute | solution.py:47
  125.3 20.6 %copy-start.1 = (bf16[6144,8]{0,1:T(8,128)(2,1)S(1)}, bf16[6144,8]{0,1:T(8,128)(2,1)}, u32[]{:S(2)}) copy-start(bf16[6144,8]{0,1:T(8,128)(2,1)} %param.23) | copy-start | bytes 294916
